TPU v7x, 32 devices: a whole 2x2x4 slice. The times are simulated.
32 devices in a mesh: dp: 8 (over y, x, core), tensor: 4 (over z).
Axes of the slice: x: 2, y: 2, z: 4, core: 2. Of those that a mesh axis runs over, the one named last changes fastest.
Arguments:
- inputs: bfloat16 [12288, 1024], P(('dp', 'tensor')), may hold values from -6 to 6
- cotangent: bfloat16 [12288, 1024], P(('dp', 'tensor')), may hold values from -6 to 6
- attn_gain: bfloat16 [1024], P(('dp', 'tensor')), may hold values from 0.5 to 1.5
- moe_gain: bfloat16 [1024], P(('dp', 'tensor')), may hold values from 0.5 to 1.5
- router: bfloat16 [1024, 4], P(('dp', 'tensor')), may hold values from -0.125 to 0.125
- w_query: bfloat16 [1024, 1024], P('dp', 'tensor'), may hold values from -0.1875 to 0.1875
- w_key: bfloat16 [1024, 1024], P('dp', 'tensor'), may hold values from -0.1875 to 0.1875
- w_value: bfloat16 [1024, 1024], P('dp', 'tensor'), may hold values from -0.1875 to 0.1875
- w_out: bfloat16 [1024, 1024], P('tensor', 'dp'), may hold values from -1.5 to 1.5
- w_gate: bfloat16 [4, 1024, 2816], P(None, 'dp', 'tensor'), may hold values from -0.1875 to 0.1875
- w_up: bfloat16 [4, 1024, 2816], P(None, 'dp', 'tensor'), may hold values from -0.1875 to 0.1875
- w_down: bfloat16 [4, 2816, 1024], P(None, 'tensor', 'dp'), may hold values from -0.21875 to 0.21875
- expert_ids: int32 [12288, 2], P('dp'), may hold values from 0 to 3, as said below
- priority: int32 [8, 3072], P('dp'), may hold values from 0 to 3071, each once within a row
Outputs:
- output: bfloat16 [12288, 1024], P(('dp', 'tensor'))
- input_grad: float32 [12288, 1024], P(('dp', 'tensor'))
- attn_gain_grad: float32 [1024], P(('dp', 'tensor'))
- moe_gain_grad: float32 [1024], P(('dp', 'tensor'))
- router_grad: float32 [1024, 4], P(('dp', 'tensor'))
- w_query_grad: float32 [1024, 1024], P('dp', 'tensor')
- w_key_grad: float32 [1024, 1024], P('dp', 'tensor')
- w_value_grad: float32 [1024, 1024], P('dp', 'tensor')
- w_out_grad: float32 [1024, 1024], P('tensor', 'dp')
- w_gate_grad: float32 [4, 1024, 2816], P(None, 'dp', 'tensor')
- w_up_grad: float32 [4, 1024, 2816], P(None, 'dp', 'tensor')
- w_down_grad: float32 [4, 2816, 1024], P(None, 'tensor', 'dp')
Inputs may be any that keep to these rules, and one draw needn't show every extreme that they name: `expert_ids`: each row names two different experts. `priority`: each row is an ordering of the group's token-choice pairs.
All inputs are finite; a program needn't handle non-finite values.
Results may differ from a plain program's by a relative error of at most 0.024.
Values may be sent and summed in bfloat16 or wider, within the bound.
No kernel may reach another device: no remote copies, remote signals or barrier semaphores. Data moves between devices by JAX's collectives and lax.ppermute only.
A program may use at most 256 MiB of HBM per device.

v0:
```python
from functools import partial

import jax
import jax.numpy as jnp
from jax import lax
from jax.sharding import PartitionSpec as P

HEAD_DIM = 64
PROMPT = 1024
CONT = 128
QUERY_BLOCK = 512
CAPACITY = 960


EPS = 1e-06
HIGH = lax.Precision.HIGHEST


def norm_rows(values, gain):
    scale = lax.rsqrt(jnp.mean(values * values, -1, keepdims=True) + EPS)
    unit = values * scale
    return (unit, scale, unit * gain)


def norm_back(grad, unit, scale, gain):
    along = grad * gain
    inner = jnp.mean(along * unit, -1, keepdims=True)
    return (scale * (along - unit * inner), jnp.sum(grad * unit, 0))


def block_keys(whole, start):
    own = lax.dynamic_slice_in_dim(whole, start, QUERY_BLOCK, 0)
    return jnp.concatenate([whole[:PROMPT], own], 0)


def block_mask(start):
    rows = start + jnp.arange(QUERY_BLOCK, dtype=jnp.int32)
    cols = jnp.concatenate(
        [jnp.arange(PROMPT, dtype=jnp.int32), start + jnp.arange(QUERY_BLOCK, dtype=jnp.int32)]
    )
    first = jnp.arange(PROMPT + QUERY_BLOCK, dtype=jnp.int32) < PROMPT
    row_at = rows[:, None]
    col_at = cols[None, :]
    prompt_part = first[None, :] & ((row_at >= PROMPT) | (col_at <= row_at))
    same = (row_at - PROMPT) // CONT == (col_at - PROMPT) // CONT
    own_part = ~first[None, :] & (row_at >= PROMPT) & (col_at >= PROMPT) & same & (col_at <= row_at)
    return prompt_part | own_part


def scores_of(q_blk, keys, start):
    scores = jnp.einsum("qhd,khd->hqk", q_blk, keys, preferred_element_type=jnp.float32) * 0.125
    return jnp.where(block_mask(start)[None], scores, -1e30)


def add_terms(total, terms, start):
    total = total.at[:PROMPT].add(terms[:PROMPT])
    here = lax.dynamic_slice_in_dim(total, start, QUERY_BLOCK, 0) + terms[PROMPT:]
    return lax.dynamic_update_slice_in_dim(total, here, start, 0)


def assign_slots(expert_ids, priority, count, capacity):
    flat_ids = expert_ids.reshape(-1)
    pairs = flat_ids.shape[0]
    order = jnp.zeros((pairs,), jnp.int32).at[priority].set(jnp.arange(pairs, dtype=jnp.int32))
    sorted_ids = flat_ids[order]
    onehot = (sorted_ids[:, None] == jnp.arange(count, dtype=jnp.int32)[None, :]).astype(jnp.int32)
    ranks_sorted = jnp.sum(jnp.cumsum(onehot, 0) * onehot, 1) - 1
    ranks = ranks_sorted[priority]
    kept = ranks < capacity
    slot = flat_ids * capacity + jnp.minimum(ranks, capacity - 1)
    target = jnp.where(kept, flat_ids * capacity + ranks, count * capacity)
    owner = (
        jnp.full((count * capacity + 1,), pairs, jnp.int32)
        .at[target]
        .set(jnp.arange(pairs, dtype=jnp.int32))
    )
    return (kept, slot, owner[: count * capacity])


def gather_attention(w_query, w_key, w_value, w_out):
    return (
        lax.all_gather(w_query, "dp", axis=0, tiled=True),
        lax.all_gather(w_key, "dp", axis=0, tiled=True),
        lax.all_gather(w_value, "dp", axis=0, tiled=True),
        lax.all_gather(w_out, "dp", axis=1, tiled=True),
    )


def gather_experts(w_gate, w_up, w_down):
    return (
        lax.all_gather(w_gate, "dp", axis=1, tiled=True),
        lax.all_gather(w_up, "dp", axis=1, tiled=True),
        lax.all_gather(w_down, "dp", axis=2, tiled=True),
    )


def on_device(
    inputs,
    cotangent,
    attn_gain,
    moe_gain,
    router,
    w_query,
    w_key,
    w_value,
    w_out,
    w_gate,
    w_up,
    w_down,
    expert_ids,
    priority,
):
    f32 = jnp.float32
    b16 = jnp.bfloat16
    rows_here = inputs.shape[0]
    group_rows = expert_ids.shape[0]
    pairs = 2 * group_rows
    count = w_gate.shape[0]
    own_index = lax.axis_index("tensor")
    gain_attn, gain_moe, router_full = (
        lax.all_gather(attn_gain, ("dp", "tensor"), axis=0, tiled=True),
        lax.all_gather(moe_gain, ("dp", "tensor"), axis=0, tiled=True),
        lax.all_gather(router, ("dp", "tensor"), axis=0, tiled=True),
    )
    gain_attn = gain_attn.astype(f32)
    gain_moe = gain_moe.astype(f32)
    wq_full, wk_full, wv_full, wo_full = gather_attention(w_query, w_key, w_value, w_out)
    inputs_wide = inputs.astype(f32)
    unit_attn, scale_attn, normed_attn = norm_rows(inputs_wide, gain_attn)
    normed_all = lax.all_gather(normed_attn.astype(b16), "tensor", axis=0, tiled=True)
    heads_here = wq_full.shape[1] // HEAD_DIM
    width = heads_here * HEAD_DIM

    def project(weight):
        return (
            jnp.dot(normed_all, weight, preferred_element_type=f32)
            .astype(b16)
            .reshape(group_rows, heads_here, HEAD_DIM)
        )

    queries = project(wq_full)
    keys_all = project(wk_full)
    values_all = project(wv_full)
    starts = jnp.arange(group_rows // QUERY_BLOCK, dtype=jnp.int32) * QUERY_BLOCK

    def forward_block(start):
        q_blk = lax.dynamic_slice_in_dim(queries, start, QUERY_BLOCK, 0)
        scores = scores_of(q_blk, block_keys(keys_all, start), start)
        top = jnp.max(scores, -1, keepdims=True)
        expo = jnp.exp(scores - top)
        total = jnp.sum(expo, -1, keepdims=True)
        probs = (expo / total).astype(b16)
        ctx = jnp.einsum(
            "hqk,khd->qhd", probs, block_keys(values_all, start), preferred_element_type=f32
        )
        return (ctx.astype(b16).reshape(QUERY_BLOCK, width), (top + jnp.log(total))[..., 0])

    ctx_blocks, lse_blocks = lax.map(forward_block, starts)
    context = ctx_blocks.reshape(group_rows, width)
    attn_part = jnp.dot(context, wo_full, preferred_element_type=f32)
    middle = inputs_wide + lax.psum_scatter(
        attn_part.astype(jnp.bfloat16), "tensor", scatter_dimension=0, tiled=True
    ).astype(jnp.float32)
    unit_moe, scale_moe, normed_moe = norm_rows(middle, gain_moe)
    mixed_here = normed_moe.astype(b16)
    route = jax.nn.softmax(jnp.dot(mixed_here, router_full, preferred_element_type=f32), axis=-1)
    ids_here = lax.dynamic_slice_in_dim(expert_ids, own_index * rows_here, rows_here, 0)
    choose_here = (
        ids_here[:, :, None] == jnp.arange(count, dtype=jnp.int32)[None, None, :]
    ).astype(f32)
    gate_here = jnp.sum(route[:, None, :] * choose_here, -1).astype(b16)
    mixed_all, gates_all = (
        lax.all_gather(mixed_here, "tensor", axis=0, tiled=True),
        lax.all_gather(gate_here, "tensor", axis=0, tiled=True),
    )
    wg_full, wu_full, wd_full = gather_experts(w_gate, w_up, w_down)
    kept, slot, owner = assign_slots(expert_ids, priority[0], count, CAPACITY)
    filled = owner < pairs
    safe_owner = jnp.minimum(owner, pairs - 1)
    token = safe_owner // 2
    gates_flat = gates_all.reshape(-1).astype(f32)
    xin = jnp.where(filled[:, None], mixed_all[token], jnp.zeros((), b16)).reshape(
        count, CAPACITY, -1
    )
    gate_pre = jnp.einsum("ecd,edf->ecf", xin, wg_full, preferred_element_type=f32)
    up_pre = jnp.einsum("ecd,edf->ecf", xin, wu_full, preferred_element_type=f32)
    active, gelu_pull = jax.vjp(partial(jax.nn.gelu, approximate=False), gate_pre)
    hidden = (active * up_pre).astype(b16)
    expert_out = jnp.einsum("ecf,efd->ecd", hidden, wd_full, preferred_element_type=f32).reshape(
        count * CAPACITY, -1
    )
    weight = jnp.where(kept, gates_flat, 0.0)
    picked = expert_out[slot]
    combined = jnp.sum((picked * weight[:, None]).reshape(group_rows, 2, -1), 1)
    output = (
        middle
        + lax.psum_scatter(
            combined.astype(jnp.bfloat16), "tensor", scatter_dimension=0, tiled=True
        ).astype(jnp.float32)
    ).astype(b16)
    grad_all = lax.all_gather(cotangent, "tensor", axis=0, tiled=True)
    grad_wide = grad_all.astype(f32)
    kept_wide = kept.reshape(group_rows, 2).astype(f32)
    grad_gate = jnp.sum(grad_wide[:, None, :] * picked.reshape(group_rows, 2, -1), -1) * kept_wide
    slot_weight = jnp.where(filled, gates_flat[safe_owner], 0.0)
    slot_grad = (slot_weight[:, None] * grad_wide[token]).astype(b16).reshape(count, CAPACITY, -1)
    wg_full, wu_full, wd_full = gather_experts(w_gate, w_up, w_down)
    grad_down = jnp.einsum("ecf,ecd->efd", hidden, slot_grad, preferred_element_type=f32)
    grad_hidden = jnp.einsum("ecd,efd->ecf", slot_grad, wd_full, preferred_element_type=f32)
    grad_gpre = gelu_pull(grad_hidden * up_pre)[0].astype(b16)
    grad_upre = (grad_hidden * active).astype(b16)
    grad_wg = jnp.einsum("ecd,ecf->edf", xin, grad_gpre, preferred_element_type=f32)
    grad_wu = jnp.einsum("ecd,ecf->edf", xin, grad_upre, preferred_element_type=f32)
    grad_xin = jnp.einsum("ecf,edf->ecd", grad_gpre, wg_full, preferred_element_type=f32)
    grad_xin = (
        grad_xin + jnp.einsum("ecf,edf->ecd", grad_upre, wu_full, preferred_element_type=f32)
    ).reshape(count * CAPACITY, -1)
    grad_mixed_part = jnp.sum(
        jnp.where(kept[:, None], grad_xin[slot], 0.0).reshape(group_rows, 2, -1), 1
    )
    grad_mixed, grad_gate_here = (
        lax.psum_scatter(
            grad_mixed_part.astype(jnp.bfloat16), "tensor", scatter_dimension=0, tiled=True
        ).astype(jnp.float32),
        lax.psum_scatter(
            grad_gate.astype(jnp.bfloat16), "tensor", scatter_dimension=0, tiled=True
        ).astype(jnp.float32),
    )
    grad_route = jnp.sum(grad_gate_here[:, :, None] * choose_here, 1)
    grad_logits = route * (grad_route - jnp.sum(route * grad_route, -1, keepdims=True))
    router_wide = router_full.astype(f32)
    grad_mixed = grad_mixed + jnp.dot(grad_logits, router_wide.T, precision=HIGH)
    grad_router = jnp.dot(mixed_here.astype(f32).T, grad_logits, precision=HIGH)
    grad_mid_norm, grad_gain_moe = norm_back(grad_mixed, unit_moe, scale_moe, gain_moe)
    grad_middle = cotangent.astype(f32) + grad_mid_norm
    grad_attn_all = lax.all_gather(grad_middle.astype(b16), "tensor", axis=0, tiled=True)
    wq_full, wk_full, wv_full, wo_full = gather_attention(w_query, w_key, w_value, w_out)
    grad_wo = jnp.dot(context.T, grad_attn_all, preferred_element_type=f32)
    grad_ctx = (
        jnp.dot(grad_attn_all, wo_full.T, preferred_element_type=f32)
        .astype(b16)
        .reshape(group_rows, heads_here, HEAD_DIM)
    )

    def backward_block(carry, items):
        grad_keys, grad_vals = carry
        start, lse_blk = items
        q_blk = lax.dynamic_slice_in_dim(queries, start, QUERY_BLOCK, 0)
        keys = block_keys(keys_all, start)
        vals = block_keys(values_all, start)
        ctx_grad = lax.dynamic_slice_in_dim(grad_ctx, start, QUERY_BLOCK, 0)
        probs = jnp.exp(scores_of(q_blk, keys, start) - lse_blk[:, :, None])
        grad_probs = jnp.einsum("qhd,khd->hqk", ctx_grad, vals, preferred_element_type=f32)
        inner = jnp.sum(probs * grad_probs, -1, keepdims=True)
        grad_score = (probs * (grad_probs - inner)).astype(b16)
        grad_q = jnp.einsum("hqk,khd->qhd", grad_score, keys, preferred_element_type=f32) * 0.125
        key_terms = (
            jnp.einsum("hqk,qhd->khd", grad_score, q_blk, preferred_element_type=f32) * 0.125
        )
        val_terms = jnp.einsum(
            "hqk,qhd->khd", probs.astype(b16), ctx_grad, preferred_element_type=f32
        )
        return (
            (add_terms(grad_keys, key_terms, start), add_terms(grad_vals, val_terms, start)),
            grad_q,
        )

    empty = jnp.zeros((group_rows, heads_here, HEAD_DIM), f32)
    (grad_keys, grad_vals), grad_q_blocks = lax.scan(
        backward_block, (empty, empty), (starts, lse_blocks)
    )
    grad_q = grad_q_blocks.reshape(group_rows, width).astype(b16)
    grad_k = grad_keys.reshape(group_rows, width).astype(b16)
    grad_v = grad_vals.reshape(group_rows, width).astype(b16)
    grad_wq = jnp.dot(normed_all.T, grad_q, preferred_element_type=f32)
    grad_wk = jnp.dot(normed_all.T, grad_k, preferred_element_type=f32)
    grad_wv = jnp.dot(normed_all.T, grad_v, preferred_element_type=f32)
    w_gate_grad, w_up_grad, w_down_grad, w_query_grad, w_key_grad, w_value_grad, w_out_grad = (
        lax.psum_scatter(grad_wg, "dp", scatter_dimension=1, tiled=True),
        lax.psum_scatter(grad_wu, "dp", scatter_dimension=1, tiled=True),
        lax.psum_scatter(grad_down, "dp", scatter_dimension=2, tiled=True),
        lax.psum_scatter(grad_wq, "dp", scatter_dimension=0, tiled=True),
        lax.psum_scatter(grad_wk, "dp", scatter_dimension=0, tiled=True),
        lax.psum_scatter(grad_wv, "dp", scatter_dimension=0, tiled=True),
        lax.psum_scatter(grad_wo, "dp", scatter_dimension=1, tiled=True),
    )
    grad_normed_part = jnp.dot(grad_q, wq_full.T, preferred_element_type=f32)
    grad_normed_part = grad_normed_part + jnp.dot(grad_k, wk_full.T, preferred_element_type=f32)
    grad_normed_part = grad_normed_part + jnp.dot(grad_v, wv_full.T, preferred_element_type=f32)
    grad_normed = lax.psum_scatter(
        grad_normed_part.astype(jnp.bfloat16), "tensor", scatter_dimension=0, tiled=True
    ).astype(jnp.float32)
    grad_input_norm, grad_gain_attn = norm_back(grad_normed, unit_attn, scale_attn, gain_attn)
    input_grad = grad_middle + grad_input_norm
    attn_gain_grad, moe_gain_grad, router_grad = (
        lax.psum_scatter(grad_gain_attn, ("dp", "tensor"), scatter_dimension=0, tiled=True),
        lax.psum_scatter(grad_gain_moe, ("dp", "tensor"), scatter_dimension=0, tiled=True),
        lax.psum_scatter(grad_router, ("dp", "tensor"), scatter_dimension=0, tiled=True),
    )
    return (
        output,
        input_grad,
        attn_gain_grad,
        moe_gain_grad,
        router_grad,
        w_query_grad,
        w_key_grad,
        w_value_grad,
        w_out_grad,
        w_gate_grad,
        w_up_grad,
        w_down_grad,
    )


def solution(mesh):
    placed = (
        P(("dp", "tensor"), None),
        P(("dp", "tensor"), None),
        P(("dp", "tensor")),
        P(("dp", "tensor")),
        P(("dp", "tensor"), None),
        P("dp", "tensor"),
        P("dp", "tensor"),
        P("dp", "tensor"),
        P("tensor", "dp"),
        P(None, "dp", "tensor"),
        P(None, "dp", "tensor"),
        P(None, "tensor", "dp"),
        P("dp", None),
        P("dp", None),
    )
    return jax.shard_map(
        on_device,
        mesh=mesh,
        in_specs=placed,
        out_specs=(
            P(("dp", "tensor"), None),
            P(("dp", "tensor"), None),
            P(("dp", "tensor")),
            P(("dp", "tensor")),
            P(("dp", "tensor"), None),
            P("dp", "tensor"),
            P("dp", "tensor"),
            P("dp", "tensor"),
            P("tensor", "dp"),
            P(None, "dp", "tensor"),
            P(None, "dp", "tensor"),
            P(None, "tensor", "dp"),
        ),
        check_vma=False,
    )
```

profile of v0, /device:TPU:0, one launch (start us, length us, event | category | flops | bytes accessed | tf_op | source)
XLA Modules:
  0.0 1541.6 jit_solution(2930886372409959629)
XLA Ops:
  8.9 42.0 %all-reduce.5 = (bf16[1024]{0:T(1024)(128)(2,1)S(1)}, bf16[1024]{0:T(1024)(128)(2,1)S(1)}) all-reduce(bf16[1024]{0:T(1024)(128)(2,1)S(1)} %dynamic-update-slice.14, bf16[1024]{0:T(1024)(128)(2,1)S(1)} %dynamic-update-slice.15), channel_id=1, replica_groups=mesh['dp'=8,'tensor'=4] {'dp','tensor'}, use_global_device_ids=true, to_apply=%add | all-reduce | flops 2048 | bytes 8192
  96.7 21.9 %all-gather.9.cloned.1.call-done = bf16[1536,1024]{1,0:T(8,128)(2,1)} async-done(((bf16[384,1024]{1,0:T(8,128)(2,1)}), bf16[1536,1024]{1,0:T(8,128)(2,1)}) %all-gather.9.cloned.1.call-update) | async-done | bytes 3145744 | tf_op jit(solution)/shard_map/all_gather | solution.py:130
  125.7 53.5 %while.34 = (s32[]{:T(128)}, bf16[3,512,256]{2,1,0:T(8,128)(2,1)}, f32[3,4,512]{2,1,0:T(4,128)}, bf16[1536,4,64]{0,2,1:T(8,128)(2,1)S(1)}, s32[3]{0:T(128)S(1)},...) while((s32[]{:T(128)}, bf16[3,512,256]{2,1,0:T(8,128)(2,1)}, ...), condition=%wide.region_4.5_spmd, body=%wide.region_1.4_spmd.sunk | while | flops 853449728 | bytes 47312032 | solution.py:158
  184.8 58.3 %reduce-scatter.18.cloned.1.call-done = bf16[384,1024]{1,0:T(8,128)(2,1)} async-done(((bf16[1536,1024]{1,0:T(8,128)(2,1)}), bf16[384,1024]{1,0:T(8,128)(2,1)}) %reduce-scatter.18.cloned.1.call-update) | async-done | bytes 786448 | tf_op jit(solution)/shard_map/reduce_scatter | solution.py:161
  262.4 17.4 %gather_fusion = s32[3072]{0:T(1024)S(1)} fusion(s32[3072]{0:T(1024)S(1)} %reshape.848, s32[3072]{0:T(1024)S(1)} %fusion.92), kind=kCustom, calls=%fused_computation | custom fusion | bytes 36864 | tf_op jit(solution)/shard_map/gather | solution.py:65
  282.4 17.4 %gather_fusion.1 = s32[3072]{0:T(1024)S(1)} fusion(s32[3072]{0:T(1024)S(1)} %get-tuple-element.402, s32[3072]{0:T(1024)S(1)} %get-tuple-element.401), kind=kCustom, calls=%fused_computation.1 | custom fusion | bytes 36864 | tf_op jit(solution)/shard_map/gather | solution.py:68
  311.7 67.9 %all-gather = bf16[32,32,4]{1,2,0:T(4,128)(2,1)S(1)} all-gather(bf16[1,32,4]{1,2,0:T(4,128)(2,1)S(1)} %bitcast.152), channel_id=1, replica_groups=mesh['dp'=8,'tensor'=4] {'dp','tensor'}, dimensions={0}, use_global_device_ids=true | all-gather | bytes 8448 | tf_op jit(solution)/shard_map/all_gather | solution.py:123
  387.5 20.2 %gather_fusion.5 = f32[3840,1024]{1,0:T(8,128)} fusion(f32[1536,1024]{1,0:T(8,128)} %convert_element_type.175, s32[4096]{0:T(1024)S(1)} %pad_clamp_fusion.1), kind=kCustom, calls=%fused_computation.5 | custom fusion | bytes 31472640 | tf_op jit(solution)/shard_map/gather | solution.py:206
  421.2 20.2 %gather_fusion.4 = f32[3840]{0:T(1024)S(1)} fusion(f32[3072]{0:T(1024)S(1)} %reshape.853, s32[4096]{0:T(1024)S(1)} %pad_clamp_fusion), kind=kCustom, calls=%fused_computation.4 | custom fusion | bytes 46080 | tf_op jit(solution)/shard_map/gather | solution.py:205
  442.7 20.2 %gather_fusion.2 = bf16[3840,1024]{1,0:T(8,128)(2,1)} fusion(bf16[1536,1024]{1,0:T(8,128)(2,1)} %all-gather.11.cloned.1.call-done, s32[4096]{0:T(1024)S(1)} %pad_clamp_fusion.1), kind=kCustom, calls=%fused_computation.2 | custom fusion | bytes 15744000 | tf_op jit(solution)/shard_map/gather | solution.py:182
  477.3 37.3 %multiply_convert_fusion.2 = (bf16[4,960,704]{1,2,0:T(8,128)(2,1)}, f32[4,960,704]{1,2,0:T(8,128)}, f32[4,960,704]{1,2,0:T(8,128)}) fusion(f32[4,960,704]{1,2,0:T(8,128)} %get-tuple-element.398, u8[960,704]{0,1:T(8,128)(4,1)S(1)} %get-tuple-element.397, bf16[4,704,1024]{2,1,0:T(8,128)(2,1)} %all-gather.17.cloned.1.call-done, ...), kind=kOutput, calls=%fused_computation.125 | convolution fusion | flops 5730877440 | bytes 60034048 | tf_op jit(solution)/shard_map/ecd,efd->ecf/dot_general | solution.py:209
  514.7 23.1 %add_convert_fusion = (bf16[4,960,704]{1,2,0:T(8,128)(2,1)}, bf16[4,960,704]{1,2,0:T(8,128)(2,1)}) fusion(f32[4,960,704]{1,2,0:T(8,128)} %get-tuple-element.370, f32[4,960,704]{1,2,0:T(8,128)} %get-tuple-element.399, f32[4,960,704]{1,2,0:T(8,128)} %get-tuple-element.398, bf16[4,1024,704]{1,2,0:T(8,128)(2,1)} %all-gather.15.cloned.1.call-done, ...), kind=kOutput, calls=%fused_computation.126 | convolution fusion | flops 5589073920 | bytes 56889088 | tf_op jit(solution)/shard_map/ecd,edf->ecf/dot_general | solution.py:186
  550.3 22.5 %gather_fusion.3 = f32[3072,1024]{1,0:T(8,128)} fusion(f32[3840,1024]{1,0:T(8,128)} %bitcast.125, s32[3072]{0:T(1024)S(1)} %copy-done.34), kind=kCustom, calls=%fused_computation.3 | custom fusion | bytes 25178112 | tf_op jit(solution)/shard_map/gather | solution.py:193
  572.8 15.4 gather.39
  588.2 26.7 %multiply_reduce_fusion.1 = (bf16[1536,2]{1,0:T(8,128)(2,1)S(1)}, bf16[1536,1024]{1,0:T(8,128)(2,1)}) fusion(f32[1536,2,1024]{2,1,0:T(2,128)} %gather.39, f32[1536,1024]{1,0:T(8,128)} %convert_element_type.175, f32[1536,2]{1,0:T(8,128)S(1)} %copy-done.25), kind=kLoop, calls=%fused_computation.119 | loop fusion | flops 11006976 | bytes 22038528 | tf_op jit(solution)/shard_map/reduce_sum | solution.py:204
  629.8 15.5 %convolution_add_fusion = f32[4,960,1024]{2,1,0:T(8,128)} fusion(f32[4,960,1024]{2,1,0:T(8,128)} %fusion.108, bf16[4,960,704]{1,2,0:T(8,128)(2,1)} %get-tuple-element.369, bf16[4,1024,704]{1,2,0:T(8,128)(2,1)} %all-gather.15.cloned.1.call-done), kind=kOutput, calls=%fused_computation.141 | convolution fusion | flops 5540413440 | bytes 42631168 | tf_op jit(solution)/shard_map/ecf,edf->ecd/dot_general | solution.py:216
  645.3 22.5 %gather_fusion.6 = f32[3072,1024]{1,0:T(8,128)} fusion(f32[3840,1024]{1,0:T(8,128)} %bitcast.124, s32[3072]{0:T(1024)S(1)} %copy-done.34), kind=kCustom, calls=%fused_computation.6 | custom fusion | bytes 25178112 | tf_op jit(solution)/shard_map/gather | solution.py:219
  667.8 15.3 gather.45
  683.3 20.7 %select_reduce_fusion = bf16[1536,1024]{1,0:T(8,128)(2,1)} fusion(f32[1536,2,1024]{2,1,0:T(2,128)} %gather.45, pred[1536,2]{1,0:T(8,128)(4,1)S(1)} %copy-done.33), kind=kLoop, calls=%fused_computation.120 | loop fusion | flops 4718592 | bytes 15731712 | tf_op jit(solution)/shard_map/reduce_sum | solution.py:218
  705.2 55.6 %reduce-scatter.22.cloned.1.call-done = bf16[384,1024]{1,0:T(8,128)(2,1)} async-done(((bf16[1536,1024]{1,0:T(8,128)(2,1)}), bf16[384,1024]{1,0:T(8,128)(2,1)}) %reduce-scatter.22.cloned.1.call-update) | async-done | bytes 786448 | tf_op jit(solution)/shard_map/reduce_scatter | solution.py:222
  768.6 61.8 %all-gather.21.cloned.1.call-done = bf16[1536,1024]{1,0:T(8,128)(2,1)} async-done(((bf16[384,1024]{1,0:T(8,128)(2,1)}), bf16[1536,1024]{1,0:T(8,128)(2,1)}) %all-gather.21.cloned.1.call-update) | async-done | bytes 3145744 | tf_op jit(solution)/shard_map/all_gather | solution.py:236
  837.0 134.9 %while.35 = (s32[]{:T(128)}, f32[1536,4,64]{0,2,1:T(8,128)}, f32[1536,4,64]{0,2,1:T(8,128)}, bf16[3,512,4,64]{1,3,2,0:T(8,128)(2,1)}, s32[3]{0:T(128)S(1)}, /*in...) while((s32[]{:T(128)}, f32[1536,4,64]{0,2,1:T(8,128)}, ...), condition=%wide.region_26.27_spmd, body=%wide.region_24.26_spmd.sunk | while | flops 2054726656 | bytes 156601328 | solution.py:269
  1012.4 15.5 %fusion.64 = f32[4,1024,704]{1,2,0:T(8,128)} fusion(bf16[4,960,704]{1,2,0:T(8,128)(2,1)} %get-tuple-element.387, bf16[4,960,1024]{2,1,0:T(8,128)(2,1)} %bitcast.133, pred[4,960]{1,0:T(4,128)(4,1)S(1)} %copy-done.63), kind=kOutput, calls=%fused_computation.144 | convolution fusion | flops 5540413440 | bytes 24809216 | tf_op jit(solution)/shard_map/ecd,ecf->edf/dot_general | solution.py:212
  1028.0 15.4 %fusion.65 = f32[4,1024,704]{1,2,0:T(8,128)} fusion(bf16[4,960,704]{1,2,0:T(8,128)(2,1)} %get-tuple-element.369, bf16[4,960,1024]{2,1,0:T(8,128)(2,1)} %bitcast.134, pred[4,960]{1,0:T(4,128)(4,1)S(1)} %copy-done.63), kind=kOutput, calls=%fused_computation.145 | convolution fusion | flops 5540413440 | bytes 24809216 | tf_op jit(solution)/shard_map/ecd,ecf->edf/dot_general | solution.py:213
  1046.8 44.0 %all-reduce.4 = (f32[1024]{0:T(1024)S(1)}, f32[1024]{0:T(1024)S(1)}) all-reduce(f32[1024]{0:T(1024)S(1)} %get-tuple-element.329, f32[1024]{0:T(1024)S(1)} %copy-done.67), channel_id=7, replica_groups=mesh['dp'=8,'tensor'=4] {'dp','tensor'}, use_global_device_ids=true, to_apply=%region_30.31.clone | all-reduce | flops 2048 | bytes 16384
  1107.6 35.3 %reduce-scatter.32.cloned.1.call-done = f32[256,128]{1,0:T(8,128)} async-done(((f32[256,1024]{1,0:T(8,128)}), f32[256,128]{1,0:T(8,128)}) %reduce-scatter.32.cloned.1.call-update) | async-done | bytes 131088 | tf_op jit(solution)/shard_map/reduce_scatter | solution.py:285
  1143.0 39.7 %reduce-scatter.26.cloned.1.call-done = f32[128,256]{1,0:T(8,128)} async-done(((f32[1024,256]{1,0:T(8,128)}), f32[128,256]{1,0:T(8,128)}) %reduce-scatter.26.cloned.1.call-update) | async-done | bytes 131088 | tf_op jit(solution)/shard_map/reduce_scatter | solution.py:282
  1182.6 39.6 %reduce-scatter.28.cloned.1.call-done = f32[128,256]{1,0:T(8,128)} async-done(((f32[1024,256]{1,0:T(8,128)}), f32[128,256]{1,0:T(8,128)}) %reduce-scatter.28.cloned.1.call-update) | async-done | bytes 131088 | tf_op jit(solution)/shard_map/reduce_scatter | solution.py:283
  1222.3 39.7 %reduce-scatter.30.cloned.1.call-done = f32[128,256]{1,0:T(8,128)} async-done(((f32[1024,256]{1,0:T(8,128)}), f32[128,256]{1,0:T(8,128)}) %reduce-scatter.30.cloned.1.call-update) | async-done | bytes 131088 | tf_op jit(solution)/shard_map/reduce_scatter | solution.py:284
  1261.9 90.7 %reduce-scatter.38.cloned.1.call-done = f32[4,704,128]{2,1,0:T(8,128)} async-done(((f32[4,704,1024]{2,1,0:T(8,128)}), f32[4,704,128]{2,1,0:T(8,128)}) %reduce-scatter.38.cloned.1.call-update) | async-done | bytes 1441808 | tf_op jit(solution)/shard_map/reduce_scatter | solution.py:281
  1352.6 90.9 %reduce-scatter.34.cloned.1.call-done = f32[4,128,704]{1,2,0:T(8,128)} async-done(((f32[4,1024,704]{1,2,0:T(8,128)}), f32[4,128,704]{1,2,0:T(8,128)}) %reduce-scatter.34.cloned.1.call-update) | async-done | bytes 1441808 | tf_op jit(solution)/shard_map/reduce_scatter | solution.py:279
  1443.5 90.7 %reduce-scatter.36.cloned.1.call-done = f32[4,128,704]{1,2,0:T(8,128)} async-done(((f32[4,1024,704]{1,2,0:T(8,128)}), f32[4,128,704]{1,2,0:T(8,128)}) %reduce-scatter.36.cloned.1.call-update) | async-done | bytes 1441808 | tf_op jit(solution)/shard_map/reduce_scatter | solution.py:280
  (458 shorter events, 409.3 us)
Async XLA Ops:
  7.2 111.4 %all-gather.9.cloned.1.call-start = ((), (), s32[]{:S(2)}) async-start(), calls=%async_computation.13 | async-start | bytes 3932160 | tf_op jit(solution)/shard_map/all_gather | solution.py:130
  55.2 187.9 %reduce-scatter.18.cloned.1.call-start = ((), (), s32[]{:S(2)}) async-start(), calls=%async_computation.14 | async-start | bytes 3932160 | tf_op jit(solution)/shard_map/reduce_scatter | solution.py:161
  184.0 197.6 %all-gather.19.cloned.1.call-start = ((), (), s32[]{:S(2)}) async-start(), calls=%async_computation.20 | async-start | bytes 3932160 | tf_op jit(solution)/shard_map/all_gather | solution.py:201
  184.7 257.9 %all-gather.11.cloned.1.call-start = ((), (), s32[]{:S(2)}) async-start(), calls=%async_computation.15 | async-start | bytes 3932160 | tf_op jit(solution)/shard_map/all_gather | solution.py:173
  184.8 95.0 %copy-start.39 = (f32[1024]{0:T(1024)}, f32[1024]{0:T(1024)S(1)}, u32[]{:S(2)}) copy-start(f32[1024]{0:T(1024)S(1)} %convert_element_type.164) | copy-start | bytes 12292
  247.5 215.3 %all-gather.13.cloned.1.call-start = ((), (), s32[]{:S(2)}) async-start(), calls=%async_computation.16 | async-start | bytes 6488064 | tf_op jit(solution)/shard_map/all_gather | solution.py:91
  248.1 229.2 %all-gather.17.cloned.1.call-start = ((), (), s32[]{:S(2)}) async-start(), calls=%async_computation.18 | async-start | bytes 6488064 | tf_op jit(solution)/shard_map/all_gather | solution.py:93
  248.7 266.0 %all-gather.15.cloned.1.call-start = ((), (), s32[]{:S(2)}) async-start(), calls=%async_computation.17 | async-start | bytes 6488064 | tf_op jit(solution)/shard_map/all_gather | solution.py:92
  249.4 454.6 %reduce-scatter.40.cloned.1.call-start = ((), (), s32[]{:S(2)}) async-start(), calls=%async_computation.31 | async-start | bytes 491520
  379.9 134.8 %copy-start.62 = (pred[4,960]{1,0:T(4,128)(4,1)}, pred[4,960]{1,0:T(4,128)(4,1)S(1)}, u32[]{:S(2)}) copy-start(pred[4,960]{1,0:T(4,128)(4,1)S(1)} %lt.151) | copy-start | bytes 11524
  616.1 144.8 %reduce-scatter.22.cloned.1.call-start = ((), (), s32[]{:S(2)}) async-start(), calls=%async_computation.21 | async-start | bytes 3932160 | tf_op jit(solution)/shard_map/reduce_scatter | solution.py:222
  683.2 77.7 %copy-start.15 = (bf16[384,1024]{1,0:T(8,128)(2,1)S(1)}, bf16[384,1024]{1,0:T(8,128)(2,1)}, u32[]{:S(2)}) copy-start(bf16[384,1024]{1,0:T(8,128)(2,1)} %param.22) | copy-start | bytes 2359300
  683.2 77.7 %copy-start.19 = (bf16[384,1024]{1,0:T(8,128)(2,1)S(1)}, bf16[384,1024]{1,0:T(8,128)(2,1)}, u32[]{:S(2)}) copy-start(bf16[384,1024]{1,0:T(8,128)(2,1)} %reduce-scatter.18.cloned.1.call-done) | copy-start | bytes 2359300
  683.2 77.7 %copy-start.40 = (f32[1024]{0:T(1024)S(1)}, f32[1024]{0:T(1024)}, u32[]{:S(2)}) copy-start(f32[1024]{0:T(1024)} %copy-done.39) | copy-start | bytes 12292
  683.2 77.7 %copy-start.46 = (f32[384,4]{0,1:T(4,128)S(1)}, f32[384,4]{0,1:T(4,128)}, u32[]{:S(2)}) copy-start(f32[384,4]{0,1:T(4,128)} %copy-done.45) | copy-start | bytes 18436
  683.2 77.6 %copy-start.48 = (bf16[1024,4]{0,1:T(4,128)(2,1)S(1)}, bf16[1024,4]{0,1:T(4,128)(2,1)}, u32[]{:S(2)}) copy-start(bf16[1024,4]{0,1:T(4,128)(2,1)} %copy-done.47) | copy-start | bytes 24580
  683.2 77.6 %copy-start.54 = (f32[384]{0:T(512)S(1)}, f32[384]{0:T(512)}, u32[]{:S(2)}) copy-start(f32[384]{0:T(512)} %copy-done.53) | copy-start | bytes 4612
  704.0 126.5 %all-gather.21.cloned.1.call-start = ((), (), s32[]{:S(2)}) async-start(), calls=%async_computation.22 | async-start | bytes 3932160 | tf_op jit(solution)/shard_map/all_gather | solution.py:236
  764.1 70.2 %copy-start.60 = (f32[384]{0:T(512)}, f32[384]{0:T(512)S(1)}, u32[]{:S(2)}) copy-start(f32[384]{0:T(512)S(1)} %broadcast_multiply_fusion.2) | copy-start | bytes 4612
  766.7 70.3 %copy-start.2 = (bf16[1536,4,64]{0,2,1:T(8,128)(2,1)S(1)}, bf16[1536,4,64]{0,2,1:T(8,128)(2,1)}, u32[]{:S(2)}) copy-start(bf16[1536,4,64]{0,2,1:T(8,128)(2,1)} %copy-done.1) | copy-start | bytes 2359300
  766.7 70.3 %copy-start.5 = (bf16[1536,4,64]{0,2,1:T(8,128)(2,1)S(1)}, bf16[1536,4,64]{0,2,1:T(8,128)(2,1)}, u32[]{:S(2)}) copy-start(bf16[1536,4,64]{0,2,1:T(8,128)(2,1)} %copy-done.4) | copy-start | bytes 2359300
  766.7 70.3 %copy-start.72 = (s32[3]{0:T(128)S(1)}, s32[3]{0:T(128)}, u32[]{:S(2)}) copy-start(s32[3]{0:T(128)} %copy-done.71) | copy-start | bytes 40
  766.8 276.8 %reduce-scatter.42.cloned.1.call-start = ((), (), s32[]{:S(2)}) async-start(), calls=%async_computation.32 | async-start | bytes 540672
  768.6 276.4 %reduce-scatter.24.cloned.1.call-start = ((), (), s32[]{:S(2)}) async-start(), calls=%async_computation.23 | async-start | bytes 3932160 | tf_op jit(solution)/shard_map/reduce_scatter | solution.py:290
  980.6 122.7 %reduce-scatter.20.cloned.1.call-start = ((), (), s32[]{:S(2)}) async-start(), calls=%async_computation.19 | async-start | bytes 3932160 | tf_op jit(solution)/shard_map/reduce_scatter | solution.py:197
  981.3 161.7 %reduce-scatter.32.cloned.1.call-start = ((), (), s32[]{:S(2)}) async-start(), calls=%async_computation.27 | async-start | bytes 1179648 | tf_op jit(solution)/shard_map/reduce_scatter | solution.py:285
  985.6 197.1 %reduce-scatter.26.cloned.1.call-start = ((), (), s32[]{:S(2)}) async-start(), calls=%async_computation.24 | async-start | bytes 1179648 | tf_op jit(solution)/shard_map/reduce_scatter | solution.py:282
  989.6 232.7 %reduce-scatter.28.cloned.1.call-start = ((), (), s32[]{:S(2)}) async-start(), calls=%async_computation.25 | async-start | bytes 1179648 | tf_op jit(solution)/shard_map/reduce_scatter | solution.py:283
  993.6 268.3 %reduce-scatter.30.cloned.1.call-start = ((), (), s32[]{:S(2)}) async-start(), calls=%async_computation.26 | async-start | bytes 1179648 | tf_op jit(solution)/shard_map/reduce_scatter | solution.py:284
  997.6 355.1 %reduce-scatter.38.cloned.1.call-start = ((), (), s32[]{:S(2)}) async-start(), calls=%async_computation.30 | async-start | bytes 12976128 | tf_op jit(solution)/shard_map/reduce_scatter | solution.py:281
  1011.8 431.8 %reduce-scatter.34.cloned.1.call-start = ((), (), s32[]{:S(2)}) async-start(), calls=%async_computation.28 | async-start | bytes 12976128 | tf_op jit(solution)/shard_map/reduce_scatter | solution.py:279
  1027.9 506.4 %reduce-scatter.36.cloned.1.call-start = ((), (), s32[]{:S(2)}) async-start(), calls=%async_computation.29 | async-start | bytes 12976128 | tf_op jit(solution)/shard_map/reduce_scatter | solution.py:280
  (77 other events, 1560.8 us)
Sparse Core Ops, SparseCore 0:
  55.3 63.2 all-gather.8
  184.1 58.8 reduce-scatter.17
  244.6 63.5 all-gather.18
  310.2 62.3 all-gather.10
  374.3 43.1 all-gather.12
  419.3 44.3 all-gather.16
  465.6 44.3 all-gather.14
  616.2 17.1 reduce-scatter.39
  704.1 56.7 reduce-scatter.21
  766.9 63.5 all-gather.20
  832.8 132.7 reduce-scatter.41
  980.7 58.8 reduce-scatter.23
  1041.9 61.3 reduce-scatter.19
  1106.9 36.0 reduce-scatter.31
  1146.6 36.0 reduce-scatter.25
  1186.2 35.9 reduce-scatter.27
  1225.9 36.0 reduce-scatter.29
  1265.9 86.7 reduce-scatter.37
  1356.7 86.7 reduce-scatter.33
  1447.5 86.7 reduce-scatter.35
where the time goes:
time: 1550 us; the launch traced here: 1540 us
  waiting for transfers between devices  639 us (41%)
  matrix products  287 us (19%)
  local copies, waits for them, and re-layouts  255 us (16%)
  blocking collectives  207 us (13%)
  other arithmetic  123 us (8%)
  between operations  15.8 us (1%)
    reduce_scatter x1, waiting for transfers between devices, on_device(): lax.psum_scatter(grad_wg, 'dp', scatter_dimension=1, tiled=True)  90.9 us
    reduce_scatter x1, waiting for transfers between devices, on_device(): lax.psum_scatter(grad_wu, 'dp', scatter_dimension=1, tiled=True)  90.7 us
    reduce_scatter x1, waiting for transfers between devices, on_device(): lax.psum_scatter(grad_down, 'dp', scatter_dimension=2, tiled=True)  90.7 us
    unnamed x2, blocking collectives  86.1 us
    all_gather x1, blocking collectives, on_device(): lax.all_gather(router, ('dp', 'tensor'), axis=0, tiled=True)  67.9 us
    all_gather x1, waiting for transfers between devices, on_device(): lax.all_gather(grad_middle.astype(b16), 'tensor', axis=0, tiled=True)  61.8 us
    reduce_scatter x1, waiting for transfers between devices, on_device(): lax.psum_scatter(attn_part.astype(jnp.bfloat16), 'tensor', scatter_dimens...  58.3 us
    reduce_scatter x1, waiting for transfers between devices, on_device(): lax.psum_scatter(grad_mixed_part.astype(jnp.bfloat16), 'tensor', scatter_...  55.6 us
  transfers between devices with their start and end apart: 20, of which 12 were waited for; matrix products, arithmetic and copies ran while one was open for 31% of the time, Pallas kernels for 0%

commit v1 on v0

v1 whole, which is shorter than its diff:
```python
import jax
import jax.numpy as jnp
from jax import lax
from jax.experimental import pallas as pl
from jax.experimental.pallas import tpu as pltpu
from jax.sharding import PartitionSpec as P

HEAD_DIM = 64
PROMPT = 1024
CONT = 128
CAPACITY = 960
EPS = 1e-06
PAIR = 2 * HEAD_DIM
MIB = 2**20

f32 = jnp.float32
b16 = jnp.bfloat16
NN = (((1,), (0,)), ((), ()))
NT = (((1,), (1,)), ((), ()))
TN = (((0,), (0,)), ((), ()))
INV_SQRT2 = 0.7071067811865476
INV_SQRT_2PI = 0.3989422804014327
MASKED = -1e30


def dot(left, right, dims):
    return lax.dot_general(left, right, dims, preferred_element_type=f32)


def params(mib):
    return pltpu.CompilerParams(vmem_limit_bytes=mib * MIB)


def whole(*_):
    return (0, 0)


def unit_of(values):
    scale = lax.rsqrt(jnp.mean(values * values, -1, keepdims=True) + EPS)
    return values * scale, scale


def keep_mask(ids, order, experts):
    rows = ids.shape[1]
    pairs = ids.shape[0] * rows
    bits = pairs.bit_length()

    def body(ids_ref, order_ref, keep_ref):
        ids_v = ids_ref[...]
        order_v = order_ref[...]
        sub = lax.broadcasted_iota(jnp.int32, (128, rows), 0)
        out = jnp.zeros((128, rows), f32)
        for expert in range(experts):
            mine = ids_v == expert
            bound = jnp.zeros((1, 1), jnp.int32)
            for bit in range(bits - 1, -1, -1):
                trial = bound + (1 << bit)
                inside = jnp.where(mine & (order_v < trial), 1.0, 0.0)
                count = jnp.sum(jnp.sum(inside, 1, keepdims=True), 0, keepdims=True)
                bound = jnp.where(count <= CAPACITY, trial, bound)
            kept = jnp.sum(jnp.where(mine & (order_v < bound), 1.0, 0.0), 0, keepdims=True)
            out = jnp.where((sub < 2 * experts) & (sub % experts == expert), kept, out)
        keep_ref[...] = jnp.transpose(out)

    return pl.pallas_call(
        body,
        out_shape=jax.ShapeDtypeStruct((rows, 128), f32),
        compiler_params=params(32),
    )(ids, order)


def attention_forward(at, slots, gains, weights):
    rows, width = slots[0].shape
    groups, _, _, cols = weights.shape
    tall = PROMPT + rows
    subs = rows // CONT
    pairs = cols // PAIR
    keys = PROMPT + CONT

    def body(at_ref, x0, x1, x2, x3, gain_ref, w_ref, a_ref, q_ref, k_ref, v_ref, p_ref, c_ref, h_ref, b_ref, xs, acc):
        step = pl.program_id(0)
        t = at_ref[0]

        @pl.when(step == 0)
        def _():
            for s, x in enumerate((x0, x1, x2, x3)):
                xs[s * rows : (s + 1) * rows] = x[...]
            gain = gain_ref[0:1]
            for start in range(0, PROMPT, rows):
                take = min(rows, PROMPT - start)
                slot = jnp.maximum(t - start // rows, 0)
                x = xs[pl.ds(pl.multiple_of(slot * rows, 128), take)].astype(f32)
                a_ref[start : start + take] = (unit_of(x)[0] * gain).astype(b16)
            a_ref[PROMPT:tall] = (unit_of(x0[...].astype(f32))[0] * gain).astype(b16)

        a = a_ref[...]
        q = dot(a_ref[PROMPT:tall], w_ref[0, 0], NN).astype(b16) * jnp.asarray(0.125, b16)
        k = dot(a, w_ref[0, 1], NN).astype(b16)
        v = dot(a, w_ref[0, 2], NN).astype(b16)
        q_ref[...] = q
        k_ref[...] = k
        v_ref[...] = v
        low = lax.broadcasted_iota(jnp.int32, (CONT, PAIR), 1) < HEAD_DIM
        row = lax.broadcasted_iota(jnp.int32, (2 * CONT, PROMPT), 0) % CONT
        col = lax.broadcasted_iota(jnp.int32, (2 * CONT, PROMPT), 1)
        own_ok = lax.broadcasted_iota(jnp.int32, (2 * CONT, CONT), 1) <= (
            lax.broadcasted_iota(jnp.int32, (2 * CONT, CONT), 0) % CONT
        )
        zero = jnp.zeros((), b16)
        for pair in range(pairs):
            lanes = slice(pair * PAIR, (pair + 1) * PAIR)
            kp, vp = k[:PROMPT, lanes], v[:PROMPT, lanes]
            for sub in range(subs):
                own = slice(PROMPT + sub * CONT, PROMPT + (sub + 1) * CONT)
                q2 = q[sub * CONT : (sub + 1) * CONT, lanes]
                qs = jnp.concatenate([jnp.where(low, q2, zero), jnp.where(low, zero, q2)], 0)
                first = t * rows + sub * CONT
                s1 = jnp.where(col <= row + first, dot(qs, kp, NT), MASKED)
                s2 = jnp.where(own_ok & (first >= PROMPT), dot(qs, k[own, lanes], NT), MASKED)
                top = jnp.maximum(jnp.max(s1, -1, keepdims=True), jnp.max(s2, -1, keepdims=True))
                e1 = jnp.exp(s1 - top)
                e2 = jnp.exp(s2 - top)
                inv = 1.0 / (jnp.sum(e1, -1, keepdims=True) + jnp.sum(e2, -1, keepdims=True))
                p1 = (e1 * inv).astype(b16)
                p2 = (e2 * inv).astype(b16)
                at_p = slice((pair * subs + sub) * 2 * CONT, (pair * subs + sub + 1) * 2 * CONT)
                p_ref[0, at_p, :PROMPT] = p1
                p_ref[0, at_p, PROMPT:] = p2
                c2 = dot(p1, vp, NN) + dot(p2, v[own, lanes], NN)
                c_ref[sub * CONT : (sub + 1) * CONT, lanes] = jnp.where(low, c2[:CONT], c2[CONT:]).astype(b16)
        out = dot(c_ref[...], w_ref[0, 3], NT)

        @pl.when(step == 0)
        def _():
            acc[...] = out

        @pl.when(step > 0)
        def _():
            acc[...] += out

        @pl.when(step == groups - 1)
        def _():
            h = x0[...].astype(f32) + acc[...]
            h_ref[...] = h
            b_ref[...] = (unit_of(h)[0] * gain_ref[1:2]).astype(b16)

    def by_group(i, at):
        return (0, i)

    return pl.pallas_call(
        body,
        grid_spec=pltpu.PrefetchScalarGridSpec(
            num_scalar_prefetch=1,
            grid=(groups,),
            in_specs=[pl.BlockSpec((rows, width), whole)] * 4
            + [
                pl.BlockSpec(gains.shape, whole),
                pl.BlockSpec((1, 4, width, cols), lambda i, at: (i, 0, 0, 0)),
            ],
            out_specs=[
                pl.BlockSpec((tall, width), whole),
                pl.BlockSpec((rows, cols), by_group),
                pl.BlockSpec((tall, cols), by_group),
                pl.BlockSpec((tall, cols), by_group),
                pl.BlockSpec((1, 2 * pairs * rows, keys), lambda i, at: (i, 0, 0)),
                pl.BlockSpec((rows, cols), by_group),
                pl.BlockSpec((rows, width), whole),
                pl.BlockSpec((rows, width), whole),
            ],
            scratch_shapes=[pltpu.VMEM((4 * rows, width), b16), pltpu.VMEM((rows, width), f32)],
        ),
        out_shape=[
            jax.ShapeDtypeStruct((tall, width), b16),
            jax.ShapeDtypeStruct((rows, width), b16),
            jax.ShapeDtypeStruct((tall, width), b16),
            jax.ShapeDtypeStruct((tall, width), b16),
            jax.ShapeDtypeStruct((groups, 2 * pairs * rows, keys), b16),
            jax.ShapeDtypeStruct((rows, width), b16),
            jax.ShapeDtypeStruct((rows, width), f32),
            jax.ShapeDtypeStruct((rows, width), b16),
        ],
        compiler_params=params(56),
        cost_estimate=pl.CostEstimate(
            flops=2 * width * width * (2 * tall + 2 * rows) + 8 * rows * keys * width,
            bytes_accessed=60 * MIB,
            transcendentals=rows * keys * 16,
        ),
    )(at, *slots, gains, weights)


def attention_backward(at, h, dy, parts, gains, a, q, k, v, p, c, weights):
    rows, width = h.shape
    groups, _, _, cols = weights.shape
    tall = PROMPT + rows
    padded = -(-PROMPT // rows) * rows
    subs = rows // CONT
    pairs = cols // PAIR
    keys = PROMPT + CONT

    def body(at_ref, h_ref, dy_ref, d0, d1, d2, d3, gain_ref, a_ref, q_ref, k_ref, v_ref, p_ref, c_ref, w_ref, dw_ref, dap_ref, dao_ref, dh_ref, sum_ref, do, acc, ds, dqs):
        step = pl.program_id(0)

        @pl.when(step == 0)
        def _():
            dn = (d0[...].astype(f32) + d1[...].astype(f32)) + (d2[...].astype(f32) + d3[...].astype(f32))
            gain = gain_ref[1:2]
            unit, scale = unit_of(h_ref[...])
            along = dn * gain
            inner = jnp.mean(along * unit, -1, keepdims=True)
            dh = dy_ref[...].astype(f32) + scale * (along - unit * inner)
            dh_ref[...] = dh
            do[...] = dh.astype(b16)
            sum_ref[...] = jnp.zeros_like(sum_ref)
            sum_ref[1:2] = jnp.sum(dn * unit, 0, keepdims=True)

        low = lax.broadcasted_iota(jnp.int32, (CONT, PAIR), 1) < HEAD_DIM
        zero = jnp.zeros((), b16)

        def stacked(two):
            return jnp.concatenate([jnp.where(low, two, zero), jnp.where(low, zero, two)], 0)

        dc = dot(do[...], w_ref[0, 3], NN).astype(b16)
        dw_ref[0, 3] = dot(do[...], c_ref[...], TN).astype(b16)
        dks, dvs = [], []
        for pair in range(pairs):
            lanes = slice(pair * PAIR, (pair + 1) * PAIR)
            kp, vp = k_ref[:PROMPT, lanes], v_ref[:PROMPT, lanes]
            qall, dcall, dko, dvo = [], [], [], []
            for sub in range(subs):
                own = slice(PROMPT + sub * CONT, PROMPT + (sub + 1) * CONT)
                mine = slice(sub * CONT, (sub + 1) * CONT)
                at_p = slice((pair * subs + sub) * 2 * CONT, (pair * subs + sub + 1) * 2 * CONT)
                dcs = stacked(dc[mine, lanes])
                qs = stacked(q_ref[mine, lanes])
                cs = stacked(c_ref[mine, lanes])
                delta = jnp.sum(dcs.astype(f32) * cs.astype(f32), -1, keepdims=True)
                p1 = p_ref[0, at_p, :PROMPT]
                p2 = p_ref[0, at_p, PROMPT:]
                ds1 = (p1.astype(f32) * (dot(dcs, vp, NT) - delta)).astype(b16)
                ds2 = (p2.astype(f32) * (dot(dcs, v_ref[own, lanes], NT) - delta)).astype(b16)
                ds[sub * 2 * CONT : (sub + 1) * 2 * CONT] = ds1
                dq2 = (dot(ds1, kp, NN) + dot(ds2, k_ref[own, lanes], NN)) * 0.125
                dqs[mine, lanes] = jnp.where(low, dq2[:CONT], dq2[CONT:]).astype(b16)
                dko.append(dot(ds2, qs, TN).astype(b16))
                dvo.append(dot(p2, dcs, TN).astype(b16))
                qall.append(qs)
                dcall.append(dcs)
            span = slice(pair * 2 * rows, (pair + 1) * 2 * rows)
            dkp = dot(ds[...], jnp.concatenate(qall, 0), TN).astype(b16)
            dvp = dot(p_ref[0, span, :PROMPT], jnp.concatenate(dcall, 0), TN).astype(b16)
            dks.append(jnp.concatenate([dkp] + dko, 0))
            dvs.append(jnp.concatenate([dvp] + dvo, 0))
        dk = jnp.concatenate(dks, 1)
        dv = jnp.concatenate(dvs, 1)
        dq = dqs[...]
        dw_ref[0, 0] = dot(a_ref[PROMPT:tall], dq, TN).astype(b16)
        dw_ref[0, 1] = dot(a_ref[...], dk, TN).astype(b16)
        dw_ref[0, 2] = dot(a_ref[...], dv, TN).astype(b16)
        terms = dot(dk, w_ref[0, 1], NT) + dot(dv, w_ref[0, 2], NT)
        own_terms = terms[PROMPT:] + dot(dq, w_ref[0, 0], NT)

        @pl.when(step == 0)
        def _():
            acc[:PROMPT] = terms[:PROMPT]
            acc[PROMPT:] = own_terms

        @pl.when(step > 0)
        def _():
            acc[:PROMPT] += terms[:PROMPT]
            acc[PROMPT:] += own_terms

        @pl.when(step == groups - 1)
        def _():
            dap_ref[:PROMPT] = acc[:PROMPT].astype(b16)
            if padded > PROMPT:
                dap_ref[PROMPT:] = jnp.zeros((padded - PROMPT, width), b16)
            dao_ref[...] = acc[PROMPT:]
            total = jnp.sum(acc[...] * a_ref[...].astype(f32), 0, keepdims=True)
            sum_ref[0:1] = total / gain_ref[0:1]

    def by_group(i, at):
        return (0, i)

    return pl.pallas_call(
        body,
        grid_spec=pltpu.PrefetchScalarGridSpec(
            num_scalar_prefetch=1,
            grid=(groups,),
            in_specs=[pl.BlockSpec((rows, width), whole)] * 6
            + [
                pl.BlockSpec(gains.shape, whole),
                pl.BlockSpec((tall, width), whole),
                pl.BlockSpec((rows, cols), by_group),
                pl.BlockSpec((tall, cols), by_group),
                pl.BlockSpec((tall, cols), by_group),
                pl.BlockSpec((1, 2 * pairs * rows, keys), lambda i, at: (i, 0, 0)),
                pl.BlockSpec((rows, cols), by_group),
                pl.BlockSpec((1, 4, width, cols), lambda i, at: (i, 0, 0, 0)),
            ],
            out_specs=[
                pl.BlockSpec((1, 4, width, cols), lambda i, at: (i, 0, 0, 0)),
                pl.BlockSpec((padded, width), whole),
                pl.BlockSpec((rows, width), whole),
                pl.BlockSpec((rows, width), whole),
                pl.BlockSpec((8, width), whole),
            ],
            scratch_shapes=[
                pltpu.VMEM((rows, width), b16),
                pltpu.VMEM((tall, width), f32),
                pltpu.VMEM((2 * rows, PROMPT), b16),
                pltpu.VMEM((rows, cols), b16),
            ],
        ),
        out_shape=[
            jax.ShapeDtypeStruct(weights.shape, b16),
            jax.ShapeDtypeStruct((padded, width), b16),
            jax.ShapeDtypeStruct((rows, width), f32),
            jax.ShapeDtypeStruct((rows, width), f32),
            jax.ShapeDtypeStruct((8, width), f32),
        ],
        compiler_params=params(60),
        cost_estimate=pl.CostEstimate(
            flops=4 * width * width * (2 * tall + 2 * rows) + 16 * rows * keys * width,
            bytes_accessed=80 * MIB,
            transcendentals=0,
        ),
    )(at, h, dy, *parts, gains, a, q, k, v, p, c, weights)


def experts_block(block, b, dy, keep, router, wg, wu, wd, experts):
    rows, width = b.shape
    units = wg.shape[0]
    own = units // experts
    chunk = 256
    steps = units // chunk

    def body(block_ref, b_ref, dy_ref, keep_ref, r_ref, wg_ref, wu_ref, wd_ref, y_ref, db_ref, rg_ref, z_ref, dg_ref, du_ref, gates, probs, dgates, y_acc, db_acc):
        i = pl.program_id(0)
        lane = lax.broadcasted_iota(jnp.int32, (rows, 128), 1)
        b_v = b_ref[...]
        dy_v = dy_ref[...]

        @pl.when(i == 0)
        def _():
            logits = dot(b_v, r_ref[...], NN)
            live = lane < experts
            top = jnp.max(jnp.where(live, logits, MASKED), -1, keepdims=True)
            grown = jnp.exp(jnp.where(lane < 2 * experts, logits, MASKED) - top)
            share = grown / jnp.sum(jnp.where(live, grown, 0.0), -1, keepdims=True)
            probs[...] = share
            gates[...] = share.astype(b16).astype(f32) * keep_ref[...]
            dgates[...] = jnp.zeros_like(dgates)

        g = dot(b_v, wg_ref[...], NT)
        u = dot(b_v, wu_ref[...], NT)
        dz_plain = dot(dy_v, wd_ref[...], NT)
        first = (i * chunk) // own
        last = (i * chunk + chunk - 1) // own
        gate_v = gates[...]
        gate_a = jnp.sum(jnp.where(lane == first, gate_v, 0.0), -1, keepdims=True)
        gate_b = jnp.sum(jnp.where(lane == last, gate_v, 0.0), -1, keepdims=True)
        is_a = lax.broadcasted_iota(jnp.int32, (rows, chunk), 1) < (first + 1) * own - i * chunk
        gate = jnp.where(is_a, gate_a, gate_b)
        cdf = 0.5 * (1.0 + lax.erf(g * INV_SQRT2))
        act = g * cdf
        z = (act * u).astype(b16).astype(f32)
        along = dz_plain * z
        all_sum = jnp.sum(along, -1, keepdims=True)
        a_sum = jnp.sum(jnp.where(is_a, along, 0.0), -1, keepdims=True)
        dgates[...] += jnp.where(lane % experts == first, a_sum, 0.0) + jnp.where(lane % experts == last, all_sum - a_sum, 0.0)
        dz = dz_plain * gate
        pdf = INV_SQRT_2PI * jnp.exp(-0.5 * g * g)
        dg = (dz * u * (cdf + g * pdf)).astype(b16)
        du = (dz * act).astype(b16)
        zg = (z * gate).astype(b16)
        z_ref[...] = zg
        dg_ref[...] = dg
        du_ref[...] = du
        y = dot(zg, wd_ref[...], NN)
        db = dot(dg, wg_ref[...], NN) + dot(du, wu_ref[...], NN)

        @pl.when(i == 0)
        def _():
            y_acc[...] = y
            db_acc[...] = db

        @pl.when(i > 0)
        def _():
            y_acc[...] += y
            db_acc[...] += db

        @pl.when(i == steps - 1)
        def _():
            share = probs[...]
            dprob = dgates[...] * keep_ref[...]
            inner = jnp.sum(jnp.where(lane < experts, share * dprob, 0.0), -1, keepdims=True)
            dl = jnp.where(lane < 2 * experts, share * (dprob - inner), 0.0)
            head = dl.astype(b16).astype(f32)
            split = jnp.where(lane < experts, head, dl - head).astype(b16)
            rg_ref[...] = dot(b_v, split, TN)
            y_ref[...] = y_acc[...].astype(b16)
            db_ref[...] = (db_acc[...] + dot(split, r_ref[...], NT)).astype(b16)

    weight = pl.BlockSpec((chunk, width), lambda i, at: (i, 0))
    hidden = pl.BlockSpec((rows, chunk), lambda i, at: (0, i))
    return pl.pallas_call(
        body,
        grid_spec=pltpu.PrefetchScalarGridSpec(
            num_scalar_prefetch=1,
            grid=(steps,),
            in_specs=[
                pl.BlockSpec((rows, width), whole),
                pl.BlockSpec((rows, width), whole),
                pl.BlockSpec((rows, 128), lambda i, at: (at[0], 0)),
                pl.BlockSpec((width, 128), whole),
                weight,
                weight,
                weight,
            ],
            out_specs=[
                pl.BlockSpec((rows, width), whole),
                pl.BlockSpec((rows, width), whole),
                pl.BlockSpec((width, 128), whole),
                hidden,
                hidden,
                hidden,
            ],
            scratch_shapes=[pltpu.VMEM((rows, 128), f32)] * 3 + [pltpu.VMEM((rows, width), f32)] * 2,
        ),
        out_shape=[
            jax.ShapeDtypeStruct((rows, width), b16),
            jax.ShapeDtypeStruct((rows, width), b16),
            jax.ShapeDtypeStruct((width, 128), f32),
        ]
        + [jax.ShapeDtypeStruct((rows, units), b16)] * 3,
        compiler_params=params(48),
        cost_estimate=pl.CostEstimate(
            flops=12 * rows * width * units,
            bytes_accessed=6 * units * width + 6 * rows * units,
            transcendentals=2 * rows * units,
        ),
    )(block, b, dy, keep, router, wg, wu, wd)


def experts_weights(bs, dys, zs, dgs, dus, parts):
    slots = len(bs)
    rows, width = bs[0].shape
    units = zs[0].shape[1]
    chunk = 256
    cut = width // parts

    def body(*refs):
        b_refs, dy_refs, z, dg, du = (refs[n * slots : (n + 1) * slots] for n in range(5))
        out_g, out_u, out_d, b_all, dy_all = refs[5 * slots :]

        @pl.when(pl.program_id(0) == 0)
        def _():
            for s in range(slots):
                b_all[s * rows : (s + 1) * rows] = b_refs[s][...]
                dy_all[s * rows : (s + 1) * rows] = dy_refs[s][...]

        for left, right, out in ((dg, b_all, out_g), (du, b_all, out_u), (z, dy_all, out_d)):
            joined = jnp.concatenate([r[...] for r in left], 0)
            value = dot(joined, right[...], TN).astype(b16)
            if parts == 1:
                out[...] = value
            else:
                for part in range(parts):
                    out[part] = value[:, part * cut : (part + 1) * cut]

    if parts == 1:
        spec = pl.BlockSpec((chunk, width), lambda i: (i, 0))
        shape = jax.ShapeDtypeStruct((units, width), b16)
    else:
        spec = pl.BlockSpec((parts, chunk, cut), lambda i: (0, i, 0))
        shape = jax.ShapeDtypeStruct((parts, units, cut), b16)
    return pl.pallas_call(
        body,
        grid=(units // chunk,),
        in_specs=[pl.BlockSpec((rows, width), whole)] * (2 * slots)
        + [pl.BlockSpec((rows, chunk), lambda i: (0, i))] * (3 * slots),
        out_specs=[spec] * 3,
        out_shape=[shape] * 3,
        scratch_shapes=[pltpu.VMEM((slots * rows, width), b16)] * 2,
        compiler_params=params(48),
        cost_estimate=pl.CostEstimate(
            flops=6 * slots * rows * width * units,
            bytes_accessed=6 * units * width + 6 * slots * rows * units,
            transcendentals=0,
        ),
    )(*bs, *dys, *zs, *dgs, *dus)


def input_gradient(dh, own, piece, sent, x, gains):
    rows, width = dh.shape

    def body(dh_ref, own_ref, piece_ref, sent_ref, x_ref, gain_ref, out_ref):
        da = own_ref[...] + (piece_ref[...].astype(f32) + sent_ref[...].astype(f32))
        unit, scale = unit_of(x_ref[...].astype(f32))
        along = da * gain_ref[0:1]
        inner = jnp.mean(along * unit, -1, keepdims=True)
        out_ref[...] = dh_ref[...] + scale * (along - unit * inner)

    block = pl.BlockSpec((CONT, width), lambda i: (i, 0))
    return pl.pallas_call(
        body,
        grid=(rows // CONT,),
        in_specs=[block] * 5 + [pl.BlockSpec(gains.shape, whole)],
        out_specs=block,
        out_shape=jax.ShapeDtypeStruct((rows, width), f32),
        compiler_params=params(32),
    )(dh, own, piece, sent, x, gains)


def on_device(inputs, cotangent, attn_gain, moe_gain, router, w_query, w_key, w_value, w_out, w_gate, w_up, w_down, expert_ids, priority):
    rows, width = inputs.shape
    experts, cut, own_units = w_gate.shape
    units = experts * own_units
    dp = lax.axis_size("dp")
    depth = lax.axis_size("tensor")
    own = lax.axis_index("tensor")
    at = jnp.full((1,), own, jnp.int32)
    up = [(i, i + 1) for i in range(depth - 1)]
    down = [(i + 1, i) for i in range(depth - 1)]

    def swap(value, bits):
        return lax.ppermute(value, "tensor", [(i, i ^ bits) for i in range(depth)])

    mine = jnp.stack([w_query, w_key, w_value, w_out.T])
    near = swap(mine, 1)
    far = swap(mine, 2)
    attention_w = lax.all_gather(jnp.stack([mine, near, far, swap(far, 1)]), "dp", axis=2, tiled=True)

    x1 = lax.ppermute(inputs, "tensor", up)
    x2 = lax.ppermute(x1, "tensor", up)
    x3 = lax.ppermute(x2, "tensor", up)

    small = jnp.concatenate([attn_gain[:, None], moe_gain[:, None], router], 1)
    small = lax.all_gather(lax.all_gather(small, "tensor", axis=0, tiled=True), "dp", axis=0, tiled=True)
    gains = jnp.concatenate([small[:, :2].T.astype(f32), jnp.zeros((6, width), f32)], 0)
    router_full = small[:, 2:]
    router_wide = jnp.concatenate(
        [router_full, router_full, jnp.zeros((width, 128 - 2 * experts), b16)], 1
    )
    keep = keep_mask(expert_ids.T, priority.reshape(-1, 2).T, experts)

    def gather_units(shard):
        return lax.all_gather(shard.reshape(units, cut), "dp", axis=1, tiled=True)

    wg = gather_units(w_gate.transpose(0, 2, 1))
    wu = gather_units(w_up.transpose(0, 2, 1))
    wd = gather_units(w_down)

    a, q, k, v, p, c, h, b = attention_forward(at, (inputs, x1, x2, x3), gains, attention_w)

    dy2 = swap(cotangent, 2)
    dys = (cotangent, swap(cotangent, 1), dy2, swap(dy2, 1))
    b2 = swap(b, 2)
    bs = (b, swap(b, 1), b2, swap(b2, 1))
    outs = [
        experts_block(jnp.full((1,), own ^ s, jnp.int32), bs[s], dys[s], keep, router_wide, wg, wu, wd, experts)
        for s in range(depth)
    ]
    ys, dbs, rgs, zs, dgs, dus = zip(*outs)
    parts = [dbs[0]] + [swap(dbs[s], s) for s in range(1, depth)]
    y_parts = [ys[0]] + [swap(ys[s], s) for s in range(1, depth)]
    blocked = cut % 128 == 0
    grads = experts_weights(bs, dys, zs, dgs, dus, dp if blocked else 1)

    def scatter_units(grad):
        if blocked:
            total = lax.psum_scatter(grad, "dp", scatter_dimension=0, tiled=True)
        else:
            total = lax.psum_scatter(grad, "dp", scatter_dimension=1, tiled=True)
        return total.reshape(experts, own_units, cut).astype(f32)

    wg_grad, wu_grad, wd_grad = (scatter_units(grad) for grad in grads)

    dw, dap, dao, dh, sums = attention_backward(at, h, cotangent, parts, gains, a, q, k, v, p, c, attention_w)
    output = h
    for part in y_parts:
        output = output + part.astype(f32)

    def chunk_of(index):
        start = jnp.clip(index, 0, dap.shape[0] // rows - 1) * rows
        piece = lax.dynamic_slice_in_dim(dap, start, rows, 0)
        valid = (index >= 0) & (index < dap.shape[0] // rows)
        return jnp.where(valid, piece, jnp.zeros((), b16))

    sent = None
    for hop in range(1, depth):
        piece = chunk_of(own - depth + hop)
        sent = lax.ppermute(piece if sent is None else piece + sent, "tensor", down)
    input_grad = input_gradient(dh, dao, chunk_of(own), sent, inputs, gains)

    dw = lax.psum_scatter(dw, "dp", scatter_dimension=2, tiled=True)
    total = dw[0].astype(f32)
    for s in range(1, depth):
        total = total + swap(dw[s], s).astype(f32)

    rg = rgs[0] + rgs[1] + rgs[2] + rgs[3]
    small_grad = jnp.concatenate([sums[:2].T, rg[:, :experts] + rg[:, experts : 2 * experts]], 1)
    small_grad = small_grad.reshape(dp, depth, width // (dp * depth), 2 + experts)
    small_grad = lax.psum_scatter(small_grad, "tensor", scatter_dimension=1, tiled=True)
    small_grad = lax.psum_scatter(small_grad, "dp", scatter_dimension=0, tiled=True)[0, 0]
    return (
        output.astype(b16),
        input_grad,
        small_grad[:, 0],
        small_grad[:, 1],
        small_grad[:, 2:],
        total[0],
        total[1],
        total[2],
        total[3].T,
        wg_grad.transpose(0, 2, 1),
        wu_grad.transpose(0, 2, 1),
        wd_grad,
    )


def solution(mesh):
    tokens = P(("dp", "tensor"), None)
    vector = P(("dp", "tensor"))
    return jax.shard_map(
        on_device,
        mesh=mesh,
        in_specs=(tokens, tokens, vector, vector, tokens)
        + (P("dp", "tensor"),) * 3
        + (P("tensor", "dp"), P(None, "dp", "tensor"), P(None, "dp", "tensor"), P(None, "tensor", "dp"))
        + (P("dp", None), P("dp", None)),
        out_specs=(tokens, tokens, vector, vector, tokens)
        + (P("dp", "tensor"),) * 3
        + (P("tensor", "dp"), P(None, "dp", "tensor"), P(None, "dp", "tensor"), P(None, "tensor", "dp")),
        check_vma=False,
    )
```

time: 1550 us -> 724 us (0.47)
  waiting for transfers between devices: 639 us -> 301 us
  matrix products: 287 us -> 0 us
  local copies, waits for them, and re-layouts: 255 us -> 15 us
  Pallas kernels: 0 us -> 231 us
  blocking collectives: 207 us -> 86.2 us
  other arithmetic: 123 us -> 22 us
  starting transfers between devices: 1.06 us -> 44.1 us
    reduce_scatter x11 -> x5, waiting for transfers between devices: 552 us -> 112 us  [the longest x3 56.9 us: scatter_units(): total = lax.psum_scatter(grad, 'dp', scatter_dimension=0, tiled=True)]
    dot_general x44 -> x0, matrix products: 286 us -> none  [the longest x1 37.3 us: on_device(): jnp.einsum('ecd,efd->ecf', slot_grad, wd_full, preferred_element_type=f32)]
    pallas_call x0 -> x9, Pallas kernels: none -> 231 us  [the longest x4 106 us: experts_block(): pl.pallas_call(body, grid_spec=pltpu.PrefetchScalarGridSpec(num_scalar_pr...]
    gather x10 -> x0, local copies, waits for them, and re-layouts: 171 us -> none  [the longest x2 37.9 us: on_device(): picked = expert_out[slot]]
    ppermute x0 -> x24, waiting for transfers between devices: none -> 146 us  [the longest x18 70.2 us: swap(): return lax.ppermute(value, 'tensor', [(i, i ^ bits) for i in range(depth)])]
    unnamed x2 -> x1, blocking collectives: 86.1 us -> 22.7 us
    reduce_sum x13 -> x0, other arithmetic: 62.7 us -> none  [the longest x1 26.7 us: on_device(): jnp.sum(grad_wide[:, None, :] * picked.reshape(group_rows, 2, -1), -1)]
    all_gather x6 -> x2, blocking collectives: 121 us -> 63.5 us  [the longest x1 54.6 us: on_device(): lax.all_gather(small, 'tensor', axis=0, tiled=True)]
  transfers between devices with their start and end apart: 20 -> 33, of which waited for: 12 -> 11; matrix products, arithmetic and copies ran while one was open for 31% -> 4% of each run, Pallas kernels for 0% -> 25%
where the time goes in v1:
time: 724 us; the launch traced here: 714 us
  waiting for transfers between devices  301 us (42%)
  Pallas kernels  231 us (32%)
  blocking collectives  86.2 us (12%)
  starting transfers between devices  44.1 us (6%)
  other arithmetic  22 us (3%)
  local copies, waits for them, and re-layouts  15 us (2%)
  between operations  14.5 us (2%)
    pallas_call x4, Pallas kernels, experts_block(): pl.pallas_call(body, grid_spec=pltpu.PrefetchScalarGridSpec(num_scalar_pr...  106 us
    ppermute x18, waiting for transfers between devices, swap(): return lax.ppermute(value, 'tensor', [(i, i ^ bits) for i in range(depth)])  70.2 us
    reduce_scatter x3, waiting for transfers between devices, scatter_units(): total = lax.psum_scatter(grad, 'dp', scatter_dimension=0, tiled=True)  56.9 us
    reduce_scatter x1, waiting for transfers between devices, on_device(): dw = lax.psum_scatter(dw, 'dp', scatter_dimension=2, tiled=True)  55.3 us
    all_gather x1, blocking collectives, on_device(): lax.all_gather(small, 'tensor', axis=0, tiled=True)  54.6 us
    pallas_call x1, Pallas kernels, attention_backward(): pl.pallas_call(body, grid_spec=pltpu.PrefetchScalarGridSpec(num_scalar_pr...  49.4 us
    ppermute x3, waiting for transfers between devices, on_device(): sent = lax.ppermute(piece if sent is None else piece + sent, 'tensor', down)  44.3 us
    all_gather x3, waiting for transfers between devices, gather_units(): return lax.all_gather(shard.reshape(units, cut), 'dp', axis=1, tiled=True)  38.6 us
  transfers between devices with their start and end apart: 33, of which 11 were waited for; matrix products, arithmetic and copies ran while one was open for 4% of the time, Pallas kernels for 25%

profile of v1, /device:TPU:0, one launch (start us, length us, event | category | flops | bytes accessed | tf_op | source)
XLA Modules:
  0.0 714.0 jit_solution(2225371497963393125)
XLA Ops:
  9.1 4.1 collective-permute-start.4
  14.8 10.5 %collective-permute-done.4 = bf16[4,128,256]{2,1,0:T(8,128)(2,1)S(1)} collective-permute-done((bf16[4,128,256]{2,1,0:T(8,128)(2,1)S(1)}, bf16[4,128,256]{2,1,0:T(8,128)(2,1)S(1)}, u32[]{:S(2)}, u32[]{:S(2)}) %collective-permute-start.4) | collective-permute-done | bytes 262176 | tf_op jit(solution)/shard_map/ppermute | solution.py:527
  25.9 6.8 collective-permute-done.5
  36.0 3.4 collective-permute-start
  39.3 16.1 %collective-permute-done.x1 = bf16[384,1024]{1,0:T(8,128)(2,1)S(1)} collective-permute-done((bf16[384,1024]{1,0:T(8,128)(2,1)S(1)}, bf16[384,1024]{1,0:T(8,128)(2,1)S(1)}, u32[]{:S(2)}, u32[]{:S(2)}) %collective-permute-start) | collective-permute-done | bytes 786464 | tf_op jit(solution)/shard_map/ppermute | solution.py:534
  55.4 4.5 collective-permute-start.1
  59.9 15.5 %collective-permute-done.1.x2 = bf16[384,1024]{1,0:T(8,128)(2,1)S(1)} collective-permute-done((bf16[384,1024]{1,0:T(8,128)(2,1)S(1)}, bf16[384,1024]{1,0:T(8,128)(2,1)S(1)}, u32[]{:S(2)}, u32[]{:S(2)}) %collective-permute-start.1) | collective-permute-done | bytes 786464 | tf_op jit(solution)/shard_map/ppermute | solution.py:535
  75.3 5.4 collective-permute-start.2
  83.0 54.6 %all-gather = bf16[4,32,6]{1,2,0:T(8,128)(2,1)S(1)} all-gather(bf16[1,32,6]{1,2,0:T(8,128)(2,1)S(1)} %maximum_bitcast_fusion), channel_id=1, replica_groups=mesh['dp'=8,'tensor'=4] {'tensor'}, dimensions={0}, use_global_device_ids=true | all-gather | bytes 1920 | tf_op jit(solution)/shard_map/all_gather | solution.py:539
  137.6 8.9 %all_gather.19 = bf16[1024,6]{0,1:T(8,128)(2,1)S(1)} all-gather(bf16[128,6]{0,1:T(8,128)(2,1)S(1)} %reshape.60), channel_id=1, replica_groups=mesh['dp'=8,'tensor'=4] {'dp'}, dimensions={0}, use_global_device_ids=true | all-gather | bytes 13824 | tf_op jit(solution)/shard_map/all_gather | solution.py:539
  147.2 36.2 %shard_map.229 = (bf16[1408,1024]{1,0:T(8,128)(2,1)}, bf16[384,1024]{1,0:T(8,128)(2,1)}, bf16[1408,1024]{1,0:T(8,128)(2,1)}, bf16[1408,1024]{1,0:T(8,128)(2,1)},...) custom-call(s32[1]{0:T(128)} %bitcast.at_ref.block_ref, ...), custom_call_target="tpu_custom_call" | custom-call | flops 11140071424 | bytes 62914560 | tf_op jit(solution)/shard_map/pallas_call | solution.py:150
  190.3 38.6 %all-gather.8.cloned.1.call-done.wg_ref = bf16[2816,1024]{1,0:T(8,128)(2,1)} async-done(((bf16[2816,128]{1,0:T(8,128)(2,1)}), bf16[2816,1024]{1,0:T(8,128)(2,1)}) %all-gather.8.cloned.1.call-update) | async-done | bytes 5767184 | tf_op jit(solution)/shard_map/all_gather | solution.py:548
  228.9 27.0 %shard_map.233 = (bf16[384,1024]{1,0:T(8,128)(2,1)S(1)}, bf16[384,1024]{1,0:T(8,128)(2,1)}, f32[1024,128]{1,0:T(8,128)S(1)}, bf16[384,2816]{1,0:T(8,128)(2,1)}, ...) custom-call(s32[1]{0:T(128)} %bitcast.22.block_ref, bf16[384,1024]{1,0:T(8,128)(2,1)} %collective-permute-done.9.b_ref.refs_2_, ...), custom_call_target="tpu_custom_call" | custom-call | flops 13287555072 | bytes 23789568 | tf_op jit(solution)/shard_map/pallas_call | solution.py:406
  255.9 2.4 collective-permute-start.16
  259.8 26.6 %shard_map.232 = (bf16[384,1024]{1,0:T(8,128)(2,1)S(1)}, bf16[384,1024]{1,0:T(8,128)(2,1)}, f32[1024,128]{1,0:T(8,128)S(1)}, bf16[384,2816]{1,0:T(8,128)(2,1)}, ...) custom-call(s32[1]{0:T(128)} %bitcast.21.block_ref, bf16[384,1024]{1,0:T(8,128)(2,1)} %collective-permute-done.6.b_ref.refs_1_, ...), custom_call_target="tpu_custom_call" | custom-call | flops 13287555072 | bytes 23789568 | tf_op jit(solution)/shard_map/pallas_call | solution.py:406
  287.0 6.8 collective-permute-done.12.b_ref.refs_3_
  293.8 26.7 %shard_map.234 = (bf16[384,1024]{1,0:T(8,128)(2,1)S(1)}, bf16[384,1024]{1,0:T(8,128)(2,1)}, f32[1024,128]{1,0:T(8,128)S(1)}, bf16[384,2816]{1,0:T(8,128)(2,1)}, ...) custom-call(s32[1]{0:T(128)} %bitcast.23.block_ref, bf16[384,1024]{1,0:T(8,128)(2,1)S(1)} %collective-permute-done.12.b_ref.refs_3_, ...), custom_call_target="tpu_custom_call" | custom-call | flops 13287555072 | bytes 23789568 | tf_op jit(solution)/shard_map/pallas_call | solution.py:406
  322.4 25.5 %shard_map.231 = (bf16[384,1024]{1,0:T(8,128)(2,1)S(1)}, bf16[384,1024]{1,0:T(8,128)(2,1)S(1)}, f32[1024,128]{1,0:T(8,128)S(1)}, bf16[384,2816]{1,0:T(8,128)(2,1...) custom-call(s32[1]{0:T(128)} %bitcast.at_ref.block_ref, bf16[384,1024]{1,0:T(8,128)(2,1)S(1)} %copy-done.12, ...), custom_call_target="tpu_custom_call" | custom-call | flops 13287555072 | bytes 23789568 | tf_op jit(solution)/shard_map/pallas_call | solution.py:406
  349.5 49.4 %shard_map.235 = (bf16[4,4,1024,256]{3,2,1,0:T(8,128)(2,1)}, bf16[1152,1024]{1,0:T(8,128)(2,1)}, f32[384,1024]{1,0:T(8,128)}, f32[384,1024]{1,0:T(8,128)}, f32[8,1024]{1,0:T(8,128)}) custom-call(s32[1]{0:T(128)} %bitcast.at_ref.block_ref, f32[384,1024]{1,0:T(8,128)} %get-tuple-element.52.h_ref, bf16[384,1024]{1,0:T(8,128)(2,1)} %refs_4_.1, ...), custom_call_target="tpu_custom_call" | custom-call | flops 22280142848 | bytes 83886080 | tf_op jit(solution)/shard_map/pallas_call | solution.py:284
  401.9 34.8 %shard_map.237 = (bf16[8,2816,128]{2,1,0:T(8,128)(2,1)}, bf16[8,2816,128]{2,1,0:T(8,128)(2,1)}, bf16[8,2816,128]{2,1,0:T(8,128)(2,1)}) custom-call(bf16[384,1024]{1,0:T(8,128)(2,1)S(1)} %copy-done.13, bf16[384,1024]{1,0:T(8,128)(2,1)} %collective-permute-done.6.b_ref.refs_1_, bf16[384,1024]{1,0:T(8,128)(2,1)} %collective-permute-done.9.b_ref.refs_2_, ...), custom_call_target="tpu_custom_call" | custom-call | flops 26575110144 | bytes 43253760 | tf_op jit(solution)/shard_map/pallas_call | solution.py:477
  441.7 27.7 %collective-permute-done.18 = bf16[384,1024]{1,0:T(8,128)(2,1)} collective-permute-done((bf16[384,1024]{1,0:T(8,128)(2,1)S(1)}, bf16[384,1024]{1,0:T(8,128)(2,1)}, u32[]{:S(2)}, u32[]{:S(2)}) %collective-permute-start.18) | collective-permute-done | bytes 786464 | tf_op jit(solution)/shard_map/ppermute | solution.py:593
  472.4 3.9 collective-permute-start.11
  477.8 16.6 %collective-permute-done.19 = bf16[384,1024]{1,0:T(8,128)(2,1)} collective-permute-done((bf16[384,1024]{1,0:T(8,128)(2,1)S(1)}, bf16[384,1024]{1,0:T(8,128)(2,1)}, u32[]{:S(2)}, u32[]{:S(2)}) %collective-permute-start.19) | collective-permute-done | bytes 786464 | tf_op jit(solution)/shard_map/ppermute | solution.py:593
  494.4 3.0 select_add_fusion.1
  499.3 46.0 %collective-permute-done.11 = bf16[384,1024]{1,0:T(8,128)(2,1)} collective-permute-done((bf16[384,1024]{1,0:T(8,128)(2,1)S(1)}, bf16[384,1024]{1,0:T(8,128)(2,1)}, u32[]{:S(2)}, u32[]{:S(2)}) %collective-permute-start.11) | collective-permute-done | bytes 786464 | tf_op jit(solution)/shard_map/ppermute | solution.py:527
  545.3 4.1 add_convert_fusion
  550.2 22.7 %all-reduce.1 = f32[8,1,32,6]{2,1,3,0:T(1,128)S(1)} all-reduce(f32[8,1,32,6]{2,1,3,0:T(1,128)S(1)} %copy.58), channel_id=3, replica_groups=mesh['dp'=8,'tensor'=4] {'dp'}, use_global_device_ids=true, to_apply=%region_1.0.clone | all-reduce | flops 1536 | bytes 12288
  576.1 3.6 shard_map.236
  579.6 2.4 convert.12
  582.0 2.4 convert_bitcast_fusion
  584.4 55.3 %reduce-scatter.8.cloned.1.call-done = bf16[4,4,128,256]{3,2,1,0:T(8,128)(2,1)} async-done(((bf16[4,4,1024,256]{3,2,1,0:T(8,128)(2,1)}), bf16[4,4,128,256]{3,2,1,0:T(8,128)(2,1)}) %reduce-scatter.8.cloned.1.call-update) | async-done | bytes 1048592 | tf_op jit(solution)/shard_map/reduce_scatter | solution.py:596
  645.4 56.9 %reduce-scatter.10.cloned.1.call-done = bf16[1,2816,128]{2,1,0:T(8,128)(2,1)} async-done(((bf16[8,2816,128]{2,1,0:T(8,128)(2,1)}), bf16[1,2816,128]{2,1,0:T(8,128)(2,1)}) %reduce-scatter.10.cloned.1.call-update) | async-done | bytes 720912 | tf_op jit(solution)/shard_map/reduce_scatter | solution.py:572
  (146 shorter events, 51.3 us)
Async XLA Ops:
  7.2 140.0 %all-gather.6.cloned.1.call-start = ((), (), s32[]{:S(2)}) async-start(), calls=%async_computation.5 | async-start | bytes 9437184 | tf_op jit(solution)/shard_map/all_gather | solution.py:532
  9.1 16.1 %collective-permute-start.4 = (bf16[4,128,256]{2,1,0:T(8,128)(2,1)S(1)}, bf16[4,128,256]{2,1,0:T(8,128)(2,1)S(1)}, u32[]{:S(2)}, u32[]{:S(2)}) collective-permute-start(bf16[4,128,256]{2,1,0:T(8,128)(2,1)S(1)} %get-tuple-element.152), channel_id=1, source_target_pairs={{0,2},{1,3},{2,0},{3,1},{4,6},{5,7},{6,4},{7,5},{8,10},{9,11},{10,... | collective-permute-start | bytes 786440 | tf_op jit(solution)/shard_map/ppermute | solution.py:527
  13.2 12.6 %collective-permute-start.3 = (bf16[4,128,256]{2,1,0:T(8,128)(2,1)S(1)}, bf16[4,128,256]{2,1,0:T(8,128)(2,1)S(1)}, u32[]{:S(2)}, u32[]{:S(2)}) collective-permute-start(bf16[4,128,256]{2,1,0:T(8,128)(2,1)S(1)} %get-tuple-element.152), channel_id=1, source_target_pairs={{0,1},{1,0},{2,3},{3,2},{4,5},{5,4},{6,7},{7,6},{8,9},{9,8},{10,11... | collective-permute-start | bytes 786440 | tf_op jit(solution)/shard_map/ppermute | solution.py:527
  33.8 156.5 %all-gather.10.cloned.1.call-start = ((), (), s32[]{:S(2)}) async-start(), calls=%async_computation.7 | async-start | bytes 6488064 | tf_op jit(solution)/shard_map/all_gather | solution.py:548
  34.6 155.8 %all-gather.12.cloned.1.call-start = ((), (), s32[]{:S(2)}) async-start(), calls=%async_computation.8 | async-start | bytes 6488064 | tf_op jit(solution)/shard_map/all_gather | solution.py:548
  35.3 193.6 %all-gather.8.cloned.1.call-start = ((), (), s32[]{:S(2)}) async-start(), calls=%async_computation.6 | async-start | bytes 6488064 | tf_op jit(solution)/shard_map/all_gather | solution.py:548
  35.9 513.5 %reduce-scatter.6.cloned.1.call-start = ((), (), s32[]{:S(2)}) async-start(), calls=%async_computation.9 | async-start | bytes 122880 | tf_op jit(solution)/shard_map/reduce_scatter | solution.py:604
  36.0 19.4 %collective-permute-start = (bf16[384,1024]{1,0:T(8,128)(2,1)S(1)}, bf16[384,1024]{1,0:T(8,128)(2,1)S(1)}, u32[]{:S(2)}, u32[]{:S(2)}) collective-permute-start(bf16[384,1024]{1,0:T(8,128)(2,1)S(1)} %copy-done.2), channel_id=1, source_target_pairs={{0,1},{1,2},{2,3},{4,5},{5,6},{6,7},{8,9},{9,10},{10,11},{12,13},{... | collective-permute-start | bytes 2359304 | tf_op jit(solution)/shard_map/ppermute | solution.py:534
  55.4 19.9 %collective-permute-start.1 = (bf16[384,1024]{1,0:T(8,128)(2,1)S(1)}, bf16[384,1024]{1,0:T(8,128)(2,1)S(1)}, u32[]{:S(2)}, u32[]{:S(2)}) collective-permute-start(bf16[384,1024]{1,0:T(8,128)(2,1)S(1)} %collective-permute-done.x1), channel_id=1, source_target_pairs={{0,1},{1,2},{2,3},{4,5},{5,6},{6,7},{8,9},{9,10},{10,11},{12,13},{... | collective-permute-start | bytes 2359304 | tf_op jit(solution)/shard_map/ppermute | solution.py:535
  75.3 71.8 %collective-permute-start.2 = (bf16[384,1024]{1,0:T(8,128)(2,1)S(1)}, bf16[384,1024]{1,0:T(8,128)(2,1)}, u32[]{:S(2)}, u32[]{:S(2)}) collective-permute-start(bf16[384,1024]{1,0:T(8,128)(2,1)S(1)} %collective-permute-done.1.x2), channel_id=1, source_target_pairs={{0,1},{1,2},{2,3},{4,5},{5,6},{6,7},{8,9},{9,10},{10,11},{12,13},{... | collective-permute-start | bytes 2359304 | tf_op jit(solution)/shard_map/ppermute | solution.py:536
  80.7 107.5 %collective-permute-start.10 = (bf16[384,1024]{1,0:T(8,128)(2,1)S(1)}, bf16[384,1024]{1,0:T(8,128)(2,1)}, u32[]{:S(2)}, u32[]{:S(2)}) collective-permute-start(bf16[384,1024]{1,0:T(8,128)(2,1)S(1)} %copy-done.7), channel_id=1, source_target_pairs={{0,2},{1,3},{2,0},{3,1},{4,6},{5,7},{6,4},{7,5},{8,10},{9,11},{10,... | collective-permute-start | bytes 2359304 | tf_op jit(solution)/shard_map/ppermute | solution.py:527
  183.4 45.5 %collective-permute-start.9 = (bf16[384,1024]{1,0:T(8,128)(2,1)}, bf16[384,1024]{1,0:T(8,128)(2,1)}, u32[]{:S(2)}, u32[]{:S(2)}) collective-permute-start(bf16[384,1024]{1,0:T(8,128)(2,1)} %get-tuple-element.53.b_ref.refs_0_), channel_id=1, source_target_pairs={{0,2},{1,3},{2,0},{3,1},{4,6},{5,7},{6,4},{7,5},{8,10},{9,11},{10,... | collective-permute-start | bytes 2359304 | tf_op jit(solution)/shard_map/ppermute | solution.py:527
  183.5 76.3 %collective-permute-start.7 = (bf16[384,1024]{1,0:T(8,128)(2,1)S(1)}, bf16[384,1024]{1,0:T(8,128)(2,1)}, u32[]{:S(2)}, u32[]{:S(2)}) collective-permute-start(bf16[384,1024]{1,0:T(8,128)(2,1)S(1)} %copy-done.7), channel_id=1, source_target_pairs={{0,1},{1,0},{2,3},{3,2},{4,5},{5,4},{6,7},{7,6},{8,9},{9,8},{10,11... | collective-permute-start | bytes 2359304 | tf_op jit(solution)/shard_map/ppermute | solution.py:527
  188.2 98.7 %collective-permute-start.13 = (bf16[384,1024]{1,0:T(8,128)(2,1)}, bf16[384,1024]{1,0:T(8,128)(2,1)}, u32[]{:S(2)}, u32[]{:S(2)}) collective-permute-start(bf16[384,1024]{1,0:T(8,128)(2,1)} %collective-permute-done.10.dy_ref.refs_6_), channel_id=1, source_target_pairs={{0,1},{1,0},{2,3},{3,2},{4,5},{5,4},{6,7},{7,6},{8,9},{9,8},{10,11... | collective-permute-start | bytes 2359304 | tf_op jit(solution)/shard_map/ppermute | solution.py:527
  189.9 70.0 %collective-permute-start.6 = (bf16[384,1024]{1,0:T(8,128)(2,1)S(1)}, bf16[384,1024]{1,0:T(8,128)(2,1)}, u32[]{:S(2)}, u32[]{:S(2)}) collective-permute-start(bf16[384,1024]{1,0:T(8,128)(2,1)S(1)} %copy-done.11), channel_id=1, source_target_pairs={{0,1},{1,0},{2,3},{3,2},{4,5},{5,4},{6,7},{7,6},{8,9},{9,8},{10,11... | collective-permute-start | bytes 2359304 | tf_op jit(solution)/shard_map/ppermute | solution.py:527
  255.9 93.6 %collective-permute-start.16 = (bf16[384,1024]{1,0:T(8,128)(2,1)}, bf16[384,1024]{1,0:T(8,128)(2,1)}, u32[]{:S(2)}, u32[]{:S(2)}) collective-permute-start(bf16[384,1024]{1,0:T(8,128)(2,1)} %get-tuple-element.60), channel_id=1, source_target_pairs={{0,2},{1,3},{2,0},{3,1},{4,6},{5,7},{6,4},{7,5},{8,10},{9,11},{10,... | collective-permute-start | bytes 2359304 | tf_op jit(solution)/shard_map/ppermute | solution.py:527
  258.3 35.5 %collective-permute-start.12 = (bf16[384,1024]{1,0:T(8,128)(2,1)}, bf16[384,1024]{1,0:T(8,128)(2,1)S(1)}, u32[]{:S(2)}, u32[]{:S(2)}) collective-permute-start(bf16[384,1024]{1,0:T(8,128)(2,1)} %collective-permute-done.9.b_ref.refs_2_), channel_id=1, source_target_pairs={{0,1},{1,0},{2,3},{3,2},{4,5},{5,4},{6,7},{7,6},{8,9},{9,8},{10,11... | collective-permute-start | bytes 2359304 | tf_op jit(solution)/shard_map/ppermute | solution.py:527
  286.5 63.0 %collective-permute-start.15 = (bf16[384,1024]{1,0:T(8,128)(2,1)}, bf16[384,1024]{1,0:T(8,128)(2,1)}, u32[]{:S(2)}, u32[]{:S(2)}) collective-permute-start(bf16[384,1024]{1,0:T(8,128)(2,1)} %get-tuple-element.59), channel_id=1, source_target_pairs={{0,1},{1,0},{2,3},{3,2},{4,5},{5,4},{6,7},{7,6},{8,9},{9,8},{10,11... | collective-permute-start | bytes 2359304 | tf_op jit(solution)/shard_map/ppermute | solution.py:527
  321.4 28.1 %collective-permute-start.17 = (bf16[384,1024]{1,0:T(8,128)(2,1)}, bf16[384,1024]{1,0:T(8,128)(2,1)}, u32[]{:S(2)}, u32[]{:S(2)}) collective-permute-start(bf16[384,1024]{1,0:T(8,128)(2,1)} %get-tuple-element.61), channel_id=1, source_target_pairs={{0,3},{1,2},{2,1},{3,0},{4,7},{5,6},{6,5},{7,4},{8,11},{9,10},{10,... | collective-permute-start | bytes 2359304 | tf_op jit(solution)/shard_map/ppermute | solution.py:527
  400.5 179.1 %reduce-scatter.14.cloned.1.call-start = ((), (), s32[]{:S(2)}) async-start(), calls=%async_computation.13 | async-start | bytes 6488064 | tf_op jit(solution)/shard_map/reduce_scatter | solution.py:572
  436.7 145.3 %reduce-scatter.12.cloned.1.call-start = ((), (), s32[]{:S(2)}) async-start(), calls=%async_computation.12 | async-start | bytes 6488064 | tf_op jit(solution)/shard_map/reduce_scatter | solution.py:572
  437.5 202.3 %reduce-scatter.8.cloned.1.call-start = ((), (), s32[]{:S(2)}) async-start(), calls=%async_computation.10 | async-start | bytes 9437184 | tf_op jit(solution)/shard_map/reduce_scatter | solution.py:596
  438.2 264.1 %reduce-scatter.10.cloned.1.call-start = ((), (), s32[]{:S(2)}) async-start(), calls=%async_computation.11 | async-start | bytes 6488064 | tf_op jit(solution)/shard_map/reduce_scatter | solution.py:572
  440.3 29.0 %collective-permute-start.18 = (bf16[384,1024]{1,0:T(8,128)(2,1)S(1)}, bf16[384,1024]{1,0:T(8,128)(2,1)}, u32[]{:S(2)}, u32[]{:S(2)}) collective-permute-start(bf16[384,1024]{1,0:T(8,128)(2,1)S(1)} %dynamic-slice_select_fusion), channel_id=1, source_target_pairs={{1,0},{2,1},{3,2},{5,4},{6,5},{7,6},{9,8},{10,9},{11,10},{13,12},{... | collective-permute-start | bytes 2359304 | tf_op jit(solution)/shard_map/ppermute | solution.py:593
  471.1 23.3 %collective-permute-start.19 = (bf16[384,1024]{1,0:T(8,128)(2,1)S(1)}, bf16[384,1024]{1,0:T(8,128)(2,1)}, u32[]{:S(2)}, u32[]{:S(2)}) collective-permute-start(bf16[384,1024]{1,0:T(8,128)(2,1)S(1)} %select_add_fusion), channel_id=1, source_target_pairs={{1,0},{2,1},{3,2},{5,4},{6,5},{7,6},{9,8},{10,9},{11,10},{13,12},{... | collective-permute-start | bytes 2359304 | tf_op jit(solution)/shard_map/ppermute | solution.py:593
  472.4 72.9 %collective-permute-start.11 = (bf16[384,1024]{1,0:T(8,128)(2,1)S(1)}, bf16[384,1024]{1,0:T(8,128)(2,1)}, u32[]{:S(2)}, u32[]{:S(2)}) collective-permute-start(bf16[384,1024]{1,0:T(8,128)(2,1)S(1)} %get-tuple-element.56), channel_id=1, source_target_pairs={{0,2},{1,3},{2,0},{3,1},{4,6},{5,7},{6,4},{7,5},{8,10},{9,11},{10,... | collective-permute-start | bytes 2359304 | tf_op jit(solution)/shard_map/ppermute | solution.py:527
  476.2 69.1 %collective-permute-start.8 = (bf16[384,1024]{1,0:T(8,128)(2,1)S(1)}, bf16[384,1024]{1,0:T(8,128)(2,1)}, u32[]{:S(2)}, u32[]{:S(2)}) collective-permute-start(bf16[384,1024]{1,0:T(8,128)(2,1)S(1)} %get-tuple-element.55), channel_id=1, source_target_pairs={{0,1},{1,0},{2,3},{3,2},{4,5},{5,4},{6,7},{7,6},{8,9},{9,8},{10,11... | collective-permute-start | bytes 2359304 | tf_op jit(solution)/shard_map/ppermute | solution.py:527
  477.6 67.7 %collective-permute-start.14 = (bf16[384,1024]{1,0:T(8,128)(2,1)S(1)}, bf16[384,1024]{1,0:T(8,128)(2,1)}, u32[]{:S(2)}, u32[]{:S(2)}) collective-permute-start(bf16[384,1024]{1,0:T(8,128)(2,1)S(1)} %copy-done.10), channel_id=1, source_target_pairs={{0,3},{1,2},{2,1},{3,0},{4,7},{5,6},{6,5},{7,4},{8,11},{9,10},{10,... | collective-permute-start | bytes 2359304 | tf_op jit(solution)/shard_map/ppermute | solution.py:527
  497.4 77.2 %collective-permute-start.20 = (bf16[384,1024]{1,0:T(8,128)(2,1)}, bf16[384,1024]{1,0:T(8,128)(2,1)}, u32[]{:S(2)}, u32[]{:S(2)}) collective-permute-start(bf16[384,1024]{1,0:T(8,128)(2,1)} %get-tuple-element.140), channel_id=1, source_target_pairs={{1,0},{2,1},{3,2},{5,4},{6,5},{7,6},{9,8},{10,9},{11,10},{13,12},{... | collective-permute-start | bytes 2359304 | tf_op jit(solution)/shard_map/ppermute | solution.py:593
  640.9 63.7 %collective-permute-start.21 = (bf16[4,128,256]{2,1,0:T(8,128)(2,1)S(1)}, bf16[4,128,256]{2,1,0:T(8,128)(2,1)S(1)}, u32[]{:S(2)}, u32[]{:S(2)}) collective-permute-start(bf16[4,128,256]{2,1,0:T(8,128)(2,1)S(1)} %get-tuple-element.142), channel_id=1, source_target_pairs={{0,1},{1,0},{2,3},{3,2},{4,5},{5,4},{6,7},{7,6},{8,9},{9,8},{10,11... | collective-permute-start | bytes 786440 | tf_op jit(solution)/shard_map/ppermute | solution.py:527
  642.5 62.1 %collective-permute-start.22 = (bf16[4,128,256]{2,1,0:T(8,128)(2,1)S(1)}, bf16[4,128,256]{2,1,0:T(8,128)(2,1)S(1)}, u32[]{:S(2)}, u32[]{:S(2)}) collective-permute-start(bf16[4,128,256]{2,1,0:T(8,128)(2,1)S(1)} %get-tuple-element.144), channel_id=1, source_target_pairs={{0,2},{1,3},{2,0},{3,1},{4,6},{5,7},{6,4},{7,5},{8,10},{9,11},{10,... | collective-permute-start | bytes 786440 | tf_op jit(solution)/shard_map/ppermute | solution.py:527
  644.9 59.7 %collective-permute-start.23 = (bf16[4,128,256]{2,1,0:T(8,128)(2,1)S(1)}, bf16[4,128,256]{2,1,0:T(8,128)(2,1)S(1)}, u32[]{:S(2)}, u32[]{:S(2)}) collective-permute-start(bf16[4,128,256]{2,1,0:T(8,128)(2,1)S(1)} %get-tuple-element.143), channel_id=1, source_target_pairs={{0,3},{1,2},{2,1},{3,0},{4,7},{5,6},{6,5},{7,4},{8,11},{9,10},{10,... | collective-permute-start | bytes 786440 | tf_op jit(solution)/shard_map/ppermute | solution.py:527
  (25 other events, 773.8 us)
Sparse Core Ops, SparseCore 0:
  34.0 56.2 all-gather.5
  92.1 44.3 all-gather.9
  138.4 44.3 all-gather.11
  184.5 44.3 all-gather.7
  400.6 25.0 reduce-scatter.5
  436.8 65.0 reduce-scatter.13
  505.3 59.2 reduce-scatter.11
  568.5 71.2 reduce-scatter.7
  643.2 59.0 reduce-scatter.9

commit v2 on v1

v2 whole, which is shorter than its diff:
```python
import jax
import jax.numpy as jnp
from jax import lax
from jax.experimental import pallas as pl
from jax.experimental.pallas import tpu as pltpu
from jax.sharding import PartitionSpec as P

HEAD_DIM = 64
PROMPT = 1024
CONT = 128
CAPACITY = 960
EPS = 1e-06
PAIR = 2 * HEAD_DIM
MIB = 2**20

f32 = jnp.float32
b16 = jnp.bfloat16
NN = (((1,), (0,)), ((), ()))
NT = (((1,), (1,)), ((), ()))
TN = (((0,), (0,)), ((), ()))
INV_SQRT2 = 0.7071067811865476
INV_SQRT_2PI = 0.3989422804014327
MASKED = -1e30
UNIT_CHUNK = 256
ESTIMATE = 4
FIRST_CHUNKS = 6


def dot(left, right, dims):
    return lax.dot_general(left, right, dims, preferred_element_type=f32)


def params(mib):
    return pltpu.CompilerParams(vmem_limit_bytes=mib * MIB)


def whole(*_):
    return (0, 0)


def unit_of(values):
    scale = lax.rsqrt(jnp.mean(values * values, -1, keepdims=True) + EPS)
    return values * scale, scale


def normal(v):
    bell = jnp.exp(-0.5 * v * v)
    t = 1.0 / (1.0 + (0.3275911 * INV_SQRT2) * jnp.abs(v))
    poly = t * (0.127414796 + t * (-0.142248368 + t * (0.710706871 + t * (-0.726576014 + t * 0.530702715))))
    tail = poly * bell
    return jnp.where(v < 0.0, tail, 1.0 - tail), INV_SQRT_2PI * bell


def keep_mask(ids, order, experts):
    rows = ids.shape[1]
    pairs = ids.shape[0] * rows
    bits = pairs.bit_length()

    def body(ids_ref, order_ref, keep_ref):
        ids_v = ids_ref[...]
        order_v = order_ref[...]
        sub = lax.broadcasted_iota(jnp.int32, (128, rows), 0)
        out = jnp.zeros((128, rows), f32)
        for expert in range(experts):
            mine = ids_v == expert
            bound = jnp.zeros((1, 1), jnp.int32)
            for bit in range(bits - 1, -1, -1):
                trial = bound + (1 << bit)
                inside = jnp.where(mine & (order_v < trial), 1.0, 0.0)
                count = jnp.sum(jnp.sum(inside, 1, keepdims=True), 0, keepdims=True)
                bound = jnp.where(count <= CAPACITY, trial, bound)
            kept = jnp.sum(jnp.where(mine & (order_v < bound), 1.0, 0.0), 0, keepdims=True)
            out = jnp.where((sub < 2 * experts) & (sub % experts == expert), kept, out)
        keep_ref[...] = jnp.transpose(out)

    return pl.pallas_call(
        body,
        out_shape=jax.ShapeDtypeStruct((rows, 128), f32),
        compiler_params=params(32),
    )(ids, order)


def attention_forward(at, slots, gains, weights):
    rows, width = slots[0].shape
    groups, _, _, cols = weights.shape
    tall = PROMPT + rows
    subs = rows // CONT
    pairs = cols // PAIR
    keys = PROMPT + CONT

    def body(at_ref, x0, x1, x2, x3, gain_ref, w_ref, a_ref, q_ref, k_ref, v_ref, p_ref, inv_ref, c_ref, h_ref, b_ref, xs, acc):
        step = pl.program_id(0)
        t = at_ref[0]

        @pl.when(step == 0)
        def _():
            for s, x in enumerate((x0, x1, x2, x3)):
                xs[s * rows : (s + 1) * rows] = x[...]
            gain = gain_ref[0:1]
            for start in range(0, PROMPT, rows):
                take = min(rows, PROMPT - start)
                slot = jnp.maximum(t - start // rows, 0)
                x = xs[pl.ds(pl.multiple_of(slot * rows, 128), take)].astype(f32)
                a_ref[start : start + take] = (unit_of(x)[0] * gain).astype(b16)
            x = x0[...].astype(f32)
            a_ref[PROMPT:tall] = (unit_of(x)[0] * gain).astype(b16)
            acc[...] = x

        q = dot(a_ref[PROMPT:tall], w_ref[0, 0], NN).astype(b16) * jnp.asarray(0.125, b16)
        kv = dot(a_ref[...], jnp.concatenate([w_ref[0, 1], w_ref[0, 2]], 1), NN).astype(b16)
        k, v = kv[:, :cols], kv[:, cols:]
        q_ref[...] = q
        k_ref[...] = k
        v_ref[...] = v
        low = lax.broadcasted_iota(jnp.int32, (CONT, PAIR), 1) < HEAD_DIM
        row = lax.broadcasted_iota(jnp.int32, (2 * CONT, PROMPT), 0) % CONT
        past = lax.broadcasted_iota(jnp.int32, (2 * CONT, PROMPT), 1) - row
        own_ok = lax.broadcasted_iota(jnp.int32, (2 * CONT, CONT), 1) <= (
            lax.broadcasted_iota(jnp.int32, (2 * CONT, CONT), 0) % CONT
        )
        lane = lax.broadcasted_iota(jnp.int32, (2 * CONT, 128), 1)
        inverses = jnp.zeros((2 * CONT, 128), f32)
        zero = jnp.zeros((), b16)
        for pair in range(pairs):
            lanes = slice(pair * PAIR, (pair + 1) * PAIR)
            kp, vp = k[:PROMPT, lanes], v[:PROMPT, lanes]
            for sub in range(subs):
                unit = pair * subs + sub
                own = slice(PROMPT + sub * CONT, PROMPT + (sub + 1) * CONT)
                q2 = q[sub * CONT : (sub + 1) * CONT, lanes]
                qs = jnp.concatenate([jnp.where(low, q2, zero), jnp.where(low, zero, q2)], 0)
                first = t * rows + sub * CONT
                s1 = jnp.where(past <= first, dot(qs, kp, NT), MASKED)
                s2 = jnp.where(own_ok & (first >= PROMPT), dot(qs, k[own, lanes], NT), MASKED)
                top = jnp.maximum(jnp.max(s1, -1, keepdims=True), jnp.max(s2, -1, keepdims=True))
                e1 = jnp.exp(s1 - top)
                e2 = jnp.exp(s2 - top)
                inv = 1.0 / (jnp.sum(e1, -1, keepdims=True) + jnp.sum(e2, -1, keepdims=True))
                inverses = jnp.where(lane == unit, inv, inverses)
                p1 = e1.astype(b16)
                p2 = e2.astype(b16)
                at_p = slice(unit * 2 * CONT, (unit + 1) * 2 * CONT)
                p_ref[0, at_p, :PROMPT] = p1
                p_ref[0, at_p, PROMPT:] = p2
                c2 = (dot(p1, vp, NN) + dot(p2, v[own, lanes], NN)) * inv
                c_ref[sub * CONT : (sub + 1) * CONT, lanes] = jnp.where(low, c2[:CONT], c2[CONT:]).astype(b16)
        inv_ref[0] = inverses
        acc[...] += dot(c_ref[...], w_ref[0, 3], NT)

        @pl.when(step == groups - 1)
        def _():
            h = acc[...]
            h_ref[...] = h
            b_ref[...] = (unit_of(h)[0] * gain_ref[1:2]).astype(b16)

    def by_group(i, at):
        return (0, i)

    return pl.pallas_call(
        body,
        grid_spec=pltpu.PrefetchScalarGridSpec(
            num_scalar_prefetch=1,
            grid=(groups,),
            in_specs=[pl.BlockSpec((rows, width), whole)] * 4
            + [
                pl.BlockSpec(gains.shape, whole),
                pl.BlockSpec((1, 4, width, cols), lambda i, at: (i, 0, 0, 0)),
            ],
            out_specs=[
                pl.BlockSpec((tall, width), whole),
                pl.BlockSpec((rows, cols), by_group),
                pl.BlockSpec((tall, cols), by_group),
                pl.BlockSpec((tall, cols), by_group),
                pl.BlockSpec((1, 2 * pairs * rows, keys), lambda i, at: (i, 0, 0)),
                pl.BlockSpec((1, 2 * CONT, 128), lambda i, at: (i, 0, 0)),
                pl.BlockSpec((rows, cols), by_group),
                pl.BlockSpec((rows, width), whole),
                pl.BlockSpec((rows, width), whole),
            ],
            scratch_shapes=[pltpu.VMEM((4 * rows, width), b16), pltpu.VMEM((rows, width), f32)],
        ),
        out_shape=[
            jax.ShapeDtypeStruct((tall, width), b16),
            jax.ShapeDtypeStruct((rows, width), b16),
            jax.ShapeDtypeStruct((tall, width), b16),
            jax.ShapeDtypeStruct((tall, width), b16),
            jax.ShapeDtypeStruct((groups, 2 * pairs * rows, keys), b16),
            jax.ShapeDtypeStruct((groups, 2 * CONT, 128), f32),
            jax.ShapeDtypeStruct((rows, width), b16),
            jax.ShapeDtypeStruct((rows, width), f32),
            jax.ShapeDtypeStruct((rows, width), b16),
        ],
        compiler_params=params(56),
        cost_estimate=pl.CostEstimate(
            flops=(2 * width * width * (2 * tall + 2 * rows) + 8 * rows * keys * width) // ESTIMATE,
            bytes_accessed=60 * MIB // ESTIMATE,
            transcendentals=rows * keys * 16,
        ),
    )(at, *slots, gains, weights)


def attention_backward(base, count, given, gains, a, q, k, v, p, inv, c, weights, parts):
    opens = base == 0
    rows, width = q.shape
    _, _, _, cols = weights.shape
    tall = PROMPT + rows
    padded = -(-PROMPT // rows) * rows
    subs = rows // CONT
    pairs = cols // PAIR
    keys = PROMPT + CONT
    cut = width // parts

    def body(*refs):
        n_given = 5 if opens else 2
        given_refs = refs[:n_given]
        gain_ref, a_ref, q_ref, k_ref, v_ref, p_ref, inv_ref, c_ref, w_ref = refs[n_given : n_given + 9]
        dw_ref, *outs = refs[n_given + 9 : n_given + 13]
        do, ds, dqs, *more = refs[n_given + 13 :]
        step = pl.program_id(0)
        acc = outs[0] if opens else more[0]
        sum_ref = outs[2]

        @pl.when(step == 0)
        def _():
            sum_ref[...] = jnp.zeros_like(sum_ref)
            if opens:
                h_ref, dy_ref, *part_refs = given_refs
                d0, d1, d2 = (r[...].astype(f32) for r in part_refs)
                dn = d0 + d1 + d2
                gain = gain_ref[1:2]
                unit, scale = unit_of(h_ref[...])
                along = dn * gain
                inner = jnp.mean(along * unit, -1, keepdims=True)
                dh = dy_ref[...].astype(f32) + scale * (along - unit * inner)
                outs[1][...] = dh
                do[...] = dh.astype(b16)
                sum_ref[1:2] = jnp.sum(dn * unit, 0, keepdims=True)
                acc[...] = jnp.zeros_like(acc)
            else:
                do[...] = given_refs[0][...].astype(b16)
                acc[...] = given_refs[1][...]

        low = lax.broadcasted_iota(jnp.int32, (CONT, PAIR), 1) < HEAD_DIM
        zero = jnp.zeros((), b16)

        def stacked(two):
            return jnp.concatenate([jnp.where(low, two, zero), jnp.where(low, zero, two)], 0)

        def weight_out(kind, left, right):
            value = dot(left, right, TN).astype(b16)
            for n in range(value.shape[0] // cols):
                piece = value[n * cols : (n + 1) * cols]
                if cut % 128 == 0:
                    for s in range(parts):
                        dw_ref[s, 0, kind + n] = piece[:, s * cut : (s + 1) * cut]
                else:
                    dw_ref[0, 0, kind + n] = piece

        dc = dot(do[...], w_ref[0, 3], NN).astype(b16)
        weight_out(3, c_ref[...], do[...])
        dks, dvs = [], []
        for pair in range(pairs):
            lanes = slice(pair * PAIR, (pair + 1) * PAIR)
            kp, vp = k_ref[:PROMPT, lanes], v_ref[:PROMPT, lanes]
            qall, dcall, dko, dvo = [], [], [], []
            for sub in range(subs):
                n = pair * subs + sub
                own = slice(PROMPT + sub * CONT, PROMPT + (sub + 1) * CONT)
                mine = slice(sub * CONT, (sub + 1) * CONT)
                at_p = slice(n * 2 * CONT, (n + 1) * 2 * CONT)
                dcs = (stacked(dc[mine, lanes]).astype(f32) * inv_ref[0][:, n : n + 1]).astype(b16)
                qs = stacked(q_ref[mine, lanes])
                cs = stacked(c_ref[mine, lanes])
                delta = jnp.sum(dcs.astype(f32) * cs.astype(f32), -1, keepdims=True)
                p1 = p_ref[0, at_p, :PROMPT]
                p2 = p_ref[0, at_p, PROMPT:]
                ds1 = (p1.astype(f32) * (dot(dcs, vp, NT) - delta)).astype(b16)
                ds2 = (p2.astype(f32) * (dot(dcs, v_ref[own, lanes], NT) - delta)).astype(b16)
                ds[sub * 2 * CONT : (sub + 1) * 2 * CONT] = ds1
                dq2 = (dot(ds1, kp, NN) + dot(ds2, k_ref[own, lanes], NN)) * 0.125
                dqs[mine, lanes] = jnp.where(low, dq2[:CONT], dq2[CONT:]).astype(b16)
                dko.append(dot(ds2, qs, TN).astype(b16))
                dvo.append(dot(p2, dcs, TN).astype(b16))
                qall.append(qs)
                dcall.append(dcs)
            span = slice(pair * 2 * rows, (pair + 1) * 2 * rows)
            dkp = dot(ds[...], jnp.concatenate(qall, 0), TN).astype(b16)
            dvp = dot(p_ref[0, span, :PROMPT], jnp.concatenate(dcall, 0), TN).astype(b16)
            dks.append(jnp.concatenate([dkp] + dko, 0))
            dvs.append(jnp.concatenate([dvp] + dvo, 0))
        dkv = jnp.concatenate(dks + dvs, 1)
        dq = dqs[...]
        weight_out(0, dq, a_ref[PROMPT:tall])
        weight_out(1, dkv, a_ref[...])
        acc[...] += dot(dkv, jnp.concatenate([w_ref[0, 1], w_ref[0, 2]], 1), NT)
        acc[PROMPT:] += dot(dq, w_ref[0, 0], NT)

        if not opens:
            @pl.when(step == count - 1)
            def _():
                dap_ref, dao_ref = outs[:2]
                dap_ref[:PROMPT] = acc[:PROMPT].astype(b16)
                if padded > PROMPT:
                    dap_ref[PROMPT:] = jnp.zeros((padded - PROMPT, width), b16)
                dao_ref[...] = acc[PROMPT:]
                total = jnp.sum(acc[...] * a_ref[...].astype(f32), 0, keepdims=True)
                sum_ref[0:1] = total / gain_ref[0:1]

    def by_group(i):
        return (0, base + i)

    row_spec = pl.BlockSpec((rows, width), whole)
    tall_spec = pl.BlockSpec((tall, width), whole)
    places, lanes_out = (parts, cut) if cut % 128 == 0 else (1, width)
    if opens:
        first_out, first_shape = tall_spec, jax.ShapeDtypeStruct((tall, width), f32)
    else:
        first_out, first_shape = pl.BlockSpec((padded, width), whole), jax.ShapeDtypeStruct((padded, width), b16)
    return pl.pallas_call(
        body,
        grid=(count,),
        in_specs=([row_spec] * 5 if opens else [row_spec, tall_spec])
        + [
            pl.BlockSpec(gains.shape, whole),
            tall_spec,
            pl.BlockSpec((rows, cols), by_group),
            pl.BlockSpec((tall, cols), by_group),
            pl.BlockSpec((tall, cols), by_group),
            pl.BlockSpec((1, 2 * pairs * rows, keys), lambda i: (base + i, 0, 0)),
            pl.BlockSpec((1, 2 * CONT, 128), lambda i: (base + i, 0, 0)),
            pl.BlockSpec((rows, cols), by_group),
            pl.BlockSpec((1, 4, width, cols), lambda i: (base + i, 0, 0, 0)),
        ],
        out_specs=[
            pl.BlockSpec((places, 1, 4, cols, lanes_out), lambda i: (0, i, 0, 0, 0)),
            first_out,
            row_spec,
            pl.BlockSpec((8, width), whole),
        ],
        scratch_shapes=[
            pltpu.VMEM((rows, width), b16),
            pltpu.VMEM((2 * rows, PROMPT), b16),
            pltpu.VMEM((rows, cols), b16),
        ]
        + ([] if opens else [pltpu.VMEM((tall, width), f32)]),
        out_shape=[
            jax.ShapeDtypeStruct((places, count, 4, cols, lanes_out), b16),
            first_shape,
            jax.ShapeDtypeStruct((rows, width), f32),
            jax.ShapeDtypeStruct((8, width), f32),
        ],
        compiler_params=params(60),
        cost_estimate=pl.CostEstimate(
            flops=count * (width * width * (2 * tall + 2 * rows) + 4 * rows * keys * width) // ESTIMATE,
            bytes_accessed=count * 20 * MIB // ESTIMATE,
            transcendentals=0,
        ),
    )(*given, gains, a, q, k, v, p, inv, c, weights)


def experts_blocks(blocks, given, keep, router, weights, start, own, experts, ends):
    rows, width = given[0].shape
    if not ends:
        rows = 2 * rows
    one = rows // 2
    units = weights.shape[1]
    n_given = len(given)

    def body(blocks_ref, *refs):
        given_refs = refs[:n_given]
        keep_a, keep_b, r_ref, wg_ref, wu_ref, wd_ref = refs[n_given : n_given + 6]
        refs = refs[n_given + 6 :]
        if ends:
            b_ref, dy_ref, y_in, db_in, dgates_in = given_refs
            y0, y1, db0, db1, rg_ref, z_ref, dg_ref, du_ref = refs
        else:
            b_ref, dy_ref, y_acc, db_acc, dgates_ref, z_ref, dg_ref, du_ref = refs
        lane = lax.broadcasted_iota(jnp.int32, (one, 128), 1)
        col = lax.broadcasted_iota(jnp.int32, (one, units), 1)
        met = range(start // own, (start + units - 1) // own + 1)
        for n in range(2):
            span = slice(n * one, (n + 1) * one)
            keep = (keep_a, keep_b)[n][...]
            if ends:
                b_v, dy_v = b_ref[span], dy_ref[span]
            else:
                b_v, dy_v = given_refs[n][...], given_refs[2 + n][...]
                b_ref[span] = b_v
                dy_ref[span] = dy_v
            logits = dot(b_v, r_ref[...], NN)
            live = lane < experts
            top = jnp.max(jnp.where(live, logits, MASKED), -1, keepdims=True)
            grown = jnp.exp(jnp.where(lane < 2 * experts, logits, MASKED) - top)
            share = grown / jnp.sum(jnp.where(live, grown, 0.0), -1, keepdims=True)
            gates = share.astype(b16).astype(f32) * keep

            g = dot(b_v, wg_ref[0], NT)
            u = dot(b_v, wu_ref[0], NT)
            dz_plain = dot(dy_v, wd_ref[0], NT)
            gate = gates[:, met[-1] : met[-1] + 1]
            for expert in met[-2::-1]:
                gate = jnp.where(col < (expert + 1) * own - start, gates[:, expert : expert + 1], gate)
            cdf, pdf = normal(g)
            act = g * cdf
            z = (act * u).astype(b16).astype(f32)
            along = dz_plain * z
            dgates = dgates_in[span] if ends else jnp.zeros((one, 128), f32)
            for expert in met:
                low, high = max(expert * own - start, 0), min((expert + 1) * own - start, units)
                inner_low, inner_high = -(-low // 128) * 128, high // 128 * 128
                part = jnp.sum(along[:, inner_low:inner_high], -1, keepdims=True)
                if low < inner_low:
                    edge = along[:, inner_low - 128 : inner_low]
                    part += jnp.sum(jnp.where(lane >= low % 128, edge, 0.0), -1, keepdims=True)
                if inner_high < high:
                    edge = along[:, inner_high : inner_high + 128]
                    part += jnp.sum(jnp.where(lane < high % 128, edge, 0.0), -1, keepdims=True)
                dgates += jnp.where(lane % experts == expert, part, 0.0)
            dz = dz_plain * gate
            dg = (dz * u * (cdf + g * pdf)).astype(b16)
            du = (dz * act).astype(b16)
            zg = (z * gate).astype(b16)
            z_ref[span] = zg
            dg_ref[span] = dg
            du_ref[span] = du
            y = dot(zg, wd_ref[0], NN)
            db = dot(dg, wg_ref[0], NN) + dot(du, wu_ref[0], NN)
            if not ends:
                y_acc[span] = y
                db_acc[span] = db
                dgates_ref[span] = dgates
            else:
                dprob = dgates * keep
                inner = jnp.sum(jnp.where(lane < experts, share * dprob, 0.0), -1, keepdims=True)
                dl = jnp.where(lane < 2 * experts, share * (dprob - inner), 0.0)
                head = dl.astype(b16).astype(f32)
                split = jnp.where(lane < experts, head, dl - head).astype(b16)
                if n == 0:
                    rg_ref[...] = dot(b_v, split, TN)
                else:
                    rg_ref[...] += dot(b_v, split, TN)
                (y0, y1)[n][...] = (y + y_in[span]).astype(b16)
                (db0, db1)[n][...] = (db + db_in[span] + dot(split, r_ref[...], NT)).astype(b16)

    def weight(kind):
        return pl.BlockSpec((1, units, width), lambda i, at: (kind, 0, 0))

    hidden = pl.BlockSpec((rows, units), whole)
    one_spec = pl.BlockSpec((one, width), whole)
    both_spec = pl.BlockSpec((rows, width), whole)
    gate_spec = pl.BlockSpec((rows, 128), whole)
    both = jax.ShapeDtypeStruct((rows, width), b16)
    sums = jax.ShapeDtypeStruct((rows, width), f32)
    if ends:
        outs = [(one_spec, jax.ShapeDtypeStruct((one, width), b16))] * 4
        outs += [(pl.BlockSpec((width, 128), whole), jax.ShapeDtypeStruct((width, 128), f32))]
    else:
        outs = [(both_spec, both)] * 2 + [(both_spec, sums)] * 2
        outs += [(gate_spec, jax.ShapeDtypeStruct((rows, 128), f32))]
    outs += [(hidden, jax.ShapeDtypeStruct((rows, units), b16))] * 3
    return pl.pallas_call(
        body,
        grid_spec=pltpu.PrefetchScalarGridSpec(
            num_scalar_prefetch=1,
            grid=(1,),
            in_specs=([both_spec] * 4 + [gate_spec] if ends else [one_spec] * 4)
            + [
                pl.BlockSpec((one, 128), lambda i, at: (at[0], 0)),
                pl.BlockSpec((one, 128), lambda i, at: (at[1], 0)),
                pl.BlockSpec((width, 128), whole),
                weight(0),
                weight(1),
                weight(2),
            ],
            out_specs=[spec for spec, _ in outs],
        ),
        out_shape=[shape for _, shape in outs],
        compiler_params=params(60),
        cost_estimate=pl.CostEstimate(
            flops=(12 * rows * width * units) // ESTIMATE,
            bytes_accessed=(6 * units * width + 6 * rows * units) // ESTIMATE,
            transcendentals=2 * rows * units,
        ),
    )(blocks, *given, keep, keep, router, weights, weights, weights)


def experts_weights(me, bs, dys, opened, closed, parts):
    pieces = len(bs)
    rows, width = bs[0].shape
    first_units, last_units = opened[0][0].shape[1], closed[0][0].shape[1]
    units = first_units + last_units
    chunk = UNIT_CHUNK
    turn = first_units // chunk
    cut = width // parts
    blocked = cut % 128 == 0

    def body(me_ref, *refs):
        b_refs, dy_refs = refs[:pieces], refs[pieces : 2 * pieces]
        begun = refs[2 * pieces : 5 * pieces]
        ended = refs[5 * pieces : 8 * pieces]
        near, far, held = refs[8 * pieces :]

        def run(hidden):
            for kind, right in enumerate((b_refs, b_refs, dy_refs)):
                left = [hidden[n * 3 + (kind + 1) % 3] for n in range(pieces)]
                value = dot(left[0][...], right[0][...], TN)
                for n in range(1, pieces):
                    value += dot(left[n][...], right[n][...], TN)
                held[kind] = value.astype(b16)

        @pl.when(pl.program_id(0) < turn)
        def _():
            run(begun)

        @pl.when(pl.program_id(0) >= turn)
        def _():
            run(ended)

        for kind in range(3):
            for s in range(parts if blocked else 0):
                lanes = pl.ds(pl.multiple_of((me_ref[0] ^ s) * cut, cut), cut)
                (far if s % 2 else near)[s // 2, kind] = held[kind, :, lanes]
            if not blocked:
                near[0, kind] = held[kind, :, : width // 2]
                far[0, kind] = held[kind, :, width // 2 :]

    places, lanes = (parts // 2, cut) if blocked else (1, width // 2)
    return pl.pallas_call(
        body,
        grid_spec=pltpu.PrefetchScalarGridSpec(
            num_scalar_prefetch=1,
            grid=(units // chunk,),
            in_specs=[pl.BlockSpec((rows, width), whole)] * (2 * pieces)
            + [pl.BlockSpec((rows, chunk), lambda i, me: (0, jnp.minimum(i, turn - 1)))] * (3 * pieces)
            + [pl.BlockSpec((rows, chunk), lambda i, me: (0, jnp.maximum(i - turn, 0)))] * (3 * pieces),
            out_specs=[pl.BlockSpec((places, 3, chunk, lanes), lambda i, me: (0, 0, i, 0))] * 2,
            scratch_shapes=[pltpu.VMEM((3, chunk, width), b16)],
        ),
        out_shape=[jax.ShapeDtypeStruct((places, 3, units, lanes), b16)] * 2,
        compiler_params=params(56),
        cost_estimate=pl.CostEstimate(
            flops=6 * pieces * rows * width * units // ESTIMATE,
            bytes_accessed=(6 * units * width + 6 * pieces * rows * units) // ESTIMATE,
            transcendentals=0,
        ),
    )(me, *bs, *dys, *(v for part in opened for v in part), *(v for part in closed for v in part))


class Halving:
    def __init__(self, near, other, low, high):
        places = near.shape[0]
        half = (high - low) // 2
        bits = [1 << n for n in range(places.bit_length() - 1)]
        self.orders = [bits, bits[::-1]]
        self.held = []
        for path in range(2):
            span = slice(low + path * half, low + (path + 1) * half)
            self.held.append({s: near[s, span].astype(f32) + other[s, span].astype(f32) for s in range(places)})

    def sends(self):
        self.bits = [order.pop(0) for order in self.orders]
        out = []
        for held, bit in zip(self.held, self.bits):
            out.append((jnp.concatenate([held[s] for s in held if s & bit], 0).astype(b16), 2 * bit, "dp"))
        return out

    def take(self, got):
        for path, (held, bit, came) in enumerate(zip(self.held, self.bits, got)):
            away = [s for s in held if s & bit]
            size = came.shape[0] // len(away)
            self.held[path] = {s ^ bit: held[s ^ bit] + came[n * size : (n + 1) * size].astype(f32) for n, s in enumerate(away)}

    def result(self):
        return jnp.concatenate([held[0] for held in self.held], 0)


def input_gradient(dh, own, piece, sent, x, gains):
    rows, width = dh.shape

    def body(dh_ref, own_ref, piece_ref, sent_ref, x_ref, gain_ref, out_ref):
        da = own_ref[...] + (piece_ref[...].astype(f32) + sent_ref[...].astype(f32))
        unit, scale = unit_of(x_ref[...].astype(f32))
        along = da * gain_ref[0:1]
        inner = jnp.mean(along * unit, -1, keepdims=True)
        out_ref[...] = dh_ref[...] + scale * (along - unit * inner)

    block = pl.BlockSpec((CONT, width), lambda i: (i, 0))
    return pl.pallas_call(
        body,
        grid=(rows // CONT,),
        in_specs=[block] * 5 + [pl.BlockSpec(gains.shape, whole)],
        out_specs=block,
        out_shape=jax.ShapeDtypeStruct((rows, width), f32),
        compiler_params=params(32),
    )(dh, own, piece, sent, x, gains)


def on_device(inputs, cotangent, attn_gain, moe_gain, router, w_query, w_key, w_value, w_out, w_gate, w_up, w_down, expert_ids, priority):
    rows, width = inputs.shape
    experts, cut, own_units = w_gate.shape
    units = experts * own_units
    dp = lax.axis_size("dp")
    depth = lax.axis_size("tensor")
    own = lax.axis_index("tensor")
    me = lax.axis_index("dp")
    at = jnp.full((1,), own, jnp.int32)
    here = jnp.full((1,), me, jnp.int32)
    up = [(i, i + 1) for i in range(depth - 1)]
    down = [(i + 1, i) for i in range(depth - 1)]
    together = lax.optimization_barrier

    def swap(value, bits, axis="tensor"):
        size = depth if axis == "tensor" else dp
        return lax.ppermute(value, axis, [(i, i ^ bits) for i in range(size)])

    def raised(value):
        return lax.ppermute(value, "tensor", up)

    mine = jnp.stack([w_query, w_key, w_value, w_out.T])
    far = swap(mine, 2)
    attention_w = jnp.stack([mine, swap(mine, 1), far, swap(far, 1)])
    attention_w = lax.all_gather(attention_w, "dp", axis=2, tiled=True)

    small = jnp.concatenate([attn_gain[None], moe_gain[None], router.T, jnp.zeros((2, router.shape[0]), b16)], 0)

    def doubled(small, other, index, bit):
        return jnp.where(index & bit != 0, jnp.concatenate([other, small], 1), jnp.concatenate([small, other], 1))

    for bit in [1 << n for n in range(dp.bit_length() - 1)]:
        small = doubled(small, swap(small, bit, "dp"), me, bit)
    x1, other = together((raised(inputs), swap(small, 1)))
    small = doubled(small, other, own, 1)
    x2, other = together((raised(x1), swap(small, 2)))
    small = doubled(small, other, own, 2)
    small = small.reshape(8, depth, dp, -1).swapaxes(1, 2).reshape(8, width)
    x3 = raised(x2)
    gains = small.astype(f32)
    router_full = small[2 : 2 + experts].T
    router_wide = jnp.concatenate(
        [router_full, router_full, jnp.zeros((width, 128 - 2 * experts), b16)], 1
    )
    keep = keep_mask(expert_ids.T, priority.reshape(-1, 2).T, experts)

    shards = [w_gate.transpose(0, 2, 1), w_up.transpose(0, 2, 1), w_down]
    shards = jnp.stack([shard.reshape(units, cut) for shard in shards])
    middle = FIRST_CHUNKS * UNIT_CHUNK
    halves = [
        lax.all_gather(piece, "dp", axis=2, tiled=True)
        for piece in (shards[:, :middle], shards[:, middle:])
    ]

    x3, gains, dy0, keep, router_wide = together((x3, gains, cotangent, keep, router_wide))
    dy1, dy2 = swap(dy0, 1), swap(dy0, 2)
    a, q, k, v, p, inv, c, h, b = attention_forward(at, (inputs, x1, x2, x3), gains, attention_w)
    b, dy1, dy2 = together((b, dy1, dy2))
    b2 = swap(b, 2)
    bs = (b, swap(b, 1), b2, swap(b2, 1))
    dys = (dy0, dy1, dy2, swap(dy2, 1))

    def run(pair, half, given):
        blocks = jnp.stack([own ^ (2 * pair), own ^ (2 * pair + 1)]).astype(jnp.int32)
        return experts_blocks(blocks, given, keep, router_wide, halves[half], half * middle, own_units, experts, half == 1)

    opened_0 = run(0, 0, (bs[0], bs[1], dys[0], dys[1]))
    second, opened_0 = together(((bs[2], bs[3], dys[2], dys[3]), opened_0))
    opened_1 = run(1, 0, second)
    closed_1 = run(1, 1, opened_1[:5])
    opened_0, closed_1 = together((opened_0, closed_1))
    near3 = swap(closed_1[3], 1)
    closed_0 = run(0, 1, opened_0[:5])
    closed_0, near3 = together((closed_0, near3))
    joined = [opened_0[0], opened_1[0]], [opened_0[1], opened_1[1]]
    d1, d2 = closed_0[3], closed_1[2] + near3
    d1, d2, joined = together((d1, d2, joined))
    near, far = experts_weights(here, *joined, (opened_0[5:], opened_1[5:]), (closed_0[5:], closed_1[5:]), dp)
    d1, d2, near, far = together((swap(d1, 1), swap(d2, 2), near, far))
    blocked = cut % 128 == 0

    def stage(sends, given=(), work=None):
        values, given = together((tuple(value for value, *_ in sends), given))
        got = tuple(swap(value, *how) if how else lax.ppermute(value, "tensor", down) for value, (_, *how) in zip(values, sends))
        return together((got, work(given) if work else given))

    def backward(base):
        return lambda given: attention_backward(base, 2, given, gains, a, q, k, v, p, inv, c, attention_w, dp)

    def summed(dw):
        if blocked:
            return lax.psum_scatter(dw, "dp", scatter_dimension=0, tiled=True)[0]
        return lax.psum_scatter(dw[0], "dp", scatter_dimension=3, tiled=True)

    sends = [(far, 1, "dp")] if blocked else []
    given = (h, cotangent, closed_0[2], d1, d2)
    got, opened = stage(sends + [(closed_1[1], 1)], given, backward(0))
    heads_0 = summed(opened[0])
    y2 = closed_1[0] + got[-1]
    halvings = []
    if blocked:
        lines = 3 * units
        near = near.reshape(dp // 2, lines, cut)
        other = got[0].reshape(dp // 2, lines, cut)
        halvings = [Halving(near, other, 0, lines // 2), Halving(near, other, lines // 2, lines)]
    sends = halvings[0].sends() if blocked else []
    got, closed = stage(sends + [(closed_0[1], 1), (y2, 2)], (opened[2], opened[1]), backward(2))
    y1, y2 = got[-2:]
    if blocked:
        halvings[0].take(got[:2])
    heads_1 = summed(closed[0])
    dap, dao, dh = closed[1], closed[2], opened[2]

    def chunk_of(index):
        start = jnp.clip(index, 0, dap.shape[0] // rows - 1) * rows
        piece = lax.dynamic_slice_in_dim(dap, start, rows, 0)
        valid = (index >= 0) & (index < dap.shape[0] // rows)
        return jnp.where(valid, piece, jnp.zeros((), b16))

    rg = closed_0[4] + closed_1[4]
    rg = (rg[:, :experts] + rg[:, experts : 2 * experts]).T
    small_grad = jnp.concatenate([opened[3][:2] + closed[3][:2], rg], 0)
    sends = halvings[1].sends() if blocked else []
    got, small_grad = stage([(chunk_of(own - depth + 1),)] + sends, small_grad, lambda v: lax.psum(v, "tensor"))
    sent = got[0]
    if blocked:
        halvings[1].take(got[1:])
    pairs = [halving.sends() for halving in halvings if halving.orders[0]]
    sends = [(jnp.concatenate([one[0], two[0]], 0), *one[1:]) for one, two in zip(*pairs)] if pairs else []
    got, small_grad = stage([(chunk_of(own - depth + 2) + sent,)] + sends, small_grad, lambda v: lax.psum(v, "dp"))
    sent = got[0]
    if sends:
        for n, halving in enumerate(halvings):
            halving.take([came[n * came.shape[0] // 2 : (n + 1) * came.shape[0] // 2] for came in got[1:]])
    sent = lax.ppermute(chunk_of(own - depth + 3) + sent, "tensor", down)
    for halving in halvings:
        while halving.orders[0]:
            halving.take([swap(*send) for send in halving.sends()])

    slots = jnp.concatenate([heads_0, heads_1], 0)
    total = slots[0].astype(f32)
    for s in range(1, depth):
        total = total + swap(slots[s], s).astype(f32)
    count = width // (dp * depth)
    small_grad = lax.dynamic_slice_in_dim(small_grad, (me * depth + own) * count, count, 1)
    input_grad = input_gradient(dh, dao, chunk_of(own), sent, inputs, gains)
    output = h + closed_0[0].astype(f32) + y1.astype(f32) + y2.astype(f32)

    if blocked:
        total_units = jnp.concatenate([halving.result() for halving in halvings], 0).reshape(3, units, cut)
    else:
        pieces = jnp.concatenate([near[0], far[0]], -1)
        total_units = lax.psum_scatter(pieces, "dp", scatter_dimension=2, tiled=True).astype(f32)
    wg_grad, wu_grad, wd_grad = (total_units[n].reshape(experts, own_units, cut) for n in range(3))
    return (
        output.astype(b16),
        input_grad,
        small_grad[0],
        small_grad[1],
        small_grad[2:].T,
        total[0].T,
        total[1].T,
        total[2].T,
        total[3],
        wg_grad.transpose(0, 2, 1),
        wu_grad.transpose(0, 2, 1),
        wd_grad,
    )


def solution(mesh):
    tokens = P(("dp", "tensor"), None)
    vector = P(("dp", "tensor"))
    return jax.shard_map(
        on_device,
        mesh=mesh,
        in_specs=(tokens, tokens, vector, vector, tokens)
        + (P("dp", "tensor"),) * 3
        + (P("tensor", "dp"), P(None, "dp", "tensor"), P(None, "dp", "tensor"), P(None, "tensor", "dp"))
        + (P("dp", None), P("dp", None)),
        out_specs=(tokens, tokens, vector, vector, tokens)
        + (P("dp", "tensor"),) * 3
        + (P("tensor", "dp"), P(None, "dp", "tensor"), P(None, "dp", "tensor"), P(None, "tensor", "dp")),
        check_vma=False,
    )
```

time: 724 us -> 561 us (0.77)
  waiting for transfers between devices: 301 us -> 105 us
  other arithmetic: 22 us -> 41.9 us
  starting transfers between devices: 44.1 us -> 59.9 us
  blocking collectives: 86.2 us -> 78.7 us
    reduce_scatter x5 -> x2, waiting for transfers between devices: 112 us -> 0.01 us  [summed(): return lax.psum_scatter(dw, 'dp', scatter_dimension=0, tiled=True)[0]]
    psum x0 -> x2, blocking collectives: none -> 78.7 us  [the longest x1 51.7 us: on_device(): lax.psum(v, 'dp')]
    all_gather x2 -> x0, blocking collectives: 63.5 us -> none  [the longest x1 54.6 us: on_device(): lax.all_gather(small, 'tensor', axis=0, tiled=True)]
    ppermute x24 -> x36, waiting for transfers between devices: 146 us -> 105 us  [the longest x30 85.7 us: swap(): return lax.ppermute(value, axis, [(i, i ^ bits) for i in range(size)])]
    all_gather x4 -> x3, waiting for transfers between devices: 38.6 us -> 0.02 us  [the longest x2 0.01 us: on_device(): lax.all_gather(piece, 'dp', axis=2, tiled=True)]
    unnamed x1 -> x0, blocking collectives: 22.7 us -> none
    ppermute x24 -> x36, starting transfers between devices: 43.6 us -> 59.7 us  [the longest x30 42.5 us: swap(): return lax.ppermute(value, axis, [(i, i ^ bits) for i in range(size)])]
    add x5 -> x9, other arithmetic: 5.88 us -> 19.2 us  [the longest x1 5.54 us: __init__(): near[s, span].astype(f32) + other[s, span].astype(f32)]
  transfers between devices with their start and end apart: 33 -> 41, of which waited for: 11 -> 15; matrix products, arithmetic and copies ran while one was open for 4% -> 8% of each run, Pallas kernels for 25% -> 38%
where the time goes in v2:
time: 561 us; the launch traced here: 552 us
  Pallas kernels  235 us (42%)
  waiting for transfers between devices  105 us (19%)
  blocking collectives  78.7 us (14%)
  starting transfers between devices  59.9 us (11%)
  other arithmetic  41.9 us (7%)
  local copies, waits for them, and re-layouts  16.4 us (3%)
  between operations  14.7 us (3%)
    pallas_call x4, Pallas kernels, experts_blocks(): pl.pallas_call(body, grid_spec=pltpu.PrefetchScalarGridSpec(num_scalar_pr...  100 us
    ppermute x30, waiting for transfers between devices, swap(): return lax.ppermute(value, axis, [(i, i ^ bits) for i in range(size)])  85.7 us
    pallas_call x2, Pallas kernels, attention_backward(): pl.pallas_call(body, grid=(count,), in_specs=([row_spec] * 5 if opens els...  57.3 us
    psum x1, blocking collectives, on_device(): lax.psum(v, 'dp')  51.7 us
    ppermute x30, starting transfers between devices, swap(): return lax.ppermute(value, axis, [(i, i ^ bits) for i in range(size)])  42.5 us
    pallas_call x1, Pallas kernels, experts_weights(): pl.pallas_call(body, grid_spec=pltpu.PrefetchScalarGridSpec(num_scalar_pr...  40.3 us
    pallas_call x1, Pallas kernels, attention_forward(): pl.pallas_call(body, grid_spec=pltpu.PrefetchScalarGridSpec(num_scalar_pr...  32.3 us
    psum x1, blocking collectives, on_device(): lax.psum(v, 'tensor')  27.1 us
  transfers between devices with their start and end apart: 41, of which 15 were waited for; matrix products, arithmetic and copies ran while one was open for 8% of the time, Pallas kernels for 38%

profile of v2, /device:TPU:0, one launch (start us, length us, event | category | flops | bytes accessed | tf_op | source)
XLA Modules:
  0.0 551.5 jit_solution(8899517168234661322)
XLA Ops:
  9.1 4.1 collective-permute-start.9
  14.8 10.5 %collective-permute-done.9 = bf16[4,128,256]{2,1,0:T(8,128)(2,1)S(1)} collective-permute-done((bf16[4,128,256]{2,1,0:T(8,128)(2,1)S(1)}, bf16[4,128,256]{2,1,0:T(8,128)(2,1)S(1)}, u32[]{:S(2)}, u32[]{:S(2)}) %collective-permute-start.9) | collective-permute-done | bytes 262176 | tf_op jit(solution)/shard_map/ppermute | solution.py:614
  25.9 6.8 %collective-permute-done.10 = bf16[4,128,256]{2,1,0:T(8,128)(2,1)S(1)} collective-permute-done((bf16[4,128,256]{2,1,0:T(8,128)(2,1)S(1)}, bf16[4,128,256]{2,1,0:T(8,128)(2,1)S(1)}, u32[]{:S(2)}, u32[]{:S(2)}) %collective-permute-start.10) | collective-permute-done | bytes 262176 | tf_op jit(solution)/shard_map/ppermute | solution.py:614
  37.2 3.4 collective-permute-start
  51.4 5.4 collective-permute-done.4
  56.7 4.4 collective-permute-start.5
  61.2 3.4 collective-permute-start.6
  64.6 12.2 %collective-permute-done.6 = bf16[8,512]{1,0:T(8,128)(2,1)S(1)} collective-permute-done((bf16[8,512]{1,0:T(8,128)(2,1)S(1)}, bf16[8,512]{1,0:T(8,128)(2,1)S(1)}, u32[]{:S(2)}, u32[]{:S(2)}) %collective-permute-start.6) | collective-permute-done | bytes 8224 | tf_op jit(solution)/shard_map/ppermute | solution.py:614
  76.8 5.5 %collective-permute-start.7 = (bf16[384,1024]{1,0:T(8,128)(2,1)S(1)}, bf16[384,1024]{1,0:T(8,128)(2,1)}, u32[]{:S(2)}, u32[]{:S(2)}) collective-permute-start(bf16[384,1024]{1,0:T(8,128)(2,1)S(1)} %collective-permute-done.5.x2), channel_id=1, source_target_pairs={{0,1},{1,2},{2,3},{4,5},{5,6},{6,7},{8,9},{9,10},{10,11},{12,13},{... | collective-permute-start | bytes 2359304 | tf_op jit(solution)/shard_map/ppermute | solution.py:617
  89.7 6.4 %collective-permute-done.7.x3 = bf16[384,1024]{1,0:T(8,128)(2,1)} collective-permute-done((bf16[384,1024]{1,0:T(8,128)(2,1)S(1)}, bf16[384,1024]{1,0:T(8,128)(2,1)}, u32[]{:S(2)}, u32[]{:S(2)}) %collective-permute-start.7) | collective-permute-done | bytes 786464 | tf_op jit(solution)/shard_map/ppermute | solution.py:617
  96.0 4.4 collective-permute-start.12
  103.0 32.3 %shard_map.230 = (bf16[1408,1024]{1,0:T(8,128)(2,1)}, bf16[384,1024]{1,0:T(8,128)(2,1)}, bf16[1408,1024]{1,0:T(8,128)(2,1)}, bf16[1408,1024]{1,0:T(8,128)(2,1)},...) custom-call(s32[1]{0:T(128)} %bitcast.at_ref, ...), custom_call_target="tpu_custom_call" | custom-call | flops 2785017856 | bytes 15728640 | tf_op jit(solution)/shard_map/pallas_call | solution.py:159
  137.6 31.4 %collective-permute-done.13.refs_0_ = bf16[384,1024]{1,0:T(8,128)(2,1)S(1)} collective-permute-done((bf16[384,1024]{1,0:T(8,128)(2,1)}, bf16[384,1024]{1,0:T(8,128)(2,1)S(1)}, u32[]{:S(2)}, u32[]{:S(2)}) %collective-permute-start.13) | collective-permute-done | bytes 786464 | tf_op jit(solution)/shard_map/ppermute | solution.py:614
  172.5 24.1 %shard_map.231 = (bf16[768,1024]{1,0:T(8,128)(2,1)}, bf16[768,1024]{1,0:T(8,128)(2,1)}, f32[768,1024]{1,0:T(8,128)}, f32[768,1024]{1,0:T(8,128)}, f32[768,128]{1...) custom-call(s32[2]{0:T(128)} %pad_add_fusion.blocks_ref, ...), custom_call_target="tpu_custom_call" | custom-call | flops 3623878656 | bytes 4128768 | tf_op jit(solution)/shard_map/pallas_call | solution.py:461
  196.7 6.2 %collective-permute-done.14.refs_1_ = bf16[384,1024]{1,0:T(8,128)(2,1)} collective-permute-done((bf16[384,1024]{1,0:T(8,128)(2,1)S(1)}, bf16[384,1024]{1,0:T(8,128)(2,1)}, u32[]{:S(2)}, u32[]{:S(2)}) %collective-permute-start.14) | collective-permute-done | bytes 786464 | tf_op jit(solution)/shard_map/ppermute | solution.py:614
  202.8 24.8 %shard_map.232 = (bf16[768,1024]{1,0:T(8,128)(2,1)}, bf16[768,1024]{1,0:T(8,128)(2,1)}, f32[768,1024]{1,0:T(8,128)}, f32[768,1024]{1,0:T(8,128)}, f32[768,128]{1...) custom-call(s32[2]{0:T(128)} %pad_add_fusion.1.blocks_ref, ...), custom_call_target="tpu_custom_call" | custom-call | flops 3623878656 | bytes 4128768 | tf_op jit(solution)/shard_map/pallas_call | solution.py:461
  227.6 25.7 %shard_map.233 = (bf16[384,1024]{1,0:T(8,128)(2,1)}, bf16[384,1024]{1,0:T(8,128)(2,1)}, bf16[384,1024]{1,0:T(8,128)(2,1)}, bf16[384,1024]{1,0:T(8,128)(2,1)}, f3...) custom-call(s32[2]{0:T(128)} %pad_add_fusion.1.blocks_ref, ...), custom_call_target="tpu_custom_call" | custom-call | flops 3019898880 | bytes 3440640 | tf_op jit(solution)/shard_map/pallas_call | solution.py:461
  253.4 25.5 %shard_map.234 = (bf16[384,1024]{1,0:T(8,128)(2,1)}, bf16[384,1024]{1,0:T(8,128)(2,1)}, bf16[384,1024]{1,0:T(8,128)(2,1)}, bf16[384,1024]{1,0:T(8,128)(2,1)}, f3...) custom-call(s32[2]{0:T(128)} %pad_add_fusion.blocks_ref, ...), custom_call_target="tpu_custom_call" | custom-call | flops 3019898880 | bytes 3440640 | tf_op jit(solution)/shard_map/pallas_call | solution.py:461
  282.4 40.3 %shard_map.235 = (bf16[4,3,2816,128]{3,2,1,0:T(8,128)(2,1)}, bf16[4,3,2816,128]{3,2,1,0:T(8,128)(2,1)}) custom-call(s32[1]{0:T(128)} %bitcast.26.me_ref, bf16[768,1024]{1,0:T(8,128)(2,1)} %get-tuple-element.232.refs_0_, bf16[768,1024]{1,0:T(8,128)(2,1)} %get-tuple-element.233.refs_0_.refs_1_, bf16[768,1024]{1,0:T(8,128)(2,1)} %get-tuple-element.234.refs_1_.refs_2_, ...), custom_call_target="tpu_custom_call" | custom-call | flops 6643777536 | bytes 10813440 | tf_op jit(solution)/shard_map/pallas_call | solution.py:528
  324.7 28.4 %shard_map.236 = (bf16[8,2,4,256,128]{4,3,2,1,0:T(8,128)(2,1)}, f32[1408,1024]{1,0:T(8,128)}, f32[384,1024]{1,0:T(8,128)}, f32[8,1024]{1,0:T(8,128)}) custom-call(f32[384,1024]{1,0:T(8,128)} %get-tuple-element.258.refs_0_, bf16[384,1024]{1,0:T(8,128)(2,1)} %refs_1_, bf16[384,1024]{1,0:T(8,128)(2,1)} %get-tuple-element.260.refs_2_, ...), custom_call_target="tpu_custom_call" | custom-call | flops 2785017856 | bytes 10485760 | tf_op jit(solution)/shard_map/pallas_call | solution.py:319
  355.8 5.5 %fusion.14 = (bf16[2112,128]{1,0:T(8,128)(2,1)S(1)}, bf16[2112,128]{1,0:T(8,128)(2,1)S(1)}, bf16[2112,128]{1,0:T(8,128)(2,1)}, bf16[2112,128]{1,0:T(8,128)(2,1)}...) fusion(bf16[4,8448,128]{2,1,0:T(8,128)(2,1)} %bitcast.28, ...), kind=kLoop, calls=%fused_computation.47 | loop fusion | flops 8650752 | bytes 12976128 | tf_op jit(solution)/shard_map/add | solution.py:558
  368.5 28.9 %shard_map.237 = (bf16[8,2,4,256,128]{4,3,2,1,0:T(8,128)(2,1)}, bf16[1152,1024]{1,0:T(8,128)(2,1)}, f32[384,1024]{1,0:T(8,128)}, f32[8,1024]{1,0:T(8,128)}) custom-call(f32[384,1024]{1,0:T(8,128)} %get-tuple-element.284.refs_0_.dh_ref, f32[1408,1024]{1,0:T(8,128)} %get-tuple-element.285.refs_1_, f32[8,1024]{1,0:T(8,128)} %reshape.131.gain_ref.refs_5_.refs_2_, ...), custom_call_target="tpu_custom_call" | custom-call | flops 2785017856 | bytes 10485760 | tf_op jit(solution)/shard_map/pallas_call | solution.py:319
  397.4 2.7 pad_maximum_fusion.6
  407.9 27.1 %psum.14 = f32[6,1024]{1,0:T(8,128)S(1)} all-reduce(f32[6,1024]{1,0:T(8,128)S(1)} %pad_maximum_fusion.13), channel_id=1, replica_groups=mesh['dp'=8,'tensor'=4] {'tensor'}, use_global_device_ids=true, to_apply=%region_0.1 | all-reduce | flops 6144 | bytes 49152 | tf_op jit(solution)/shard_map/psum | solution.py:721
  437.4 3.6 fusion.5
  447.4 2.8 add_convert_fusion
  450.2 51.7 %psum.15 = f32[6,1024]{1,0:T(8,128)S(1)} all-reduce(f32[6,1024]{1,0:T(8,128)S(1)} %psum.14), channel_id=1, replica_groups=mesh['dp'=8,'tensor'=4] {'dp'}, use_global_device_ids=true, to_apply=%region_1.2 | all-reduce | flops 6144 | bytes 49152 | tf_op jit(solution)/shard_map/psum | solution.py:727
  501.9 3.0 select_add_fusion.1
  506.3 4.4 fusion
  513.9 2.7 collective-permute-start.33
  521.3 12.8 %collective-permute-done.32.sent_ref = bf16[384,1024]{1,0:T(8,128)(2,1)} collective-permute-done((bf16[384,1024]{1,0:T(8,128)(2,1)}, bf16[384,1024]{1,0:T(8,128)(2,1)}, u32[]{:S(2)}, u32[]{:S(2)}) %collective-permute-start.32) | collective-permute-done | bytes 786464 | tf_op jit(solution)/shard_map/ppermute | solution.py:732
  535.5 3.5 shard_map.238
  (194 shorter events, 83.1 us)
Async XLA Ops:
  7.2 95.8 %all-gather.4.cloned.1.call-start = ((), (), s32[]{:S(2)}) async-start(), calls=%async_computation.2 | async-start | bytes 9437184 | tf_op jit(solution)/shard_map/all_gather | solution.py:622
  33.8 138.7 %all-gather.6.cloned.1.call-start = ((), (), s32[]{:S(2)}) async-start(), calls=%async_computation.3 | async-start | bytes 10616832 | tf_op jit(solution)/shard_map/all_gather | solution.py:648
  36.0 191.6 %all-gather.8.cloned.1.call-start = ((), (), s32[]{:S(2)}) async-start(), calls=%async_computation.4 | async-start | bytes 8847360 | tf_op jit(solution)/shard_map/all_gather | solution.py:648
  37.1 475.7 %reduce-scatter.3.cloned.1.call-start = ((), (), s32[]{:S(2)}) async-start(), calls=%async_computation.5 | async-start | bytes 4718592 | tf_op jit(solution)/shard_map/reduce_scatter | solution.py:689
  37.2 19.5 %collective-permute-start = (bf16[384,1024]{1,0:T(8,128)(2,1)S(1)}, bf16[384,1024]{1,0:T(8,128)(2,1)S(1)}, u32[]{:S(2)}, u32[]{:S(2)}) collective-permute-start(bf16[384,1024]{1,0:T(8,128)(2,1)S(1)} %copy-done.3), channel_id=1, source_target_pairs={{0,1},{1,2},{2,3},{4,5},{5,6},{6,7},{8,9},{9,10},{10,11},{12,13},{... | collective-permute-start | bytes 2359304 | tf_op jit(solution)/shard_map/ppermute | solution.py:617
  56.7 20.0 %collective-permute-start.5 = (bf16[384,1024]{1,0:T(8,128)(2,1)S(1)}, bf16[384,1024]{1,0:T(8,128)(2,1)S(1)}, u32[]{:S(2)}, u32[]{:S(2)}) collective-permute-start(bf16[384,1024]{1,0:T(8,128)(2,1)S(1)} %collective-permute-done.x1), channel_id=1, source_target_pairs={{0,1},{1,2},{2,3},{4,5},{5,6},{6,7},{8,9},{9,10},{10,11},{12,13},{... | collective-permute-start | bytes 2359304 | tf_op jit(solution)/shard_map/ppermute | solution.py:617
  96.0 39.2 %collective-permute-start.12 = (bf16[384,1024]{1,0:T(8,128)(2,1)S(1)}, bf16[384,1024]{1,0:T(8,128)(2,1)S(1)}, u32[]{:S(2)}, u32[]{:S(2)}) collective-permute-start(bf16[384,1024]{1,0:T(8,128)(2,1)S(1)} %copy-done.9), channel_id=1, source_target_pairs={{0,2},{1,3},{2,0},{3,1},{4,6},{5,7},{6,4},{7,5},{8,10},{9,11},{10,... | collective-permute-start | bytes 2359304 | tf_op jit(solution)/shard_map/ppermute | solution.py:614
  100.5 34.8 %collective-permute-start.11 = (bf16[384,1024]{1,0:T(8,128)(2,1)S(1)}, bf16[384,1024]{1,0:T(8,128)(2,1)S(1)}, u32[]{:S(2)}, u32[]{:S(2)}) collective-permute-start(bf16[384,1024]{1,0:T(8,128)(2,1)S(1)} %copy-done.9), channel_id=1, source_target_pairs={{0,1},{1,0},{2,3},{3,2},{4,5},{5,4},{6,7},{7,6},{8,9},{9,8},{10,11... | collective-permute-start | bytes 2359304 | tf_op jit(solution)/shard_map/ppermute | solution.py:614
  135.3 33.7 %collective-permute-start.13 = (bf16[384,1024]{1,0:T(8,128)(2,1)}, bf16[384,1024]{1,0:T(8,128)(2,1)S(1)}, u32[]{:S(2)}, u32[]{:S(2)}) collective-permute-start(bf16[384,1024]{1,0:T(8,128)(2,1)} %get-tuple-element.174.refs_0_), channel_id=1, source_target_pairs={{0,2},{1,3},{2,0},{3,1},{4,6},{5,7},{6,4},{7,5},{8,10},{9,11},{10,... | collective-permute-start | bytes 2359304 | tf_op jit(solution)/shard_map/ppermute | solution.py:614
  135.5 37.0 %collective-permute-start.16 = (bf16[384,1024]{1,0:T(8,128)(2,1)}, bf16[384,1024]{1,0:T(8,128)(2,1)}, u32[]{:S(2)}, u32[]{:S(2)}) collective-permute-start(bf16[384,1024]{1,0:T(8,128)(2,1)} %get-tuple-element.174.refs_0_), channel_id=1, source_target_pairs={{0,1},{1,0},{2,3},{3,2},{4,5},{5,4},{6,7},{7,6},{8,9},{9,8},{10,11... | collective-permute-start | bytes 2359304 | tf_op jit(solution)/shard_map/ppermute | solution.py:614
  135.9 60.8 %collective-permute-start.15 = (bf16[384,1024]{1,0:T(8,128)(2,1)S(1)}, bf16[384,1024]{1,0:T(8,128)(2,1)S(1)}, u32[]{:S(2)}, u32[]{:S(2)}) collective-permute-start(bf16[384,1024]{1,0:T(8,128)(2,1)S(1)} %collective-permute-done.12.refs_2_), channel_id=1, source_target_pairs={{0,1},{1,0},{2,3},{3,2},{4,5},{5,4},{6,7},{7,6},{8,9},{9,8},{10,11... | collective-permute-start | bytes 2359304 | tf_op jit(solution)/shard_map/ppermute | solution.py:614
  168.9 33.9 %collective-permute-start.14 = (bf16[384,1024]{1,0:T(8,128)(2,1)S(1)}, bf16[384,1024]{1,0:T(8,128)(2,1)}, u32[]{:S(2)}, u32[]{:S(2)}) collective-permute-start(bf16[384,1024]{1,0:T(8,128)(2,1)S(1)} %collective-permute-done.13.refs_0_), channel_id=1, source_target_pairs={{0,1},{1,0},{2,3},{3,2},{4,5},{5,4},{6,7},{7,6},{8,9},{9,8},{10,11... | collective-permute-start | bytes 2359304 | tf_op jit(solution)/shard_map/ppermute | solution.py:614
  253.3 25.6 %collective-permute-start.17 = (bf16[384,1024]{1,0:T(8,128)(2,1)}, bf16[384,1024]{1,0:T(8,128)(2,1)S(1)}, u32[]{:S(2)}, u32[]{:S(2)}) collective-permute-start(bf16[384,1024]{1,0:T(8,128)(2,1)} %get-tuple-element.225), channel_id=1, source_target_pairs={{0,1},{1,0},{2,3},{3,2},{4,5},{5,4},{6,7},{7,6},{8,9},{9,8},{10,11... | collective-permute-start | bytes 2359304 | tf_op jit(solution)/shard_map/ppermute | solution.py:614
  280.1 42.7 %collective-permute-start.18 = (bf16[384,1024]{1,0:T(8,128)(2,1)S(1)}, bf16[384,1024]{1,0:T(8,128)(2,1)S(1)}, u32[]{:S(2)}, u32[]{:S(2)}) collective-permute-start(bf16[384,1024]{1,0:T(8,128)(2,1)S(1)} %copy-done.33), channel_id=1, source_target_pairs={{0,1},{1,0},{2,3},{3,2},{4,5},{5,4},{6,7},{7,6},{8,9},{9,8},{10,11... | collective-permute-start | bytes 2359304 | tf_op jit(solution)/shard_map/ppermute | solution.py:614
  281.9 40.8 %collective-permute-start.19 = (bf16[384,1024]{1,0:T(8,128)(2,1)S(1)}, bf16[384,1024]{1,0:T(8,128)(2,1)S(1)}, u32[]{:S(2)}, u32[]{:S(2)}) collective-permute-start(bf16[384,1024]{1,0:T(8,128)(2,1)S(1)} %add.214), channel_id=1, source_target_pairs={{0,2},{1,3},{2,0},{3,1},{4,6},{5,7},{6,4},{7,5},{8,10},{9,11},{10,... | collective-permute-start | bytes 2359304 | tf_op jit(solution)/shard_map/ppermute | solution.py:614
  322.8 30.3 %collective-permute-start.20 = (bf16[4,3,2816,128]{3,2,1,0:T(8,128)(2,1)}, bf16[4,3,2816,128]{3,2,1,0:T(8,128)(2,1)}, u32[]{:S(2)}, u32[]{:S(2)}) collective-permute-start(bf16[4,3,2816,128]{3,2,1,0:T(8,128)(2,1)} %get-tuple-element.256), channel_id=1, source_target_pairs={{0,4},{4,0},{8,12},{12,8},{16,20},{20,16},{24,28},{28,24},{1,5},{5... | collective-permute-start | bytes 25952264 | tf_op jit(solution)/shard_map/ppermute | solution.py:614
  322.9 30.2 %collective-permute-start.21 = (bf16[384,1024]{1,0:T(8,128)(2,1)S(1)}, bf16[384,1024]{1,0:T(8,128)(2,1)S(1)}, u32[]{:S(2)}, u32[]{:S(2)}) collective-permute-start(bf16[384,1024]{1,0:T(8,128)(2,1)S(1)} %copy-done.32), channel_id=1, source_target_pairs={{0,1},{1,0},{2,3},{3,2},{4,5},{5,4},{6,7},{7,6},{8,9},{9,8},{10,11... | collective-permute-start | bytes 2359304 | tf_op jit(solution)/shard_map/ppermute | solution.py:614
  353.2 163.4 %reduce-scatter.5.cloned.1.call-start = ((), (), s32[]{:S(2)}) async-start(), calls=%async_computation.6 | async-start | bytes 4718592 | tf_op jit(solution)/shard_map/reduce_scatter | solution.py:689
  362.8 41.2 %collective-permute-start.22 = (bf16[4224,128]{1,0:T(8,128)(2,1)}, bf16[4224,128]{1,0:T(8,128)(2,1)}, u32[]{:S(2)}, u32[]{:S(2)}) collective-permute-start(bf16[4224,128]{1,0:T(8,128)(2,1)} %get-tuple-element.280), channel_id=1, source_target_pairs={{0,8},{4,12},{8,0},{12,4},{16,24},{20,28},{24,16},{28,20},{1,9},{5... | collective-permute-start | bytes 3244040 | tf_op jit(solution)/shard_map/ppermute | solution.py:614
  364.3 39.7 %collective-permute-start.23 = (bf16[4224,128]{1,0:T(8,128)(2,1)}, bf16[4224,128]{1,0:T(8,128)(2,1)}, u32[]{:S(2)}, u32[]{:S(2)}) collective-permute-start(bf16[4224,128]{1,0:T(8,128)(2,1)} %get-tuple-element.281), channel_id=1, source_target_pairs={{0,16},{4,20},{8,24},{12,28},{16,0},{20,4},{24,8},{28,12},{1,17},{... | collective-permute-start | bytes 3244040 | tf_op jit(solution)/shard_map/ppermute | solution.py:614
  366.7 34.7 %collective-permute-start.24 = (bf16[384,1024]{1,0:T(8,128)(2,1)}, bf16[384,1024]{1,0:T(8,128)(2,1)}, u32[]{:S(2)}, u32[]{:S(2)}) collective-permute-start(bf16[384,1024]{1,0:T(8,128)(2,1)} %get-tuple-element.282), channel_id=1, source_target_pairs={{0,1},{1,0},{2,3},{3,2},{4,5},{5,4},{6,7},{7,6},{8,9},{9,8},{10,11... | collective-permute-start | bytes 2359304 | tf_op jit(solution)/shard_map/ppermute | solution.py:614
  367.7 36.3 %collective-permute-start.25 = (bf16[384,1024]{1,0:T(8,128)(2,1)}, bf16[384,1024]{1,0:T(8,128)(2,1)}, u32[]{:S(2)}, u32[]{:S(2)}) collective-permute-start(bf16[384,1024]{1,0:T(8,128)(2,1)} %add.223), channel_id=1, source_target_pairs={{0,2},{1,3},{2,0},{3,1},{4,6},{5,7},{6,4},{7,5},{8,10},{9,11},{10,... | collective-permute-start | bytes 2359304 | tf_op jit(solution)/shard_map/ppermute | solution.py:614
  405.9 29.1 %collective-permute-start.27 = (bf16[4224,128]{1,0:T(8,128)(2,1)}, bf16[4224,128]{1,0:T(8,128)(2,1)S(1)}, u32[]{:S(2)}, u32[]{:S(2)}) collective-permute-start(bf16[4224,128]{1,0:T(8,128)(2,1)} %get-tuple-element.299), channel_id=1, source_target_pairs={{0,8},{4,12},{8,0},{12,4},{16,24},{20,28},{24,16},{28,20},{1,9},{5... | collective-permute-start | bytes 3244040 | tf_op jit(solution)/shard_map/ppermute | solution.py:614
  406.3 28.7 %collective-permute-start.28 = (bf16[4224,128]{1,0:T(8,128)(2,1)}, bf16[4224,128]{1,0:T(8,128)(2,1)}, u32[]{:S(2)}, u32[]{:S(2)}) collective-permute-start(bf16[4224,128]{1,0:T(8,128)(2,1)} %get-tuple-element.300), channel_id=1, source_target_pairs={{0,16},{4,20},{8,24},{12,28},{16,0},{20,4},{24,8},{28,12},{1,17},{... | collective-permute-start | bytes 3244040 | tf_op jit(solution)/shard_map/ppermute | solution.py:614
  406.6 28.4 %collective-permute-start.26 = (bf16[384,1024]{1,0:T(8,128)(2,1)}, bf16[384,1024]{1,0:T(8,128)(2,1)}, u32[]{:S(2)}, u32[]{:S(2)}) collective-permute-start(bf16[384,1024]{1,0:T(8,128)(2,1)} %dynamic-slice_select_fusion), channel_id=1, source_target_pairs={{1,0},{2,1},{3,2},{5,4},{6,5},{7,6},{9,8},{10,9},{11,10},{13,12},{... | collective-permute-start | bytes 2359304 | tf_op jit(solution)/shard_map/ppermute | solution.py:681
  443.2 58.6 %collective-permute-start.30 = (bf16[4224,128]{1,0:T(8,128)(2,1)}, bf16[4224,128]{1,0:T(8,128)(2,1)}, u32[]{:S(2)}, u32[]{:S(2)}) collective-permute-start(bf16[4224,128]{1,0:T(8,128)(2,1)} %pad_maximum_fusion.8), channel_id=1, source_target_pairs={{0,16},{4,20},{8,24},{12,28},{16,0},{20,4},{24,8},{28,12},{1,17},{... | collective-permute-start | bytes 3244040 | tf_op jit(solution)/shard_map/ppermute | solution.py:614
  444.6 57.2 %collective-permute-start.31 = (bf16[4224,128]{1,0:T(8,128)(2,1)}, bf16[4224,128]{1,0:T(8,128)(2,1)}, u32[]{:S(2)}, u32[]{:S(2)}) collective-permute-start(bf16[4224,128]{1,0:T(8,128)(2,1)} %pad_maximum_fusion.9), channel_id=1, source_target_pairs={{0,8},{4,12},{8,0},{12,4},{16,24},{20,28},{24,16},{28,20},{1,9},{5... | collective-permute-start | bytes 3244040 | tf_op jit(solution)/shard_map/ppermute | solution.py:614
  446.1 55.8 %collective-permute-start.29 = (bf16[384,1024]{1,0:T(8,128)(2,1)}, bf16[384,1024]{1,0:T(8,128)(2,1)}, u32[]{:S(2)}, u32[]{:S(2)}) collective-permute-start(bf16[384,1024]{1,0:T(8,128)(2,1)} %select_add_fusion), channel_id=1, source_target_pairs={{1,0},{2,1},{3,2},{5,4},{6,5},{7,6},{9,8},{10,9},{11,10},{13,12},{... | collective-permute-start | bytes 2359304 | tf_op jit(solution)/shard_map/ppermute | solution.py:681
  504.9 29.1 %collective-permute-start.32 = (bf16[384,1024]{1,0:T(8,128)(2,1)}, bf16[384,1024]{1,0:T(8,128)(2,1)}, u32[]{:S(2)}, u32[]{:S(2)}) collective-permute-start(bf16[384,1024]{1,0:T(8,128)(2,1)} %get-tuple-element.372), channel_id=1, source_target_pairs={{1,0},{2,1},{3,2},{5,4},{6,5},{7,6},{9,8},{10,9},{11,10},{13,12},{... | collective-permute-start | bytes 2359304 | tf_op jit(solution)/shard_map/ppermute | solution.py:732
  513.9 26.8 %collective-permute-start.33 = (bf16[4,256,128]{2,1,0:T(8,128)(2,1)S(1)}, bf16[4,256,128]{2,1,0:T(8,128)(2,1)}, u32[]{:S(2)}, u32[]{:S(2)}) collective-permute-start(bf16[4,256,128]{2,1,0:T(8,128)(2,1)S(1)} %slice_bitcast_fusion.2), channel_id=1, source_target_pairs={{0,1},{1,0},{2,3},{3,2},{4,5},{5,4},{6,7},{7,6},{8,9},{9,8},{10,11... | collective-permute-start | bytes 786440 | tf_op jit(solution)/shard_map/ppermute | solution.py:614
  517.7 23.0 %collective-permute-start.34 = (bf16[4,256,128]{2,1,0:T(8,128)(2,1)S(1)}, bf16[4,256,128]{2,1,0:T(8,128)(2,1)S(1)}, u32[]{:S(2)}, u32[]{:S(2)}) collective-permute-start(bf16[4,256,128]{2,1,0:T(8,128)(2,1)S(1)} %get-tuple-element.381), channel_id=1, source_target_pairs={{0,2},{1,3},{2,0},{3,1},{4,6},{5,7},{6,4},{7,5},{8,10},{9,11},{10,... | collective-permute-start | bytes 786440 | tf_op jit(solution)/shard_map/ppermute | solution.py:614
  517.8 22.9 %collective-permute-start.35 = (bf16[4,256,128]{2,1,0:T(8,128)(2,1)S(1)}, bf16[4,256,128]{2,1,0:T(8,128)(2,1)S(1)}, u32[]{:S(2)}, u32[]{:S(2)}) collective-permute-start(bf16[4,256,128]{2,1,0:T(8,128)(2,1)S(1)} %get-tuple-element.382), channel_id=1, source_target_pairs={{0,3},{1,2},{2,1},{3,0},{4,7},{5,6},{6,5},{7,4},{8,11},{9,10},{10,... | collective-permute-start | bytes 786440 | tf_op jit(solution)/shard_map/ppermute | solution.py:614
  (43 other events, 582.3 us)
Sparse Core Ops, SparseCore 0:
  33.9 56.2 all-gather.3
  92.7 60.5 all-gather.5
  155.8 53.6 all-gather.7
  353.3 67.0 reduce-scatter.2
  424.0 63.3 reduce-scatter.4

commit v3 on v2

--- a/solution.py
+++ b/solution.py
@@ -21,6 +21,7 @@
 INV_SQRT2 = 0.7071067811865476
 INV_SQRT_2PI = 0.3989422804014327
 MASKED = -1e30
+SMALL_ROWS = 32
 UNIT_CHUNK = 256
 ESTIMATE = 4
 FIRST_CHUNKS = 6
@@ -199,7 +200,7 @@
     )(at, *slots, gains, weights)
 
 
-def attention_backward(base, count, given, gains, a, q, k, v, p, inv, c, weights, parts):
+def attention_backward(me, base, count, given, rest, gains, a, q, k, v, p, inv, c, weights, parts):
     opens = base == 0
     rows, width = q.shape
     _, _, _, cols = weights.shape
@@ -209,32 +210,36 @@
     pairs = cols // PAIR
     keys = PROMPT + CONT
     cut = width // parts
-
-    def body(*refs):
-        n_given = 5 if opens else 2
+    blocked = cut % 128 == 0
+    places, lanes_out = (parts // 2, cut) if blocked else (1, width // 2)
+
+    def body(me_ref, *refs):
+        n_given = 6 if opens else 2
         given_refs = refs[:n_given]
         gain_ref, a_ref, q_ref, k_ref, v_ref, p_ref, inv_ref, c_ref, w_ref = refs[n_given : n_given + 9]
-        dw_ref, *outs = refs[n_given + 9 : n_given + 13]
-        do, ds, dqs, *more = refs[n_given + 13 :]
+        rest_refs = refs[n_given + 9 : n_given + 9 + len(rest)]
+        refs = refs[n_given + 9 + len(rest) :]
+        near, far, first_out, row_out, *refs = refs
+        if opens:
+            sum_ref, *refs = refs
+        do, ds, dqs, held, *more = refs
         step = pl.program_id(0)
-        acc = outs[0] if opens else more[0]
-        sum_ref = outs[2]
+        acc = first_out if opens else more[0]
 
         @pl.when(step == 0)
         def _():
-            sum_ref[...] = jnp.zeros_like(sum_ref)
             if opens:
                 h_ref, dy_ref, *part_refs = given_refs
-                d0, d1, d2 = (r[...].astype(f32) for r in part_refs)
-                dn = d0 + d1 + d2
+                d0, d1 = (r[...].astype(f32) for r in part_refs[:2])
+                dn = d0 + d1 + jnp.concatenate([r[...] for r in part_refs[2:]], 0).astype(f32)
                 gain = gain_ref[1:2]
                 unit, scale = unit_of(h_ref[...])
                 along = dn * gain
                 inner = jnp.mean(along * unit, -1, keepdims=True)
                 dh = dy_ref[...].astype(f32) + scale * (along - unit * inner)
-                outs[1][...] = dh
+                row_out[...] = dh
                 do[...] = dh.astype(b16)
-                sum_ref[1:2] = jnp.sum(dn * unit, 0, keepdims=True)
+                sum_ref[...] = jnp.broadcast_to(jnp.sum(dn * unit, 0, keepdims=True), sum_ref.shape)
                 acc[...] = jnp.zeros_like(acc)
             else:
                 do[...] = given_refs[0][...].astype(b16)
@@ -246,15 +251,19 @@
         def stacked(two):
             return jnp.concatenate([jnp.where(low, two, zero), jnp.where(low, zero, two)], 0)
 
+        def cut_out(span, piece):
+            count = piece.shape[0]
+            held[:count] = piece
+            for s in range(parts if blocked else 2):
+                start = (me_ref[0] ^ s) * cut if blocked else s * lanes_out
+                lanes = pl.ds(pl.multiple_of(start, lanes_out), lanes_out)
+                (far if s % 2 else near)[s // 2, span] = held[:count, lanes]
+
         def weight_out(kind, left, right):
             value = dot(left, right, TN).astype(b16)
             for n in range(value.shape[0] // cols):
                 piece = value[n * cols : (n + 1) * cols]
-                if cut % 128 == 0:
-                    for s in range(parts):
-                        dw_ref[s, 0, kind + n] = piece[:, s * cut : (s + 1) * cut]
-                else:
-                    dw_ref[0, 0, kind + n] = piece
+                cut_out(pl.ds(pl.multiple_of((step * 4 + kind + n) * cols, 128), cols), piece)
 
         dc = dot(do[...], w_ref[0, 3], NN).astype(b16)
         weight_out(3, c_ref[...], do[...])
@@ -298,175 +307,172 @@
         if not opens:
             @pl.when(step == count - 1)
             def _():
-                dap_ref, dao_ref = outs[:2]
-                dap_ref[:PROMPT] = acc[:PROMPT].astype(b16)
+                first_out[:PROMPT] = acc[:PROMPT].astype(b16)
                 if padded > PROMPT:
-                    dap_ref[PROMPT:] = jnp.zeros((padded - PROMPT, width), b16)
-                dao_ref[...] = acc[PROMPT:]
+                    first_out[PROMPT:] = jnp.zeros((padded - PROMPT, width), b16)
+                row_out[...] = acc[PROMPT:]
                 total = jnp.sum(acc[...] * a_ref[...].astype(f32), 0, keepdims=True)
-                sum_ref[0:1] = total / gain_ref[0:1]
-
-    def by_group(i):
+                sums_ref, router_ref = rest_refs
+                rows_out = jnp.concatenate(
+                    [total / gain_ref[0:1], sums_ref[0:1], router_ref[...], jnp.zeros((SMALL_ROWS - 10, width), f32)], 0
+                )
+                cut_out(slice(count * 4 * cols, count * 4 * cols + SMALL_ROWS), rows_out.astype(b16))
+
+    def by_group(i, me):
         return (0, base + i)
 
     row_spec = pl.BlockSpec((rows, width), whole)
+    half_spec = pl.BlockSpec((rows // 2, width), whole)
     tall_spec = pl.BlockSpec((tall, width), whole)
-    places, lanes_out = (parts, cut) if cut % 128 == 0 else (1, width)
+    lines = count * 4 * cols + (0 if opens else SMALL_ROWS)
     if opens:
-        first_out, first_shape = tall_spec, jax.ShapeDtypeStruct((tall, width), f32)
+        first_spec, first_shape = tall_spec, jax.ShapeDtypeStruct((tall, width), f32)
     else:
-        first_out, first_shape = pl.BlockSpec((padded, width), whole), jax.ShapeDtypeStruct((padded, width), b16)
+        first_spec, first_shape = pl.BlockSpec((padded, width), whole), jax.ShapeDtypeStruct((padded, width), b16)
     return pl.pallas_call(
         body,
-        grid=(count,),
-        in_specs=([row_spec] * 5 if opens else [row_spec, tall_spec])
+        grid_spec=pltpu.PrefetchScalarGridSpec(
+            num_scalar_prefetch=1,
+            grid=(count,),
+        in_specs=([row_spec] * 4 + [half_spec] * 2 if opens else [row_spec, tall_spec])
         + [
             pl.BlockSpec(gains.shape, whole),
             tall_spec,
             pl.BlockSpec((rows, cols), by_group),
             pl.BlockSpec((tall, cols), by_group),
             pl.BlockSpec((tall, cols), by_group),
-            pl.BlockSpec((1, 2 * pairs * rows, keys), lambda i: (base + i, 0, 0)),
-            pl.BlockSpec((1, 2 * CONT, 128), lambda i: (base + i, 0, 0)),
+            pl.BlockSpec((1, 2 * pairs * rows, keys), lambda i, me: (base + i, 0, 0)),
+            pl.BlockSpec((1, 2 * CONT, 128), lambda i, me: (base + i, 0, 0)),
             pl.BlockSpec((rows, cols), by_group),
-            pl.BlockSpec((1, 4, width, cols), lambda i: (base + i, 0, 0, 0)),
-        ],
-        out_specs=[
-            pl.BlockSpec((places, 1, 4, cols, lanes_out), lambda i: (0, i, 0, 0, 0)),
-            first_out,
-            row_spec,
-            pl.BlockSpec((8, width), whole),
-        ],
+            pl.BlockSpec((1, 4, width, cols), lambda i, me: (base + i, 0, 0, 0)),
+        ]
+        + [pl.BlockSpec((8, width), whole)] * len(rest),
+        out_specs=[pl.BlockSpec((places, lines, lanes_out), lambda i, me: (0, 0, 0))] * 2
+        + [first_spec, row_spec]
+        + ([pl.BlockSpec((8, width), whole)] if opens else []),
         scratch_shapes=[
             pltpu.VMEM((rows, width), b16),
             pltpu.VMEM((2 * rows, PROMPT), b16),
             pltpu.VMEM((rows, cols), b16),
+            pltpu.VMEM((cols, width), b16),
         ]
         + ([] if opens else [pltpu.VMEM((tall, width), f32)]),
+        ),
         out_shape=[
-            jax.ShapeDtypeStruct((places, count, 4, cols, lanes_out), b16),
+            jax.ShapeDtypeStruct((places, lines, lanes_out), b16),
+            jax.ShapeDtypeStruct((places, lines, lanes_out), b16),
             first_shape,
             jax.ShapeDtypeStruct((rows, width), f32),
-            jax.ShapeDtypeStruct((8, width), f32),
-        ],
+        ]
+        + ([jax.ShapeDtypeStruct((8, width), f32)] if opens else []),
         compiler_params=params(60),
         cost_estimate=pl.CostEstimate(
             flops=count * (width * width * (2 * tall + 2 * rows) + 4 * rows * keys * width) // ESTIMATE,
             bytes_accessed=count * 20 * MIB // ESTIMATE,
             transcendentals=0,
         ),
-    )(*given, gains, a, q, k, v, p, inv, c, weights)
-
-
-def experts_blocks(blocks, given, keep, router, weights, start, own, experts, ends):
-    rows, width = given[0].shape
-    if not ends:
-        rows = 2 * rows
-    one = rows // 2
+    )(me, *given, gains, a, q, k, v, p, inv, c, weights, *rest)
+
+
+def experts_blocks(blocks, given, begun, place, keep, router, weights, start, own, experts, ends):
+    width, one = router.shape[0], given[0].shape[0] // (2 if ends else 1)
     units = weights.shape[1]
-    n_given = len(given)
+    n_given, n_begun = len(given), len(begun)
+    met = range(start // own, (start + units - 1) // own + 1)
 
     def body(blocks_ref, *refs):
         given_refs = refs[:n_given]
-        keep_a, keep_b, r_ref, wg_ref, wu_ref, wd_ref = refs[n_given : n_given + 6]
-        refs = refs[n_given + 6 :]
+        keep_ref, r_ref, wg_ref, wu_ref, wd_ref = refs[n_given + n_begun : n_given + n_begun + 5]
+        refs = refs[n_given + n_begun + 5 :]
+        b_v, dy_v, keep = given_refs[0][...], given_refs[1][...], keep_ref[...]
         if ends:
-            b_ref, dy_ref, y_in, db_in, dgates_in = given_refs
-            y0, y1, db0, db1, rg_ref, z_ref, dg_ref, du_ref = refs
+            y_ref, db_ref, rg_ref, z_ref, dg_ref, du_ref = refs
         else:
-            b_ref, dy_ref, y_acc, db_acc, dgates_ref, z_ref, dg_ref, du_ref = refs
+            b_ref, dy_ref, y_ref, db_ref, dgates_ref, z_ref, dg_ref, du_ref = refs
+            b_ref[...] = b_v
+            dy_ref[...] = dy_v
         lane = lax.broadcasted_iota(jnp.int32, (one, 128), 1)
         col = lax.broadcasted_iota(jnp.int32, (one, units), 1)
-        met = range(start // own, (start + units - 1) // own + 1)
-        for n in range(2):
-            span = slice(n * one, (n + 1) * one)
-            keep = (keep_a, keep_b)[n][...]
-            if ends:
-                b_v, dy_v = b_ref[span], dy_ref[span]
-            else:
-                b_v, dy_v = given_refs[n][...], given_refs[2 + n][...]
-                b_ref[span] = b_v
-                dy_ref[span] = dy_v
-            logits = dot(b_v, r_ref[...], NN)
-            live = lane < experts
-            top = jnp.max(jnp.where(live, logits, MASKED), -1, keepdims=True)
-            grown = jnp.exp(jnp.where(lane < 2 * experts, logits, MASKED) - top)
-            share = grown / jnp.sum(jnp.where(live, grown, 0.0), -1, keepdims=True)
-            gates = share.astype(b16).astype(f32) * keep
-
-            g = dot(b_v, wg_ref[0], NT)
-            u = dot(b_v, wu_ref[0], NT)
-            dz_plain = dot(dy_v, wd_ref[0], NT)
-            gate = gates[:, met[-1] : met[-1] + 1]
-            for expert in met[-2::-1]:
-                gate = jnp.where(col < (expert + 1) * own - start, gates[:, expert : expert + 1], gate)
-            cdf, pdf = normal(g)
-            act = g * cdf
-            z = (act * u).astype(b16).astype(f32)
-            along = dz_plain * z
-            dgates = dgates_in[span] if ends else jnp.zeros((one, 128), f32)
-            for expert in met:
-                low, high = max(expert * own - start, 0), min((expert + 1) * own - start, units)
-                inner_low, inner_high = -(-low // 128) * 128, high // 128 * 128
-                part = jnp.sum(along[:, inner_low:inner_high], -1, keepdims=True)
-                if low < inner_low:
-                    edge = along[:, inner_low - 128 : inner_low]
-                    part += jnp.sum(jnp.where(lane >= low % 128, edge, 0.0), -1, keepdims=True)
-                if inner_high < high:
-                    edge = along[:, inner_high : inner_high + 128]
-                    part += jnp.sum(jnp.where(lane < high % 128, edge, 0.0), -1, keepdims=True)
-                dgates += jnp.where(lane % experts == expert, part, 0.0)
-            dz = dz_plain * gate
-            dg = (dz * u * (cdf + g * pdf)).astype(b16)
-            du = (dz * act).astype(b16)
-            zg = (z * gate).astype(b16)
-            z_ref[span] = zg
-            dg_ref[span] = dg
-            du_ref[span] = du
-            y = dot(zg, wd_ref[0], NN)
-            db = dot(dg, wg_ref[0], NN) + dot(du, wu_ref[0], NN)
-            if not ends:
-                y_acc[span] = y
-                db_acc[span] = db
-                dgates_ref[span] = dgates
-            else:
-                dprob = dgates * keep
-                inner = jnp.sum(jnp.where(lane < experts, share * dprob, 0.0), -1, keepdims=True)
-                dl = jnp.where(lane < 2 * experts, share * (dprob - inner), 0.0)
-                head = dl.astype(b16).astype(f32)
-                split = jnp.where(lane < experts, head, dl - head).astype(b16)
-                if n == 0:
-                    rg_ref[...] = dot(b_v, split, TN)
-                else:
-                    rg_ref[...] += dot(b_v, split, TN)
-                (y0, y1)[n][...] = (y + y_in[span]).astype(b16)
-                (db0, db1)[n][...] = (db + db_in[span] + dot(split, r_ref[...], NT)).astype(b16)
+        logits = dot(b_v, r_ref[...], NN)
+        live = lane < experts
+        top = jnp.max(jnp.where(live, logits, MASKED), -1, keepdims=True)
+        grown = jnp.exp(jnp.where(lane < 2 * experts, logits, MASKED) - top)
+        share = grown / jnp.sum(jnp.where(live, grown, 0.0), -1, keepdims=True)
+        gates = share.astype(b16).astype(f32) * keep
+
+        g = dot(b_v, wg_ref[0], NT)
+        u = dot(b_v, wu_ref[0], NT)
+        dz_plain = dot(dy_v, wd_ref[0], NT)
+        gate = gates[:, met[-1] : met[-1] + 1]
+        for expert in met[-2::-1]:
+            gate = jnp.where(col < (expert + 1) * own - start, gates[:, expert : expert + 1], gate)
+        cdf, pdf = normal(g)
+        act = g * cdf
+        z = (act * u).astype(b16).astype(f32)
+        along = dz_plain * z
+        dgates = given_refs[4][...] if ends else jnp.zeros((one, 128), f32)
+        for expert in met:
+            low, high = max(expert * own - start, 0), min((expert + 1) * own - start, units)
+            inner_low, inner_high = -(-low // 128) * 128, high // 128 * 128
+            part = jnp.sum(along[:, inner_low:inner_high], -1, keepdims=True)
+            if low < inner_low:
+                edge = along[:, inner_low - 128 : inner_low]
+                part += jnp.sum(jnp.where(lane >= low % 128, edge, 0.0), -1, keepdims=True)
+            if inner_high < high:
+                edge = along[:, inner_high : inner_high + 128]
+                part += jnp.sum(jnp.where(lane < high % 128, edge, 0.0), -1, keepdims=True)
+            dgates += jnp.where(lane % experts == expert, part, 0.0)
+        dz = dz_plain * gate
+        dg = (dz * u * (cdf + g * pdf)).astype(b16)
+        du = (dz * act).astype(b16)
+        zg = (z * gate).astype(b16)
+        z_ref[...] = zg
+        dg_ref[...] = dg
+        du_ref[...] = du
+        y = dot(zg, wd_ref[0], NN)
+        db = dot(dg, wg_ref[0], NN) + dot(du, wu_ref[0], NN)
+        if not ends:
+            y_ref[...] = y
+            db_ref[...] = db
+            dgates_ref[...] = dgates
+        else:
+            dprob = dgates * keep
+            inner = jnp.sum(jnp.where(lane < experts, share * dprob, 0.0), -1, keepdims=True)
+            dl = jnp.where(lane < 2 * experts, share * (dprob - inner), 0.0)
+            head = dl.astype(b16).astype(f32)
+            split = jnp.where(lane < experts, head, dl - head).astype(b16)
+            rg_ref[0] = dot(b_v, split, TN)
+            y_ref[0] = (y + given_refs[2][...]).astype(b16)
+            db_ref[0] = (db + given_refs[3][...] + dot(split, r_ref[...], NT)).astype(b16)
 
     def weight(kind):
         return pl.BlockSpec((1, units, width), lambda i, at: (kind, 0, 0))
 
-    hidden = pl.BlockSpec((rows, units), whole)
-    one_spec = pl.BlockSpec((one, width), whole)
-    both_spec = pl.BlockSpec((rows, width), whole)
-    gate_spec = pl.BlockSpec((rows, 128), whole)
-    both = jax.ShapeDtypeStruct((rows, width), b16)
-    sums = jax.ShapeDtypeStruct((rows, width), f32)
+    def by_place(i, at):
+        return (i if ends else place, 0)
+
+    wide = pl.BlockSpec((one, width), by_place)
+    thin = pl.BlockSpec((one, 128), by_place)
+    hidden = pl.BlockSpec((one, units), by_place)
+    hidden_shape = jax.ShapeDtypeStruct((2 * one, units), b16)
     if ends:
-        outs = [(one_spec, jax.ShapeDtypeStruct((one, width), b16))] * 4
-        outs += [(pl.BlockSpec((width, 128), whole), jax.ShapeDtypeStruct((width, 128), f32))]
+        own_block = pl.BlockSpec((1, one, width), lambda i, at: (i, 0, 0))
+        outs = [(own_block, jax.ShapeDtypeStruct((2, one, width), b16))] * 2
+        outs += [(pl.BlockSpec((1, width, 128), lambda i, at: (i, 0, 0)), jax.ShapeDtypeStruct((2, width, 128), f32))]
     else:
-        outs = [(both_spec, both)] * 2 + [(both_spec, sums)] * 2
-        outs += [(gate_spec, jax.ShapeDtypeStruct((rows, 128), f32))]
-    outs += [(hidden, jax.ShapeDtypeStruct((rows, units), b16))] * 3
+        outs = [(wide, jax.ShapeDtypeStruct((2 * one, width), b16))] * 2
+        outs += [(wide, jax.ShapeDtypeStruct((2 * one, width), f32))] * 2
+        outs += [(thin, jax.ShapeDtypeStruct((2 * one, 128), f32))]
+    outs += [(hidden, hidden_shape)] * 3
     return pl.pallas_call(
         body,
         grid_spec=pltpu.PrefetchScalarGridSpec(
             num_scalar_prefetch=1,
-            grid=(1,),
-            in_specs=([both_spec] * 4 + [gate_spec] if ends else [one_spec] * 4)
+            grid=(2 if ends else 1,),
+            in_specs=([wide] * 4 + [thin] if ends else [pl.BlockSpec((one, width), whole)] * 2)
+            + [pl.BlockSpec(memory_space=pl.ANY)] * n_begun
             + [
-                pl.BlockSpec((one, 128), lambda i, at: (at[0], 0)),
-                pl.BlockSpec((one, 128), lambda i, at: (at[1], 0)),
+                pl.BlockSpec((one, 128), lambda i, at: (at[i], 0)),
                 pl.BlockSpec((width, 128), whole),
                 weight(0),
                 weight(1),
@@ -475,48 +481,32 @@
             out_specs=[spec for spec, _ in outs],
         ),
         out_shape=[shape for _, shape in outs],
+        input_output_aliases={1 + n_given + n: n for n in range(n_begun)},
         compiler_params=params(60),
         cost_estimate=pl.CostEstimate(
-            flops=(12 * rows * width * units) // ESTIMATE,
-            bytes_accessed=(6 * units * width + 6 * rows * units) // ESTIMATE,
-            transcendentals=2 * rows * units,
+            flops=(24 if ends else 12) * one * width * units // ESTIMATE,
+            bytes_accessed=(6 * units * width + 6 * one * units) // ESTIMATE,
+            transcendentals=2 * one * units,
         ),
-    )(blocks, *given, keep, keep, router, weights, weights, weights)
-
-
-def experts_weights(me, bs, dys, opened, closed, parts):
+    )(blocks, *given, *begun, keep, router, weights, weights, weights)
+
+
+def experts_weights(me, bs, dys, zs, dgs, dus, parts):
     pieces = len(bs)
     rows, width = bs[0].shape
-    first_units, last_units = opened[0][0].shape[1], closed[0][0].shape[1]
-    units = first_units + last_units
+    units = zs[0].shape[1]
     chunk = UNIT_CHUNK
-    turn = first_units // chunk
     cut = width // parts
     blocked = cut % 128 == 0
 
     def body(me_ref, *refs):
-        b_refs, dy_refs = refs[:pieces], refs[pieces : 2 * pieces]
-        begun = refs[2 * pieces : 5 * pieces]
-        ended = refs[5 * pieces : 8 * pieces]
-        near, far, held = refs[8 * pieces :]
-
-        def run(hidden):
-            for kind, right in enumerate((b_refs, b_refs, dy_refs)):
-                left = [hidden[n * 3 + (kind + 1) % 3] for n in range(pieces)]
-                value = dot(left[0][...], right[0][...], TN)
-                for n in range(1, pieces):
-                    value += dot(left[n][...], right[n][...], TN)
-                held[kind] = value.astype(b16)
-
-        @pl.when(pl.program_id(0) < turn)
-        def _():
-            run(begun)
-
-        @pl.when(pl.program_id(0) >= turn)
-        def _():
-            run(ended)
-
-        for kind in range(3):
+        b_refs, dy_refs, z, dg, du = (refs[n * pieces : (n + 1) * pieces] for n in range(5))
+        near, far, held = refs[5 * pieces :]
+        for kind, (left, right) in enumerate(((dg, b_refs), (du, b_refs), (z, dy_refs))):
+            value = dot(left[0][...], right[0][...], TN)
+            for n in range(1, pieces):
+                value += dot(left[n][...], right[n][...], TN)
+            held[kind] = value.astype(b16)
             for s in range(parts if blocked else 0):
                 lanes = pl.ds(pl.multiple_of((me_ref[0] ^ s) * cut, cut), cut)
                 (far if s % 2 else near)[s // 2, kind] = held[kind, :, lanes]
@@ -531,19 +521,18 @@
             num_scalar_prefetch=1,
             grid=(units // chunk,),
             in_specs=[pl.BlockSpec((rows, width), whole)] * (2 * pieces)
-            + [pl.BlockSpec((rows, chunk), lambda i, me: (0, jnp.minimum(i, turn - 1)))] * (3 * pieces)
-            + [pl.BlockSpec((rows, chunk), lambda i, me: (0, jnp.maximum(i - turn, 0)))] * (3 * pieces),
+            + [pl.BlockSpec((rows, chunk), lambda i, me: (0, i))] * (3 * pieces),
             out_specs=[pl.BlockSpec((places, 3, chunk, lanes), lambda i, me: (0, 0, i, 0))] * 2,
             scratch_shapes=[pltpu.VMEM((3, chunk, width), b16)],
         ),
         out_shape=[jax.ShapeDtypeStruct((places, 3, units, lanes), b16)] * 2,
         compiler_params=params(56),
         cost_estimate=pl.CostEstimate(
-            flops=6 * pieces * rows * width * units // ESTIMATE,
+            flops=(6 * pieces * rows * width * units) // ESTIMATE,
             bytes_accessed=(6 * units * width + 6 * pieces * rows * units) // ESTIMATE,
             transcendentals=0,
         ),
-    )(me, *bs, *dys, *(v for part in opened for v in part), *(v for part in closed for v in part))
+    )(me, *bs, *dys, *zs, *dgs, *dus)
 
 
 class Halving:
@@ -653,27 +642,30 @@
     dy1, dy2 = swap(dy0, 1), swap(dy0, 2)
     a, q, k, v, p, inv, c, h, b = attention_forward(at, (inputs, x1, x2, x3), gains, attention_w)
     b, dy1, dy2 = together((b, dy1, dy2))
-    b2 = swap(b, 2)
-    bs = (b, swap(b, 1), b2, swap(b2, 1))
-    dys = (dy0, dy1, dy2, swap(dy2, 1))
-
-    def run(pair, half, given):
+    b1, b2 = swap(b, 1), swap(b, 2)
+    bs, dys = [b], [dy0]
+
+    def open_block(slot, begun):
+        block = jnp.full((1,), own ^ slot, jnp.int32)
+        return experts_blocks(block, (bs[slot], dys[slot]), begun, slot % 2, keep, router_wide, halves[0], 0, own_units, experts, False)
+
+    def close_pair(pair, given):
         blocks = jnp.stack([own ^ (2 * pair), own ^ (2 * pair + 1)]).astype(jnp.int32)
-        return experts_blocks(blocks, given, keep, router_wide, halves[half], half * middle, own_units, experts, half == 1)
-
-    opened_0 = run(0, 0, (bs[0], bs[1], dys[0], dys[1]))
-    second, opened_0 = together(((bs[2], bs[3], dys[2], dys[3]), opened_0))
-    opened_1 = run(1, 0, second)
-    closed_1 = run(1, 1, opened_1[:5])
+        return experts_blocks(blocks, given, (), 0, keep, router_wide, halves[1], middle, own_units, experts, True)
+
+    opened_0 = open_block(0, ())
+    opened_0, b2 = together((opened_0, b2))
+    bs += [b1, b2, swap(b2, 1)]
+    dys += [dy1, dy2, swap(dy2, 1)]
+    opened_0 = open_block(1, opened_0)
+    opened_1 = open_block(3, open_block(2, ()))
+    opened_0, opened_1 = together((opened_0, opened_1))
+    closed_1 = close_pair(1, opened_1[:5])
     opened_0, closed_1 = together((opened_0, closed_1))
-    near3 = swap(closed_1[3], 1)
-    closed_0 = run(0, 1, opened_0[:5])
+    near3 = swap(closed_1[1][1], 1)
+    closed_0 = close_pair(0, opened_0[:5])
     closed_0, near3 = together((closed_0, near3))
     joined = [opened_0[0], opened_1[0]], [opened_0[1], opened_1[1]]
-    d1, d2 = closed_0[3], closed_1[2] + near3
-    d1, d2, joined = together((d1, d2, joined))
-    near, far = experts_weights(here, *joined, (opened_0[5:], opened_1[5:]), (closed_0[5:], closed_1[5:]), dp)
-    d1, d2, near, far = together((swap(d1, 1), swap(d2, 2), near, far))
     blocked = cut % 128 == 0
 
     def stage(sends, given=(), work=None):
@@ -681,32 +673,68 @@
         got = tuple(swap(value, *how) if how else lax.ppermute(value, "tensor", down) for value, (_, *how) in zip(values, sends))
         return together((got, work(given) if work else given))
 
-    def backward(base):
-        return lambda given: attention_backward(base, 2, given, gains, a, q, k, v, p, inv, c, attention_w, dp)
-
-    def summed(dw):
-        if blocked:
-            return lax.psum_scatter(dw, "dp", scatter_dimension=0, tiled=True)[0]
-        return lax.psum_scatter(dw[0], "dp", scatter_dimension=3, tiled=True)
-
-    sends = [(far, 1, "dp")] if blocked else []
-    given = (h, cotangent, closed_0[2], d1, d2)
-    got, opened = stage(sends + [(closed_1[1], 1)], given, backward(0))
-    heads_0 = summed(opened[0])
-    y2 = closed_1[0] + got[-1]
-    halvings = []
-    if blocked:
-        lines = 3 * units
-        near = near.reshape(dp // 2, lines, cut)
-        other = got[0].reshape(dp // 2, lines, cut)
-        halvings = [Halving(near, other, 0, lines // 2), Halving(near, other, lines // 2, lines)]
-    sends = halvings[0].sends() if blocked else []
-    got, closed = stage(sends + [(closed_0[1], 1), (y2, 2)], (opened[2], opened[1]), backward(2))
-    y1, y2 = got[-2:]
-    if blocked:
-        halvings[0].take(got[:2])
-    heads_1 = summed(closed[0])
-    dap, dao, dh = closed[1], closed[2], opened[2]
+    def joint(*halvings):
+        lists = {}
+        for halving in halvings:
+            if halving is not None and halving.orders[0]:
+                for path, (value, *how) in enumerate(halving.sends()):
+                    lists.setdefault(tuple(how), []).append((halving, path, value))
+        sends = [(jnp.concatenate([value for *_, value in items], 0), *how) for how, items in lists.items()]
+
+        def take(got):
+            came = {}
+            for whole_value, items in zip(got, lists.values()):
+                start = 0
+                for halving, path, value in items:
+                    came.setdefault(id(halving), (halving, {}))[1][path] = whole_value[start : start + value.shape[0]]
+                    start += value.shape[0]
+            for halving, paths in came.values():
+                halving.take([paths[0], paths[1]])
+
+        return sends, take
+
+    def flat(value):
+        return value.reshape(value.shape[0], -1, value.shape[-1])
+
+    def weights_of(units):
+        hidden = (opened_0[5:], opened_1[5:]) if units == 0 else (closed_0[3:], closed_1[3:])
+        return lambda given: [flat(v) for v in experts_weights(here, *given, *zip(*hidden), dp)]
+
+    def core_send(far):
+        return [(far, 1, "dp")] if blocked else []
+
+    def halving_of(near, got):
+        return Halving(near, got[0], 0, near.shape[1]) if blocked else None
+
+    d2 = closed_1[1][0] + near3
+    half = rows // 2
+    got, (near_0, far_0) = stage([(d2[:half], 2), (closed_1[0][1], 1)], joined, weights_of(0))
+    d2_low, near3 = got
+    y2 = closed_1[0][0] + near3
+    sends = core_send(far_0)
+    got, (near_1, far_1) = stage([(closed_0[1][1], 1), (d2[half:], 2)] + sends, joined, weights_of(1))
+    d1, d2_high = got[:2]
+    units_0 = halving_of(near_0, got[2:])
+
+    rg = (closed_0[2] + closed_1[2]).sum(0)
+    rg = (rg[:, :experts] + rg[:, experts : 2 * experts]).T
+    rg = jnp.concatenate([rg, jnp.zeros((8 - experts, width), f32)], 0)
+
+    def backward(base, rest):
+        return lambda given: attention_backward(here, base, 2, given, rest, gains, a, q, k, v, p, inv, c, attention_w, dp)
+
+    given = (h, cotangent, closed_0[1][0], d1, d2_low, d2_high)
+    sends, take = joint(units_0)
+    got, opened = stage([(closed_0[0][1], 1)] + core_send(far_1) + sends, given, backward(0, ()))
+    y1 = got[0]
+    units_1 = halving_of(near_1, got[1:])
+    take(got[2:])
+    sends, take = joint(units_1, units_0)
+    got, closed = stage([(y2, 2)] + core_send(opened[1]) + sends, (opened[3], opened[2]), backward(2, (opened[4], rg)))
+    y2 = got[0]
+    heads_0 = halving_of(opened[0], got[1:])
+    take(got[2:])
+    dap, dao, dh = closed[2], closed[3], opened[3]
 
     def chunk_of(index):
         start = jnp.clip(index, 0, dap.shape[0] // rows - 1) * rows
@@ -714,40 +742,51 @@
         valid = (index >= 0) & (index < dap.shape[0] // rows)
         return jnp.where(valid, piece, jnp.zeros((), b16))
 
-    rg = closed_0[4] + closed_1[4]
-    rg = (rg[:, :experts] + rg[:, experts : 2 * experts]).T
-    small_grad = jnp.concatenate([opened[3][:2] + closed[3][:2], rg], 0)
-    sends = halvings[1].sends() if blocked else []
-    got, small_grad = stage([(chunk_of(own - depth + 1),)] + sends, small_grad, lambda v: lax.psum(v, "tensor"))
+    sends, take = joint(units_1, heads_0)
+    got, _ = stage([(chunk_of(own - depth + 1),)] + core_send(closed[1]) + sends)
     sent = got[0]
+    heads_1 = halving_of(closed[0], got[1:])
+    take(got[2:])
+    sends, take = joint(heads_1, heads_0)
+    got, _ = stage([(chunk_of(own - depth + 2) + sent,)] + sends)
+    sent = got[0]
+    take(got[1:])
+    sends, take = joint(heads_1)
+    got, _ = stage([(chunk_of(own - depth + 3) + sent,)] + sends)
+    sent = got[0]
+    take(got[1:])
     if blocked:
-        halvings[1].take(got[1:])
-    pairs = [halving.sends() for halving in halvings if halving.orders[0]]
-    sends = [(jnp.concatenate([one[0], two[0]], 0), *one[1:]) for one, two in zip(*pairs)] if pairs else []
-    got, small_grad = stage([(chunk_of(own - depth + 2) + sent,)] + sends, small_grad, lambda v: lax.psum(v, "dp"))
-    sent = got[0]
-    if sends:
-        for n, halving in enumerate(halvings):
-            halving.take([came[n * came.shape[0] // 2 : (n + 1) * came.shape[0] // 2] for came in got[1:]])
-    sent = lax.ppermute(chunk_of(own - depth + 3) + sent, "tensor", down)
-    for halving in halvings:
-        while halving.orders[0]:
-            halving.take([swap(*send) for send in halving.sends()])
-
-    slots = jnp.concatenate([heads_0, heads_1], 0)
-    total = slots[0].astype(f32)
+        for halving in (units_0, units_1, heads_0, heads_1):
+            while halving.orders[0]:
+                halving.take([swap(*send) for send in halving.sends()])
+        heads_0, heads_1 = heads_0.result(), heads_1.result()
+        total_units = jnp.concatenate([part.result().reshape(3, -1, cut) for part in (units_0, units_1)], 1)
+    else:
+        def summed(near, far):
+            return lax.psum_scatter(jnp.concatenate([near[0], far[0]], -1), "dp", scatter_dimension=1, tiled=True)
+
+        heads_0, heads_1 = summed(*opened[:2]), summed(*closed[:2])
+        total_units = [summed(*pair).reshape(3, -1, cut) for pair in ((near_0, far_0), (near_1, far_1))]
+        total_units = jnp.concatenate(total_units, 1).astype(f32)
+
+    cols = attention_w.shape[-1]
+    lines = 4 * cols
+    count = width // (dp * depth)
+
+    def slot_of(s):
+        head = (heads_0, heads_1)[s // 2][s % 2 * lines : (s % 2 + 1) * lines]
+        share = lax.dynamic_slice_in_dim(heads_1[2 * lines :], (own ^ s) * count, count, 1)
+        share = jnp.pad(share, ((0, 0), (0, head.shape[1] - count)))
+        return jnp.concatenate([head, share], 0)
+
+    total = slot_of(0).astype(f32)
     for s in range(1, depth):
-        total = total + swap(slots[s], s).astype(f32)
-    count = width // (dp * depth)
-    small_grad = lax.dynamic_slice_in_dim(small_grad, (me * depth + own) * count, count, 1)
+        total = total + swap(slot_of(s).astype(b16), s).astype(f32)
+    small_grad = total[lines : lines + 2 + experts, :count]
+    total = total[:lines].reshape(4, cols, -1)
     input_grad = input_gradient(dh, dao, chunk_of(own), sent, inputs, gains)
-    output = h + closed_0[0].astype(f32) + y1.astype(f32) + y2.astype(f32)
-
-    if blocked:
-        total_units = jnp.concatenate([halving.result() for halving in halvings], 0).reshape(3, units, cut)
-    else:
-        pieces = jnp.concatenate([near[0], far[0]], -1)
-        total_units = lax.psum_scatter(pieces, "dp", scatter_dimension=2, tiled=True).astype(f32)
+    output = h + closed_0[0][0].astype(f32) + y1.astype(f32) + y2.astype(f32)
+
     wg_grad, wu_grad, wd_grad = (total_units[n].reshape(experts, own_units, cut) for n in range(3))
     return (
         output.astype(b16),

time: 561 us -> 531 us (0.947)
  blocking collectives: 78.7 us -> 0 us
  starting transfers between devices: 59.9 us -> 78.2 us
  waiting for transfers between devices: 105 us -> 123 us
  Pallas kernels: 235 us -> 242 us
    psum x2 -> x0, blocking collectives: 78.7 us -> none  [the longest x1 51.7 us: on_device(): lax.psum(v, 'dp')]
    ppermute x2 -> x3, waiting for transfers between devices: 0.01 us -> 40.2 us  [stage(): lax.ppermute(value, 'tensor', down)]
    ppermute x30 -> x38, starting transfers between devices: 42.5 us -> 60.2 us  [swap(): return lax.ppermute(value, axis, [(i, i ^ bits) for i in range(size)])]
    ppermute x30 -> x38, waiting for transfers between devices: 85.7 us -> 70.1 us  [swap(): return lax.ppermute(value, axis, [(i, i ^ bits) for i in range(size)])]
    ppermute x1 -> x0, waiting for transfers between devices: 12.8 us -> none  [on_device(): sent = lax.ppermute(chunk_of(own - depth + 3) + sent, 'tensor', down)]
    add x7 -> x5, other arithmetic: 9.27 us -> 1.97 us  [the longest x1 0.96 us: on_device(): y2 = closed_1[0][0] + near3]
    pallas_call x1 -> x2, Pallas kernels: 40.3 us -> 43.8 us  [experts_weights(): pl.pallas_call(body, grid_spec=pltpu.PrefetchScalarGridSpec(num_scalar_pr...]
    pallas_call x4 -> x6, Pallas kernels: 100 us -> 103 us  [experts_blocks(): pl.pallas_call(body, grid_spec=pltpu.PrefetchScalarGridSpec(num_scalar_pr...]
  transfers between devices with their start and end apart: 41 -> 47, of which waited for: 15 -> 23; matrix products, arithmetic and copies ran while one was open for 8% -> 5% of each run, Pallas kernels for 38% -> 42%
where the time goes in v3:
time: 531 us; the launch traced here: 522 us
  Pallas kernels  242 us (46%)
  waiting for transfers between devices  123 us (23%)
  starting transfers between devices  78.2 us (15%)
  other arithmetic  44.8 us (8%)
  local copies, waits for them, and re-layouts  19.3 us (4%)
  between operations  14.8 us (3%)
    pallas_call x6, Pallas kernels, experts_blocks(): pl.pallas_call(body, grid_spec=pltpu.PrefetchScalarGridSpec(num_scalar_pr...  103 us
    ppermute x38, waiting for transfers between devices, swap(): return lax.ppermute(value, axis, [(i, i ^ bits) for i in range(size)])  70.1 us
    ppermute x38, starting transfers between devices, swap(): return lax.ppermute(value, axis, [(i, i ^ bits) for i in range(size)])  60.2 us
    pallas_call x2, Pallas kernels, attention_backward(): pl.pallas_call(body, grid_spec=pltpu.PrefetchScalarGridSpec(num_scalar_pr...  59 us
    pallas_call x2, Pallas kernels, experts_weights(): pl.pallas_call(body, grid_spec=pltpu.PrefetchScalarGridSpec(num_scalar_pr...  43.8 us
    ppermute x3, waiting for transfers between devices, stage(): lax.ppermute(value, 'tensor', down)  40.2 us
    pallas_call x1, Pallas kernels, attention_forward(): pl.pallas_call(body, grid_spec=pltpu.PrefetchScalarGridSpec(num_scalar_pr...  32.3 us
    ppermute x3, starting transfers between devices, raised(): return lax.ppermute(value, 'tensor', up)  13.3 us
  transfers between devices with their start and end apart: 47, of which 23 were waited for; matrix products, arithmetic and copies ran while one was open for 5% of the time, Pallas kernels for 42%

profile of v3, /device:TPU:0, one launch (start us, length us, event | category | flops | bytes accessed | tf_op | source)
XLA Modules:
  0.0 522.2 jit_solution(9606663413453781935)
XLA Ops:
  9.2 4.1 collective-permute-start.9
  14.8 10.5 %collective-permute-done.9 = bf16[4,128,256]{2,1,0:T(8,128)(2,1)S(1)} collective-permute-done((bf16[4,128,256]{2,1,0:T(8,128)(2,1)S(1)}, bf16[4,128,256]{2,1,0:T(8,128)(2,1)S(1)}, u32[]{:S(2)}, u32[]{:S(2)}) %collective-permute-start.9) | collective-permute-done | bytes 262176 | tf_op jit(solution)/shard_map/ppermute | solution.py:603
  25.9 6.8 %collective-permute-done.10 = bf16[4,128,256]{2,1,0:T(8,128)(2,1)S(1)} collective-permute-done((bf16[4,128,256]{2,1,0:T(8,128)(2,1)S(1)}, bf16[4,128,256]{2,1,0:T(8,128)(2,1)S(1)}, u32[]{:S(2)}, u32[]{:S(2)}) %collective-permute-start.10) | collective-permute-done | bytes 262176 | tf_op jit(solution)/shard_map/ppermute | solution.py:603
  36.5 3.4 collective-permute-start
  50.7 5.4 %collective-permute-done.4 = bf16[8,256]{1,0:T(8,128)(2,1)S(1)} collective-permute-done((bf16[8,256]{1,0:T(8,128)(2,1)S(1)}, bf16[8,256]{1,0:T(8,128)(2,1)S(1)}, u32[]{:S(2)}, u32[]{:S(2)}) %collective-permute-start.4) | collective-permute-done | bytes 4128 | tf_op jit(solution)/shard_map/ppermute | solution.py:603
  56.1 4.4 collective-permute-start.5
  60.5 3.4 collective-permute-start.6
  63.9 12.2 %collective-permute-done.6 = bf16[8,512]{1,0:T(8,128)(2,1)S(1)} collective-permute-done((bf16[8,512]{1,0:T(8,128)(2,1)S(1)}, bf16[8,512]{1,0:T(8,128)(2,1)S(1)}, u32[]{:S(2)}, u32[]{:S(2)}) %collective-permute-start.6) | collective-permute-done | bytes 8224 | tf_op jit(solution)/shard_map/ppermute | solution.py:603
  76.1 5.6 %collective-permute-start.7 = (bf16[384,1024]{1,0:T(8,128)(2,1)S(1)}, bf16[384,1024]{1,0:T(8,128)(2,1)}, u32[]{:S(2)}, u32[]{:S(2)}) collective-permute-start(bf16[384,1024]{1,0:T(8,128)(2,1)S(1)} %collective-permute-done.5.x2), channel_id=1, source_target_pairs={{0,1},{1,2},{2,3},{4,5},{5,6},{6,7},{8,9},{9,10},{10,11},{12,13},{... | collective-permute-start | bytes 2359304 | tf_op jit(solution)/shard_map/ppermute | solution.py:606
  89.0 6.9 %collective-permute-done.7.x3 = bf16[384,1024]{1,0:T(8,128)(2,1)} collective-permute-done((bf16[384,1024]{1,0:T(8,128)(2,1)S(1)}, bf16[384,1024]{1,0:T(8,128)(2,1)}, u32[]{:S(2)}, u32[]{:S(2)}) %collective-permute-start.7) | collective-permute-done | bytes 786464 | tf_op jit(solution)/shard_map/ppermute | solution.py:606
  98.4 3.4 collective-permute-start.12
  101.8 32.3 %shard_map.230 = (bf16[1408,1024]{1,0:T(8,128)(2,1)}, bf16[384,1024]{1,0:T(8,128)(2,1)}, bf16[1408,1024]{1,0:T(8,128)(2,1)}, bf16[1408,1024]{1,0:T(8,128)(2,1)},...) custom-call(s32[1]{0:T(128)} %bitcast.at_ref.blocks_ref, ...), custom_call_target="tpu_custom_call" | custom-call | flops 2785017856 | bytes 15728640 | tf_op jit(solution)/shard_map/pallas_call | solution.py:160
  134.7 13.2 %collective-permute-start.13 = (bf16[384,1024]{1,0:T(8,128)(2,1)}, bf16[384,1024]{1,0:T(8,128)(2,1)}, u32[]{:S(2)}, u32[]{:S(2)}) collective-permute-start(bf16[384,1024]{1,0:T(8,128)(2,1)} %get-tuple-element.220.refs_0_), channel_id=1, source_target_pairs={{0,1},{1,0},{2,3},{3,2},{4,5},{5,4},{6,7},{7,6},{8,9},{9,8},{10,11... | collective-permute-start | bytes 2359304 | tf_op jit(solution)/shard_map/ppermute | solution.py:603
  147.9 5.4 %all-gather.6.cloned.1.call-done.refs_4_.refs_5_.refs_6_.refs_12_.refs_13_.refs_14_ = bf16[3,1536,1024]{2,1,0:T(8,128)(2,1)} async-done(((bf16[3,1536,128]{2,1,0:T(8,128)(2,1)}), bf16[3,1536,1024]{2,1,0:T(8,128)(2,1)}) %all-gather.6.cloned.1.call-update) | async-done | bytes 9437200 | tf_op jit(solution)/shard_map/all_gather | solution.py:637
  153.4 14.1 %shard_map.231 = (bf16[768,1024]{1,0:T(8,128)(2,1)}, bf16[768,1024]{1,0:T(8,128)(2,1)}, f32[768,1024]{1,0:T(8,128)}, f32[768,1024]{1,0:T(8,128)}, f32[768,128]{1...) custom-call(s32[1]{0:T(128)} %bitcast.at_ref.blocks_ref, ...), custom_call_target="tpu_custom_call" | custom-call | flops 1811939328 | bytes 3244032 | tf_op jit(solution)/shard_map/pallas_call | solution.py:467
  169.7 14.3 %shard_map.233 = (bf16[768,1024]{1,0:T(8,128)(2,1)}, bf16[768,1024]{1,0:T(8,128)(2,1)}, f32[768,1024]{1,0:T(8,128)}, f32[768,1024]{1,0:T(8,128)}, f32[768,128]{1...) custom-call(s32[1]{0:T(128)} %bitcast.25.blocks_ref, ...), custom_call_target="tpu_custom_call" | custom-call | flops 1811939328 | bytes 3244032 | tf_op jit(solution)/shard_map/pallas_call | solution.py:467
  184.0 14.5 %shard_map.232 = (bf16[768,1024]{1,0:T(8,128)(2,1)}, bf16[768,1024]{1,0:T(8,128)(2,1)}, f32[768,1024]{1,0:T(8,128)}, f32[768,1024]{1,0:T(8,128)}, f32[768,128]{1...) custom-call(s32[1]{0:T(128)} %bitcast.18.blocks_ref, ...), custom_call_target="tpu_custom_call", output_to_operand_aliasing={{0}: (3, {}), {1}: (4, {}), {2}: (5, {}), {3}: (6, {}), {4}... | custom-call | flops 1811939328 | bytes 3244032 | tf_op jit(solution)/shard_map/pallas_call | solution.py:467
  201.3 14.5 %shard_map.234 = (bf16[768,1024]{1,0:T(8,128)(2,1)}, bf16[768,1024]{1,0:T(8,128)(2,1)}, f32[768,1024]{1,0:T(8,128)}, f32[768,1024]{1,0:T(8,128)}, f32[768,128]{1...) custom-call(s32[1]{0:T(128)} %bitcast.24.blocks_ref, ...), custom_call_target="tpu_custom_call", output_to_operand_aliasing={{0}: (3, {}), {1}: (4, {}), {2}: (5, {}), {3}: (6, {}), {4}... | custom-call | flops 1811939328 | bytes 3244032 | tf_op jit(solution)/shard_map/pallas_call | solution.py:467
  215.8 22.9 %shard_map.235 = (bf16[2,384,1024]{2,1,0:T(8,128)(2,1)}, bf16[2,384,1024]{2,1,0:T(8,128)(2,1)}, f32[2,1024,128]{2,1,0:T(8,128)}, bf16[768,1280]{1,0:T(8,128)(2,1...) custom-call(s32[2]{0:T(128)} %pad_add_fusion.1.blocks_ref, ...), custom_call_target="tpu_custom_call" | custom-call | flops 3019898880 | bytes 2703360 | tf_op jit(solution)/shard_map/pallas_call | solution.py:467
  240.8 23.2 %shard_map.236 = (bf16[2,384,1024]{2,1,0:T(8,128)(2,1)}, bf16[2,384,1024]{2,1,0:T(8,128)(2,1)}, f32[2,1024,128]{2,1,0:T(8,128)}, bf16[768,1280]{1,0:T(8,128)(2,1...) custom-call(s32[2]{0:T(128)} %pad_add_fusion.blocks_ref, bf16[768,1024]{1,0:T(8,128)(2,1)} %get-tuple-element.319.refs_0_, ...), custom_call_target="tpu_custom_call" | custom-call | flops 3019898880 | bytes 2703360 | tf_op jit(solution)/shard_map/pallas_call | solution.py:467
  268.5 23.2 %shard_map.237 = (bf16[4,3,1536,128]{3,2,1,0:T(8,128)(2,1)}, bf16[4,3,1536,128]{3,2,1,0:T(8,128)(2,1)}) custom-call(s32[1]{0:T(128)} %bitcast.32.me_ref, bf16[768,1024]{1,0:T(8,128)(2,1)} %get-tuple-element.319.refs_0_, bf16[768,1024]{1,0:T(8,128)(2,1)} %get-tuple-element.320.refs_0_.refs_1_, bf16[768,1024]{1,0:T(8,128)(2,1)} %get-tuple-element.321.refs_1_.refs_2_, ...), custom_call_target="tpu_custom_call" | custom-call | flops 3623878656 | bytes 5898240 | tf_op jit(solution)/shard_map/pallas_call | solution.py:518
  295.6 20.6 %shard_map.238 = (bf16[4,3,1280,128]{3,2,1,0:T(8,128)(2,1)}, bf16[4,3,1280,128]{3,2,1,0:T(8,128)(2,1)}) custom-call(s32[1]{0:T(128)} %bitcast.32.me_ref, bf16[768,1024]{1,0:T(8,128)(2,1)} %get-tuple-element.319.refs_0_, bf16[768,1024]{1,0:T(8,128)(2,1)} %get-tuple-element.320.refs_0_.refs_1_, bf16[768,1024]{1,0:T(8,128)(2,1)} %get-tuple-element.321.refs_1_.refs_2_, ...), custom_call_target="tpu_custom_call" | custom-call | flops 3019898880 | bytes 4915200 | tf_op jit(solution)/shard_map/pallas_call | solution.py:518
  316.2 3.4 collective-permute-done.21.refs_5_
  330.0 28.8 %shard_map.239 = (bf16[4,2048,128]{2,1,0:T(8,128)(2,1)}, bf16[4,2048,128]{2,1,0:T(8,128)(2,1)}, f32[1408,1024]{1,0:T(8,128)}, f32[384,1024]{1,0:T(8,128)}, f32[8,1024]{1,0:T(8,128)}) custom-call(s32[1]{0:T(128)} %bitcast.32.me_ref, f32[384,1024]{1,0:T(8,128)} %get-tuple-element.341.refs_0_, bf16[384,1024]{1,0:T(8,128)(2,1)} %refs_1_.1, ...), custom_call_target="tpu_custom_call" | custom-call | flops 2785017856 | bytes 10485760 | tf_op jit(solution)/shard_map/pallas_call | solution.py:332
  358.9 3.9 fusion.7
  371.5 30.2 %shard_map.240 = (bf16[4,2080,128]{2,1,0:T(8,128)(2,1)}, bf16[4,2080,128]{2,1,0:T(8,128)(2,1)}, bf16[1152,1024]{1,0:T(8,128)(2,1)}, f32[384,1024]{1,0:T(8,128)}) custom-call(s32[1]{0:T(128)} %bitcast.32.me_ref, f32[384,1024]{1,0:T(8,128)} %get-tuple-element.372.refs_0_.dh_ref, f32[1408,1024]{1,0:T(8,128)} %get-tuple-element.373.refs_1_, ...), custom_call_target="tpu_custom_call" | custom-call | flops 2785017856 | bytes 10485760 | tf_op jit(solution)/shard_map/pallas_call | solution.py:332
  401.7 3.4 collective-permute-done.27
  420.0 17.0 %collective-permute-done.31 = bf16[384,1024]{1,0:T(8,128)(2,1)S(1)} collective-permute-done((bf16[384,1024]{1,0:T(8,128)(2,1)}, bf16[384,1024]{1,0:T(8,128)(2,1)S(1)}, u32[]{:S(2)}, u32[]{:S(2)}) %collective-permute-start.31) | collective-permute-done | bytes 786464 | tf_op jit(solution)/shard_map/ppermute | solution.py:673
  448.8 14.3 %collective-permute-done.35 = bf16[384,1024]{1,0:T(8,128)(2,1)S(1)} collective-permute-done((bf16[384,1024]{1,0:T(8,128)(2,1)S(1)}, bf16[384,1024]{1,0:T(8,128)(2,1)S(1)}, u32[]{:S(2)}, u32[]{:S(2)}) %collective-permute-start.35) | collective-permute-done | bytes 786464 | tf_op jit(solution)/shard_map/ppermute | solution.py:673
  472.5 3.9 collective-permute-done.39
  476.9 8.9 %collective-permute-done.38.sent_ref = bf16[384,1024]{1,0:T(8,128)(2,1)S(1)} collective-permute-done((bf16[384,1024]{1,0:T(8,128)(2,1)S(1)}, bf16[384,1024]{1,0:T(8,128)(2,1)S(1)}, u32[]{:S(2)}, u32[]{:S(2)}) %collective-permute-start.38) | collective-permute-done | bytes 786464 | tf_op jit(solution)/shard_map/ppermute | solution.py:673
  498.5 12.7 %collective-permute-done.42 = bf16[1056,128]{1,0:T(8,128)(2,1)S(1)} collective-permute-done((bf16[1056,128]{1,0:T(8,128)(2,1)S(1)}, bf16[1056,128]{1,0:T(8,128)(2,1)S(1)}, u32[]{:S(2)}, u32[]{:S(2)}) %collective-permute-start.42) | collective-permute-done | bytes 270368 | tf_op jit(solution)/shard_map/ppermute | solution.py:603
  (250 shorter events, 116.6 us)
Async XLA Ops:
  7.2 94.7 %all-gather.4.cloned.1.call-start = ((), (), s32[]{:S(2)}) async-start(), calls=%async_computation | async-start | bytes 9437184 | tf_op jit(solution)/shard_map/all_gather | solution.py:611
  33.8 119.5 %all-gather.6.cloned.1.call-start = ((), (), s32[]{:S(2)}) async-start(), calls=%async_computation.1 | async-start | bytes 10616832 | tf_op jit(solution)/shard_map/all_gather | solution.py:637
  35.3 180.4 %all-gather.8.cloned.1.call-start = ((), (), s32[]{:S(2)}) async-start(), calls=%async_computation.2 | async-start | bytes 8847360 | tf_op jit(solution)/shard_map/all_gather | solution.py:637
  56.1 20.0 %collective-permute-start.5 = (bf16[384,1024]{1,0:T(8,128)(2,1)S(1)}, bf16[384,1024]{1,0:T(8,128)(2,1)S(1)}, u32[]{:S(2)}, u32[]{:S(2)}) collective-permute-start(bf16[384,1024]{1,0:T(8,128)(2,1)S(1)} %collective-permute-done.x1), channel_id=1, source_target_pairs={{0,1},{1,2},{2,3},{4,5},{5,6},{6,7},{8,9},{9,10},{10,11},{12,13},{... | collective-permute-start | bytes 2359304 | tf_op jit(solution)/shard_map/ppermute | solution.py:606
  95.9 38.3 %collective-permute-start.11 = (bf16[384,1024]{1,0:T(8,128)(2,1)S(1)}, bf16[384,1024]{1,0:T(8,128)(2,1)S(1)}, u32[]{:S(2)}, u32[]{:S(2)}) collective-permute-start(bf16[384,1024]{1,0:T(8,128)(2,1)S(1)} %copy-done.11), channel_id=1, source_target_pairs={{0,1},{1,0},{2,3},{3,2},{4,5},{5,4},{6,7},{7,6},{8,9},{9,8},{10,11... | collective-permute-start | bytes 2359304 | tf_op jit(solution)/shard_map/ppermute | solution.py:603
  98.4 35.8 %collective-permute-start.12 = (bf16[384,1024]{1,0:T(8,128)(2,1)S(1)}, bf16[384,1024]{1,0:T(8,128)(2,1)S(1)}, u32[]{:S(2)}, u32[]{:S(2)}) collective-permute-start(bf16[384,1024]{1,0:T(8,128)(2,1)S(1)} %copy-done.11), channel_id=1, source_target_pairs={{0,2},{1,3},{2,0},{3,1},{4,6},{5,7},{6,4},{7,5},{8,10},{9,11},{10,... | collective-permute-start | bytes 2359304 | tf_op jit(solution)/shard_map/ppermute | solution.py:603
  134.2 33.3 %collective-permute-start.14 = (bf16[384,1024]{1,0:T(8,128)(2,1)}, bf16[384,1024]{1,0:T(8,128)(2,1)S(1)}, u32[]{:S(2)}, u32[]{:S(2)}) collective-permute-start(bf16[384,1024]{1,0:T(8,128)(2,1)} %get-tuple-element.220.refs_0_), channel_id=1, source_target_pairs={{0,2},{1,3},{2,0},{3,1},{4,6},{5,7},{6,4},{7,5},{8,10},{9,11},{10,... | collective-permute-start | bytes 2359304 | tf_op jit(solution)/shard_map/ppermute | solution.py:603
  134.7 49.3 %collective-permute-start.13 = (bf16[384,1024]{1,0:T(8,128)(2,1)}, bf16[384,1024]{1,0:T(8,128)(2,1)}, u32[]{:S(2)}, u32[]{:S(2)}) collective-permute-start(bf16[384,1024]{1,0:T(8,128)(2,1)} %get-tuple-element.220.refs_0_), channel_id=1, source_target_pairs={{0,1},{1,0},{2,3},{3,2},{4,5},{5,4},{6,7},{7,6},{8,9},{9,8},{10,11... | collective-permute-start | bytes 2359304 | tf_op jit(solution)/shard_map/ppermute | solution.py:603
  147.9 50.5 %collective-permute-start.16 = (bf16[384,1024]{1,0:T(8,128)(2,1)S(1)}, bf16[384,1024]{1,0:T(8,128)(2,1)S(1)}, u32[]{:S(2)}, u32[]{:S(2)}) collective-permute-start(bf16[384,1024]{1,0:T(8,128)(2,1)S(1)} %collective-permute-done.12.refs_1_), channel_id=1, source_target_pairs={{0,1},{1,0},{2,3},{3,2},{4,5},{5,4},{6,7},{7,6},{8,9},{9,8},{10,11... | collective-permute-start | bytes 2359304 | tf_op jit(solution)/shard_map/ppermute | solution.py:603
  167.5 32.9 %collective-permute-start.15 = (bf16[384,1024]{1,0:T(8,128)(2,1)S(1)}, bf16[384,1024]{1,0:T(8,128)(2,1)S(1)}, u32[]{:S(2)}, u32[]{:S(2)}) collective-permute-start(bf16[384,1024]{1,0:T(8,128)(2,1)S(1)} %collective-permute-done.14.refs_0_), channel_id=1, source_target_pairs={{0,1},{1,0},{2,3},{3,2},{4,5},{5,4},{6,7},{7,6},{8,9},{9,8},{10,11... | collective-permute-start | bytes 2359304 | tf_op jit(solution)/shard_map/ppermute | solution.py:603
  240.0 23.9 %collective-permute-start.17 = (bf16[384,1024]{1,0:T(8,128)(2,1)S(1)}, bf16[384,1024]{1,0:T(8,128)(2,1)S(1)}, u32[]{:S(2)}, u32[]{:S(2)}) collective-permute-start(bf16[384,1024]{1,0:T(8,128)(2,1)S(1)} %slice_bitcast_fusion.4), channel_id=1, source_target_pairs={{0,1},{1,0},{2,3},{3,2},{4,5},{5,4},{6,7},{7,6},{8,9},{9,8},{10,11... | collective-permute-start | bytes 2359304 | tf_op jit(solution)/shard_map/ppermute | solution.py:603
  264.1 27.5 %collective-permute-start.19 = (bf16[384,1024]{1,0:T(8,128)(2,1)S(1)}, bf16[384,1024]{1,0:T(8,128)(2,1)S(1)}, u32[]{:S(2)}, u32[]{:S(2)}) collective-permute-start(bf16[384,1024]{1,0:T(8,128)(2,1)S(1)} %slice_bitcast_fusion.1), channel_id=1, source_target_pairs={{0,1},{1,0},{2,3},{3,2},{4,5},{5,4},{6,7},{7,6},{8,9},{9,8},{10,11... | collective-permute-start | bytes 2359304 | tf_op jit(solution)/shard_map/ppermute | solution.py:603
  266.2 25.4 %collective-permute-start.18 = (bf16[192,1024]{1,0:T(8,128)(2,1)S(1)}, bf16[192,1024]{1,0:T(8,128)(2,1)S(1)}, u32[]{:S(2)}, u32[]{:S(2)}) collective-permute-start(bf16[192,1024]{1,0:T(8,128)(2,1)S(1)} %get-tuple-element.301), channel_id=1, source_target_pairs={{0,2},{1,3},{2,0},{3,1},{4,6},{5,7},{6,4},{7,5},{8,10},{9,11},{10,... | collective-permute-start | bytes 1179656 | tf_op jit(solution)/shard_map/ppermute | solution.py:603
  291.7 28.7 %collective-permute-start.22 = (bf16[4,4608,128]{2,1,0:T(8,128)(2,1)}, bf16[4,4608,128]{2,1,0:T(8,128)(2,1)}, u32[]{:S(2)}, u32[]{:S(2)}) collective-permute-start(bf16[4,4608,128]{2,1,0:T(8,128)(2,1)} %bitcast.213), channel_id=1, source_target_pairs={{0,4},{4,0},{8,12},{12,8},{16,20},{20,16},{24,28},{28,24},{1,5},{5... | collective-permute-start | bytes 14155784 | tf_op jit(solution)/shard_map/ppermute | solution.py:603
  291.8 28.6 %collective-permute-start.20 = (bf16[384,1024]{1,0:T(8,128)(2,1)S(1)}, bf16[384,1024]{1,0:T(8,128)(2,1)S(1)}, u32[]{:S(2)}, u32[]{:S(2)}) collective-permute-start(bf16[384,1024]{1,0:T(8,128)(2,1)S(1)} %get-tuple-element.316), channel_id=1, source_target_pairs={{0,1},{1,0},{2,3},{3,2},{4,5},{5,4},{6,7},{7,6},{8,9},{9,8},{10,11... | collective-permute-start | bytes 2359304 | tf_op jit(solution)/shard_map/ppermute | solution.py:603
  293.8 25.8 %collective-permute-start.21 = (bf16[192,1024]{1,0:T(8,128)(2,1)S(1)}, bf16[192,1024]{1,0:T(8,128)(2,1)S(1)}, u32[]{:S(2)}, u32[]{:S(2)}) collective-permute-start(bf16[192,1024]{1,0:T(8,128)(2,1)S(1)} %get-tuple-element.317), channel_id=1, source_target_pairs={{0,2},{1,3},{2,0},{3,1},{4,6},{5,7},{6,4},{7,5},{8,10},{9,11},{10,... | collective-permute-start | bytes 1179656 | tf_op jit(solution)/shard_map/ppermute | solution.py:603
  324.5 34.4 %collective-permute-start.24 = (bf16[4,3840,128]{2,1,0:T(8,128)(2,1)}, bf16[4,3840,128]{2,1,0:T(8,128)(2,1)S(1)}, u32[]{:S(2)}, u32[]{:S(2)}) collective-permute-start(bf16[4,3840,128]{2,1,0:T(8,128)(2,1)} %bitcast.36), channel_id=1, source_target_pairs={{0,4},{4,0},{8,12},{12,8},{16,20},{20,16},{24,28},{28,24},{1,5},{5... | collective-permute-start | bytes 11796488 | tf_op jit(solution)/shard_map/ppermute | solution.py:603
  324.5 34.3 %collective-permute-start.25 = (bf16[4608,128]{1,0:T(8,128)(2,1)}, bf16[4608,128]{1,0:T(8,128)(2,1)}, u32[]{:S(2)}, u32[]{:S(2)}) collective-permute-start(bf16[4608,128]{1,0:T(8,128)(2,1)} %get-tuple-element.339), channel_id=1, source_target_pairs={{0,8},{4,12},{8,0},{12,4},{16,24},{20,28},{24,16},{28,20},{1,9},{5... | collective-permute-start | bytes 3538952 | tf_op jit(solution)/shard_map/ppermute | solution.py:603
  326.0 32.9 %collective-permute-start.26 = (bf16[4608,128]{1,0:T(8,128)(2,1)}, bf16[4608,128]{1,0:T(8,128)(2,1)}, u32[]{:S(2)}, u32[]{:S(2)}) collective-permute-start(bf16[4608,128]{1,0:T(8,128)(2,1)} %get-tuple-element.340), channel_id=1, source_target_pairs={{0,16},{4,20},{8,24},{12,28},{16,0},{20,4},{24,8},{28,12},{1,17},{... | collective-permute-start | bytes 3538952 | tf_op jit(solution)/shard_map/ppermute | solution.py:603
  327.4 31.4 %collective-permute-start.23 = (bf16[384,1024]{1,0:T(8,128)(2,1)}, bf16[384,1024]{1,0:T(8,128)(2,1)}, u32[]{:S(2)}, u32[]{:S(2)}) collective-permute-start(bf16[384,1024]{1,0:T(8,128)(2,1)} %slice_bitcast_fusion.3), channel_id=1, source_target_pairs={{0,1},{1,0},{2,3},{3,2},{4,5},{5,4},{6,7},{7,6},{8,9},{9,8},{10,11... | collective-permute-start | bytes 2359304 | tf_op jit(solution)/shard_map/ppermute | solution.py:603
  366.5 38.6 %collective-permute-start.28 = (bf16[4,2048,128]{2,1,0:T(8,128)(2,1)}, bf16[4,2048,128]{2,1,0:T(8,128)(2,1)}, u32[]{:S(2)}, u32[]{:S(2)}) collective-permute-start(bf16[4,2048,128]{2,1,0:T(8,128)(2,1)} %get-tuple-element.369), channel_id=1, source_target_pairs={{0,4},{4,0},{8,12},{12,8},{16,20},{20,16},{24,28},{28,24},{1,5},{5... | collective-permute-start | bytes 6291464 | tf_op jit(solution)/shard_map/ppermute | solution.py:603
  366.5 38.6 %collective-permute-start.29 = (bf16[6144,128]{1,0:T(8,128)(2,1)}, bf16[6144,128]{1,0:T(8,128)(2,1)S(1)}, u32[]{:S(2)}, u32[]{:S(2)}) collective-permute-start(bf16[6144,128]{1,0:T(8,128)(2,1)} %pad_maximum_fusion.3), channel_id=1, source_target_pairs={{0,8},{4,12},{8,0},{12,4},{16,24},{20,28},{24,16},{28,20},{1,9},{5... | collective-permute-start | bytes 4718600 | tf_op jit(solution)/shard_map/ppermute | solution.py:603
  367.0 38.1 %collective-permute-start.30 = (bf16[6144,128]{1,0:T(8,128)(2,1)}, bf16[6144,128]{1,0:T(8,128)(2,1)}, u32[]{:S(2)}, u32[]{:S(2)}) collective-permute-start(bf16[6144,128]{1,0:T(8,128)(2,1)} %pad_maximum_fusion.4), channel_id=1, source_target_pairs={{0,16},{4,20},{8,24},{12,28},{16,0},{20,4},{24,8},{28,12},{1,17},{... | collective-permute-start | bytes 4718600 | tf_op jit(solution)/shard_map/ppermute | solution.py:603
  367.7 37.4 %collective-permute-start.27 = (bf16[384,1024]{1,0:T(8,128)(2,1)}, bf16[384,1024]{1,0:T(8,128)(2,1)}, u32[]{:S(2)}, u32[]{:S(2)}) collective-permute-start(bf16[384,1024]{1,0:T(8,128)(2,1)} %bitcast_add_fusion.8), channel_id=1, source_target_pairs={{0,2},{1,3},{2,0},{3,1},{4,6},{5,7},{6,4},{7,5},{8,10},{9,11},{10,... | collective-permute-start | bytes 2359304 | tf_op jit(solution)/shard_map/ppermute | solution.py:603
  412.4 26.3 %collective-permute-start.32 = (bf16[4,2080,128]{2,1,0:T(8,128)(2,1)}, bf16[4,2080,128]{2,1,0:T(8,128)(2,1)}, u32[]{:S(2)}, u32[]{:S(2)}) collective-permute-start(bf16[4,2080,128]{2,1,0:T(8,128)(2,1)} %get-tuple-element.390), channel_id=1, source_target_pairs={{0,4},{4,0},{8,12},{12,8},{16,20},{20,16},{24,28},{28,24},{1,5},{5... | collective-permute-start | bytes 6389768 | tf_op jit(solution)/shard_map/ppermute | solution.py:603
  412.4 25.0 %collective-permute-start.33 = (bf16[3968,128]{1,0:T(8,128)(2,1)S(1)}, bf16[3968,128]{1,0:T(8,128)(2,1)}, u32[]{:S(2)}, u32[]{:S(2)}) collective-permute-start(bf16[3968,128]{1,0:T(8,128)(2,1)S(1)} %pad_maximum_fusion.9), channel_id=1, source_target_pairs={{0,16},{4,20},{8,24},{12,28},{16,0},{20,4},{24,8},{28,12},{1,17},{... | collective-permute-start | bytes 3047432 | tf_op jit(solution)/shard_map/ppermute | solution.py:603
  413.8 24.9 %collective-permute-start.34 = (bf16[3968,128]{1,0:T(8,128)(2,1)}, bf16[3968,128]{1,0:T(8,128)(2,1)}, u32[]{:S(2)}, u32[]{:S(2)}) collective-permute-start(bf16[3968,128]{1,0:T(8,128)(2,1)} %pad_maximum_fusion.10), channel_id=1, source_target_pairs={{0,8},{4,12},{8,0},{12,4},{16,24},{20,28},{24,16},{28,20},{1,9},{5... | collective-permute-start | bytes 3047432 | tf_op jit(solution)/shard_map/ppermute | solution.py:603
  415.4 21.6 %collective-permute-start.31 = (bf16[384,1024]{1,0:T(8,128)(2,1)}, bf16[384,1024]{1,0:T(8,128)(2,1)S(1)}, u32[]{:S(2)}, u32[]{:S(2)}) collective-permute-start(bf16[384,1024]{1,0:T(8,128)(2,1)} %dynamic-slice_select_fusion), channel_id=1, source_target_pairs={{1,0},{2,1},{3,2},{5,4},{6,5},{7,6},{9,8},{10,9},{11,10},{13,12},{... | collective-permute-start | bytes 2359304 | tf_op jit(solution)/shard_map/ppermute | solution.py:673
  442.1 21.0 %collective-permute-start.35 = (bf16[384,1024]{1,0:T(8,128)(2,1)S(1)}, bf16[384,1024]{1,0:T(8,128)(2,1)S(1)}, u32[]{:S(2)}, u32[]{:S(2)}) collective-permute-start(bf16[384,1024]{1,0:T(8,128)(2,1)S(1)} %select_add_fusion), channel_id=1, source_target_pairs={{1,0},{2,1},{3,2},{5,4},{6,5},{7,6},{9,8},{10,9},{11,10},{13,12},{... | collective-permute-start | bytes 2359304 | tf_op jit(solution)/shard_map/ppermute | solution.py:673
  465.9 19.9 %collective-permute-start.38 = (bf16[384,1024]{1,0:T(8,128)(2,1)S(1)}, bf16[384,1024]{1,0:T(8,128)(2,1)S(1)}, u32[]{:S(2)}, u32[]{:S(2)}) collective-permute-start(bf16[384,1024]{1,0:T(8,128)(2,1)S(1)} %get-tuple-element.404), channel_id=1, source_target_pairs={{1,0},{2,1},{3,2},{5,4},{6,5},{7,6},{9,8},{10,9},{11,10},{13,12},{... | collective-permute-start | bytes 2359304 | tf_op jit(solution)/shard_map/ppermute | solution.py:673
  487.3 23.9 %collective-permute-start.42 = (bf16[1056,128]{1,0:T(8,128)(2,1)S(1)}, bf16[1056,128]{1,0:T(8,128)(2,1)S(1)}, u32[]{:S(2)}, u32[]{:S(2)}) collective-permute-start(bf16[1056,128]{1,0:T(8,128)(2,1)S(1)} %fusion.41), channel_id=1, source_target_pairs={{0,2},{1,3},{2,0},{3,1},{4,6},{5,7},{6,4},{7,5},{8,10},{9,11},{10,... | collective-permute-start | bytes 811016 | tf_op jit(solution)/shard_map/ppermute | solution.py:603
  490.6 20.6 %collective-permute-start.41 = (bf16[1056,128]{1,0:T(8,128)(2,1)S(1)}, bf16[1056,128]{1,0:T(8,128)(2,1)S(1)}, u32[]{:S(2)}, u32[]{:S(2)}) collective-permute-start(bf16[1056,128]{1,0:T(8,128)(2,1)S(1)} %fusion.40), channel_id=1, source_target_pairs={{0,1},{1,0},{2,3},{3,2},{4,5},{5,4},{6,7},{7,6},{8,9},{9,8},{10,11... | collective-permute-start | bytes 811016 | tf_op jit(solution)/shard_map/ppermute | solution.py:603
  (59 other events, 721.5 us)
Sparse Core Ops, SparseCore 0:
  34.0 56.2 all-gather.3
  92.7 60.5 all-gather.5
  155.8 53.6 all-gather.7

commit v4 on v3

--- a/solution.py
+++ b/solution.py
@@ -89,9 +89,11 @@
     pairs = cols // PAIR
     keys = PROMPT + CONT
 
-    def body(at_ref, x0, x1, x2, x3, gain_ref, w_ref, a_ref, q_ref, k_ref, v_ref, p_ref, inv_ref, c_ref, h_ref, b_ref, xs, acc):
+    def body(at_ref, x0, x1, x2, x3, gain_ref, w_ref, a_out, q_ref, k_ref, v_ref, p_ref, inv_ref, c_ref, h_ref, b_ref, xs, acc, a_s, a_sem):
         step = pl.program_id(0)
         t = at_ref[0]
+        a_ref = a_s
+        store = pltpu.make_async_copy(a_s, a_out, a_sem)
 
         @pl.when(step == 0)
         def _():
@@ -106,6 +108,7 @@
             x = x0[...].astype(f32)
             a_ref[PROMPT:tall] = (unit_of(x)[0] * gain).astype(b16)
             acc[...] = x
+            store.start()
 
         q = dot(a_ref[PROMPT:tall], w_ref[0, 0], NN).astype(b16) * jnp.asarray(0.125, b16)
         kv = dot(a_ref[...], jnp.concatenate([w_ref[0, 1], w_ref[0, 2]], 1), NN).astype(b16)
@@ -150,6 +153,7 @@
 
         @pl.when(step == groups - 1)
         def _():
+            store.wait()
             h = acc[...]
             h_ref[...] = h
             b_ref[...] = (unit_of(h)[0] * gain_ref[1:2]).astype(b16)
@@ -168,7 +172,7 @@
                 pl.BlockSpec((1, 4, width, cols), lambda i, at: (i, 0, 0, 0)),
             ],
             out_specs=[
-                pl.BlockSpec((tall, width), whole),
+                pl.BlockSpec(memory_space=pl.ANY),
                 pl.BlockSpec((rows, cols), by_group),
                 pl.BlockSpec((tall, cols), by_group),
                 pl.BlockSpec((tall, cols), by_group),
@@ -178,7 +182,12 @@
                 pl.BlockSpec((rows, width), whole),
                 pl.BlockSpec((rows, width), whole),
             ],
-            scratch_shapes=[pltpu.VMEM((4 * rows, width), b16), pltpu.VMEM((rows, width), f32)],
+            scratch_shapes=[
+                pltpu.VMEM((4 * rows, width), b16),
+                pltpu.VMEM((rows, width), f32),
+                pltpu.VMEM((tall, width), b16),
+                pltpu.SemaphoreType.DMA,
+            ],
         ),
         out_shape=[
             jax.ShapeDtypeStruct((tall, width), b16),
@@ -224,7 +233,7 @@
             sum_ref, *refs = refs
         do, ds, dqs, held, *more = refs
         step = pl.program_id(0)
-        acc = first_out if opens else more[0]
+        acc = more[0]
 
         @pl.when(step == 0)
         def _():
@@ -243,7 +252,7 @@
                 acc[...] = jnp.zeros_like(acc)
             else:
                 do[...] = given_refs[0][...].astype(b16)
-                acc[...] = given_refs[1][...]
+                acc[...] = given_refs[1][...].astype(f32)
 
         low = lax.broadcasted_iota(jnp.int32, (CONT, PAIR), 1) < HEAD_DIM
         zero = jnp.zeros((), b16)
@@ -251,22 +260,24 @@
         def stacked(two):
             return jnp.concatenate([jnp.where(low, two, zero), jnp.where(low, zero, two)], 0)
 
-        def cut_out(span, piece):
+        def cut_out(start_line, piece):
             count = piece.shape[0]
+            span = pl.ds(start_line, count)
             held[:count] = piece
             for s in range(parts if blocked else 2):
                 start = (me_ref[0] ^ s) * cut if blocked else s * lanes_out
                 lanes = pl.ds(pl.multiple_of(start, lanes_out), lanes_out)
                 (far if s % 2 else near)[s // 2, span] = held[:count, lanes]
 
-        def weight_out(kind, left, right):
-            value = dot(left, right, TN).astype(b16)
+        def weight_out(kind, left, right, dims):
+            value = dot(left, right, dims).astype(b16)
             for n in range(value.shape[0] // cols):
                 piece = value[n * cols : (n + 1) * cols]
-                cut_out(pl.ds(pl.multiple_of((step * 4 + kind + n) * cols, 128), cols), piece)
+                line = (kind + n) * cols
+                cut_out(line if opens else pl.multiple_of(step * 4 * cols + line, 128), piece)
 
         dc = dot(do[...], w_ref[0, 3], NN).astype(b16)
-        weight_out(3, c_ref[...], do[...])
+        weight_out(3, c_ref[...], do[...], TN)
         dks, dvs = [], []
         for pair in range(pairs):
             lanes = slice(pair * PAIR, (pair + 1) * PAIR)
@@ -288,25 +299,27 @@
                 ds[sub * 2 * CONT : (sub + 1) * 2 * CONT] = ds1
                 dq2 = (dot(ds1, kp, NN) + dot(ds2, k_ref[own, lanes], NN)) * 0.125
                 dqs[mine, lanes] = jnp.where(low, dq2[:CONT], dq2[CONT:]).astype(b16)
-                dko.append(dot(ds2, qs, TN).astype(b16))
-                dvo.append(dot(p2, dcs, TN).astype(b16))
+                dko.append(dot(qs, ds2, TN).astype(b16))
+                dvo.append(dot(dcs, p2, TN).astype(b16))
                 qall.append(qs)
                 dcall.append(dcs)
             span = slice(pair * 2 * rows, (pair + 1) * 2 * rows)
-            dkp = dot(ds[...], jnp.concatenate(qall, 0), TN).astype(b16)
-            dvp = dot(p_ref[0, span, :PROMPT], jnp.concatenate(dcall, 0), TN).astype(b16)
-            dks.append(jnp.concatenate([dkp] + dko, 0))
-            dvs.append(jnp.concatenate([dvp] + dvo, 0))
-        dkv = jnp.concatenate(dks + dvs, 1)
+            dkp = dot(jnp.concatenate(qall, 0), ds[...], TN).astype(b16)
+            dvp = dot(jnp.concatenate(dcall, 0), p_ref[0, span, :PROMPT], TN).astype(b16)
+            dks.append(jnp.concatenate([dkp] + dko, 1))
+            dvs.append(jnp.concatenate([dvp] + dvo, 1))
+        turned = jnp.concatenate(dks + dvs, 0)
         dq = dqs[...]
-        weight_out(0, dq, a_ref[PROMPT:tall])
-        weight_out(1, dkv, a_ref[...])
-        acc[...] += dot(dkv, jnp.concatenate([w_ref[0, 1], w_ref[0, 2]], 1), NT)
+        weight_out(0, dq, a_ref[PROMPT:tall], TN)
+        weight_out(1, turned, a_ref[...], NN)
+        acc[...] += dot(jnp.transpose(turned), jnp.concatenate([w_ref[0, 1], w_ref[0, 2]], 1), NT)
         acc[PROMPT:] += dot(dq, w_ref[0, 0], NT)
 
-        if not opens:
-            @pl.when(step == count - 1)
-            def _():
+        @pl.when(step == count - 1)
+        def _():
+            if opens:
+                first_out[...] = acc[...].astype(b16)
+            else:
                 first_out[:PROMPT] = acc[:PROMPT].astype(b16)
                 if padded > PROMPT:
                     first_out[PROMPT:] = jnp.zeros((padded - PROMPT, width), b16)
@@ -316,7 +329,7 @@
                 rows_out = jnp.concatenate(
                     [total / gain_ref[0:1], sums_ref[0:1], router_ref[...], jnp.zeros((SMALL_ROWS - 10, width), f32)], 0
                 )
-                cut_out(slice(count * 4 * cols, count * 4 * cols + SMALL_ROWS), rows_out.astype(b16))
+                cut_out(count * 4 * cols, rows_out.astype(b16))
 
     def by_group(i, me):
         return (0, base + i)
@@ -326,7 +339,7 @@
     tall_spec = pl.BlockSpec((tall, width), whole)
     lines = count * 4 * cols + (0 if opens else SMALL_ROWS)
     if opens:
-        first_spec, first_shape = tall_spec, jax.ShapeDtypeStruct((tall, width), f32)
+        first_spec, first_shape = tall_spec, jax.ShapeDtypeStruct((tall, width), b16)
     else:
         first_spec, first_shape = pl.BlockSpec((padded, width), whole), jax.ShapeDtypeStruct((padded, width), b16)
     return pl.pallas_call(
@@ -347,7 +360,12 @@
             pl.BlockSpec((1, 4, width, cols), lambda i, me: (base + i, 0, 0, 0)),
         ]
         + [pl.BlockSpec((8, width), whole)] * len(rest),
-        out_specs=[pl.BlockSpec((places, lines, lanes_out), lambda i, me: (0, 0, 0))] * 2
+        out_specs=[
+            pl.BlockSpec((places, 4 * cols, lanes_out), lambda i, me: (0, i, 0))
+            if opens
+            else pl.BlockSpec((places, lines, lanes_out), lambda i, me: (0, 0, 0))
+        ]
+        * 2
         + [first_spec, row_spec]
         + ([pl.BlockSpec((8, width), whole)] if opens else []),
         scratch_shapes=[
@@ -356,7 +374,7 @@
             pltpu.VMEM((rows, cols), b16),
             pltpu.VMEM((cols, width), b16),
         ]
-        + ([] if opens else [pltpu.VMEM((tall, width), f32)]),
+        + [pltpu.VMEM((tall, width), f32)],
         ),
         out_shape=[
             jax.ShapeDtypeStruct((places, lines, lanes_out), b16),
@@ -441,7 +459,7 @@
             dl = jnp.where(lane < 2 * experts, share * (dprob - inner), 0.0)
             head = dl.astype(b16).astype(f32)
             split = jnp.where(lane < experts, head, dl - head).astype(b16)
-            rg_ref[0] = dot(b_v, split, TN)
+            rg_ref[0] = dot(split, b_v, TN)[:8]
             y_ref[0] = (y + given_refs[2][...]).astype(b16)
             db_ref[0] = (db + given_refs[3][...] + dot(split, r_ref[...], NT)).astype(b16)
 
@@ -458,7 +476,7 @@
     if ends:
         own_block = pl.BlockSpec((1, one, width), lambda i, at: (i, 0, 0))
         outs = [(own_block, jax.ShapeDtypeStruct((2, one, width), b16))] * 2
-        outs += [(pl.BlockSpec((1, width, 128), lambda i, at: (i, 0, 0)), jax.ShapeDtypeStruct((2, width, 128), f32))]
+        outs += [(pl.BlockSpec((1, 8, width), lambda i, at: (i, 0, 0)), jax.ShapeDtypeStruct((2, 8, width), f32))]
     else:
         outs = [(wide, jax.ShapeDtypeStruct((2 * one, width), b16))] * 2
         outs += [(wide, jax.ShapeDtypeStruct((2 * one, width), f32))] * 2
@@ -669,9 +687,13 @@
     blocked = cut % 128 == 0
 
     def stage(sends, given=(), work=None):
-        values, given = together((tuple(value for value, *_ in sends), given))
-        got = tuple(swap(value, *how) if how else lax.ppermute(value, "tensor", down) for value, (_, *how) in zip(values, sends))
-        return together((got, work(given) if work else given))
+        values = tuple(value for value, *_ in sends)
+        if work is None:
+            values = together(values)
+        else:
+            values, given = together((values, given))
+        got = tuple(swap(value, *how) for value, (_, *how) in zip(values, sends))
+        return together((got, given if work is None else work(given)))
 
     def joint(*halvings):
         lists = {}
@@ -717,8 +739,7 @@
     units_0 = halving_of(near_0, got[2:])
 
     rg = (closed_0[2] + closed_1[2]).sum(0)
-    rg = (rg[:, :experts] + rg[:, experts : 2 * experts]).T
-    rg = jnp.concatenate([rg, jnp.zeros((8 - experts, width), f32)], 0)
+    rg = jnp.concatenate([rg[:experts] + rg[experts : 2 * experts], jnp.zeros((8 - experts, width), f32)], 0)
 
     def backward(base, rest):
         return lambda given: attention_backward(here, base, 2, given, rest, gains, a, q, k, v, p, inv, c, attention_w, dp)
@@ -742,19 +763,22 @@
         valid = (index >= 0) & (index < dap.shape[0] // rows)
         return jnp.where(valid, piece, jnp.zeros((), b16))
 
+    def hop(index, sent=None):
+        piece = chunk_of(own - depth + index)
+        return lax.ppermute(piece if sent is None else piece + sent, "tensor", down)
+
+    sent = hop(1)
     sends, take = joint(units_1, heads_0)
-    got, _ = stage([(chunk_of(own - depth + 1),)] + core_send(closed[1]) + sends)
-    sent = got[0]
-    heads_1 = halving_of(closed[0], got[1:])
-    take(got[2:])
+    got, sent = stage(core_send(closed[1]) + sends, sent)
+    heads_1 = halving_of(closed[0], got)
+    take(got[1:])
+    sent = hop(2, sent)
     sends, take = joint(heads_1, heads_0)
-    got, _ = stage([(chunk_of(own - depth + 2) + sent,)] + sends)
-    sent = got[0]
-    take(got[1:])
+    got, sent = stage(sends, sent)
+    take(got)
+    sent = hop(3, sent)
     sends, take = joint(heads_1)
-    got, _ = stage([(chunk_of(own - depth + 3) + sent,)] + sends)
-    sent = got[0]
-    take(got[1:])
+    take([swap(*send) for send in sends])
     if blocked:
         for halving in (units_0, units_1, heads_0, heads_1):
             while halving.orders[0]:

time: 531 us -> 524 us (0.987)
  other arithmetic: 44.8 us -> 38.7 us
  transfers between devices with their start and end apart: 47 -> 47, of which waited for: 23 -> 19; matrix products, arithmetic and copies ran while one was open for 5% -> 5% of each run, Pallas kernels for 42% -> 42%
where the time goes in v4:
time: 524 us; the launch traced here: 515 us
  Pallas kernels  238 us (45%)
  waiting for transfers between devices  125 us (24%)
  starting transfers between devices  80.4 us (15%)
  other arithmetic  38.7 us (7%)
  local copies, waits for them, and re-layouts  18.4 us (4%)
  between operations  14.8 us (3%)
    pallas_call x6, Pallas kernels, experts_blocks(): pl.pallas_call(body, grid_spec=pltpu.PrefetchScalarGridSpec(num_scalar_pr...  103 us
    ppermute x38, waiting for transfers between devices, swap(): return lax.ppermute(value, axis, [(i, i ^ bits) for i in range(size)])  72.7 us
    ppermute x38, starting transfers between devices, swap(): return lax.ppermute(value, axis, [(i, i ^ bits) for i in range(size)])  62.8 us
    pallas_call x2, Pallas kernels, attention_backward(): pl.pallas_call(body, grid_spec=pltpu.PrefetchScalarGridSpec(num_scalar_pr...  54.9 us
    pallas_call x2, Pallas kernels, experts_weights(): pl.pallas_call(body, grid_spec=pltpu.PrefetchScalarGridSpec(num_scalar_pr...  43.8 us
    ppermute x3, waiting for transfers between devices, hop(): return lax.ppermute(piece if sent is None else piece + sent, 'tensor', down)  40.7 us
    pallas_call x1, Pallas kernels, attention_forward(): pl.pallas_call(body, grid_spec=pltpu.PrefetchScalarGridSpec(num_scalar_pr...  31.6 us
    ppermute x3, starting transfers between devices, raised(): return lax.ppermute(value, 'tensor', up)  13.3 us
  transfers between devices with their start and end apart: 47, of which 19 were waited for; matrix products, arithmetic and copies ran while one was open for 5% of the time, Pallas kernels for 42%

profile of v4, /device:TPU:0, one launch (start us, length us, event | category | flops | bytes accessed | tf_op | source)
XLA Modules:
  0.0 515.0 jit_solution(3171063981182022768)
XLA Ops:
  9.2 4.1 collective-permute-start.9
  14.8 10.5 %collective-permute-done.9 = bf16[4,128,256]{2,1,0:T(8,128)(2,1)S(1)} collective-permute-done((bf16[4,128,256]{2,1,0:T(8,128)(2,1)S(1)}, bf16[4,128,256]{2,1,0:T(8,128)(2,1)S(1)}, u32[]{:S(2)}, u32[]{:S(2)}) %collective-permute-start.9) | collective-permute-done | bytes 262176 | tf_op jit(solution)/shard_map/ppermute | solution.py:621
  25.9 6.8 %collective-permute-done.10 = bf16[4,128,256]{2,1,0:T(8,128)(2,1)S(1)} collective-permute-done((bf16[4,128,256]{2,1,0:T(8,128)(2,1)S(1)}, bf16[4,128,256]{2,1,0:T(8,128)(2,1)S(1)}, u32[]{:S(2)}, u32[]{:S(2)}) %collective-permute-start.10) | collective-permute-done | bytes 262176 | tf_op jit(solution)/shard_map/ppermute | solution.py:621
  36.5 3.4 collective-permute-start
  50.7 5.4 %collective-permute-done.4 = bf16[8,256]{1,0:T(8,128)(2,1)S(1)} collective-permute-done((bf16[8,256]{1,0:T(8,128)(2,1)S(1)}, bf16[8,256]{1,0:T(8,128)(2,1)S(1)}, u32[]{:S(2)}, u32[]{:S(2)}) %collective-permute-start.4) | collective-permute-done | bytes 4128 | tf_op jit(solution)/shard_map/ppermute | solution.py:621
  56.1 4.4 collective-permute-start.5
  60.5 3.4 collective-permute-start.6
  63.9 12.2 %collective-permute-done.6 = bf16[8,512]{1,0:T(8,128)(2,1)S(1)} collective-permute-done((bf16[8,512]{1,0:T(8,128)(2,1)S(1)}, bf16[8,512]{1,0:T(8,128)(2,1)S(1)}, u32[]{:S(2)}, u32[]{:S(2)}) %collective-permute-start.6) | collective-permute-done | bytes 8224 | tf_op jit(solution)/shard_map/ppermute | solution.py:621
  76.1 5.5 %collective-permute-start.7 = (bf16[384,1024]{1,0:T(8,128)(2,1)S(1)}, bf16[384,1024]{1,0:T(8,128)(2,1)}, u32[]{:S(2)}, u32[]{:S(2)}) collective-permute-start(bf16[384,1024]{1,0:T(8,128)(2,1)S(1)} %collective-permute-done.5.x2), channel_id=1, source_target_pairs={{0,1},{1,2},{2,3},{4,5},{5,6},{6,7},{8,9},{9,10},{10,11},{12,13},{... | collective-permute-start | bytes 2359304 | tf_op jit(solution)/shard_map/ppermute | solution.py:624
  88.9 6.9 %collective-permute-done.7.x3 = bf16[384,1024]{1,0:T(8,128)(2,1)} collective-permute-done((bf16[384,1024]{1,0:T(8,128)(2,1)S(1)}, bf16[384,1024]{1,0:T(8,128)(2,1)}, u32[]{:S(2)}, u32[]{:S(2)}) %collective-permute-start.7) | collective-permute-done | bytes 786464 | tf_op jit(solution)/shard_map/ppermute | solution.py:624
  98.4 3.4 collective-permute-start.12
  101.8 31.6 %shard_map.230 = (bf16[1408,1024]{1,0:T(8,128)(2,1)}, bf16[384,1024]{1,0:T(8,128)(2,1)}, bf16[1408,1024]{1,0:T(8,128)(2,1)}, bf16[1408,1024]{1,0:T(8,128)(2,1)},...) custom-call(s32[1]{0:T(128)} %bitcast.at_ref.blocks_ref, ...), custom_call_target="tpu_custom_call" | custom-call | flops 2785017856 | bytes 15728640 | tf_op jit(solution)/shard_map/pallas_call | solution.py:164
  133.9 14.7 %collective-permute-start.13 = (bf16[384,1024]{1,0:T(8,128)(2,1)}, bf16[384,1024]{1,0:T(8,128)(2,1)}, u32[]{:S(2)}, u32[]{:S(2)}) collective-permute-start(bf16[384,1024]{1,0:T(8,128)(2,1)} %get-tuple-element.212.refs_0_), channel_id=1, source_target_pairs={{0,1},{1,0},{2,3},{3,2},{4,5},{5,4},{6,7},{7,6},{8,9},{9,8},{10,11... | collective-permute-start | bytes 2359304 | tf_op jit(solution)/shard_map/ppermute | solution.py:621
  148.7 4.7 all-gather.6.cloned.1.call-done.refs_4_.refs_5_.refs_6_.refs_12_.refs_13_.refs_14_
  153.4 14.1 %shard_map.231 = (bf16[768,1024]{1,0:T(8,128)(2,1)}, bf16[768,1024]{1,0:T(8,128)(2,1)}, f32[768,1024]{1,0:T(8,128)}, f32[768,1024]{1,0:T(8,128)}, f32[768,128]{1...) custom-call(s32[1]{0:T(128)} %bitcast.at_ref.blocks_ref, ...), custom_call_target="tpu_custom_call" | custom-call | flops 1811939328 | bytes 3244032 | tf_op jit(solution)/shard_map/pallas_call | solution.py:485
  169.6 14.3 %shard_map.233 = (bf16[768,1024]{1,0:T(8,128)(2,1)}, bf16[768,1024]{1,0:T(8,128)(2,1)}, f32[768,1024]{1,0:T(8,128)}, f32[768,1024]{1,0:T(8,128)}, f32[768,128]{1...) custom-call(s32[1]{0:T(128)} %bitcast.25.blocks_ref, ...), custom_call_target="tpu_custom_call" | custom-call | flops 1811939328 | bytes 3244032 | tf_op jit(solution)/shard_map/pallas_call | solution.py:485
  183.9 14.5 %shard_map.232 = (bf16[768,1024]{1,0:T(8,128)(2,1)}, bf16[768,1024]{1,0:T(8,128)(2,1)}, f32[768,1024]{1,0:T(8,128)}, f32[768,1024]{1,0:T(8,128)}, f32[768,128]{1...) custom-call(s32[1]{0:T(128)} %bitcast.18.blocks_ref, ...), custom_call_target="tpu_custom_call", output_to_operand_aliasing={{0}: (3, {}), {1}: (4, {}), {2}: (5, {}), {3}: (6, {}), {4}... | custom-call | flops 1811939328 | bytes 3244032 | tf_op jit(solution)/shard_map/pallas_call | solution.py:485
  200.8 14.5 %shard_map.234 = (bf16[768,1024]{1,0:T(8,128)(2,1)}, bf16[768,1024]{1,0:T(8,128)(2,1)}, f32[768,1024]{1,0:T(8,128)}, f32[768,1024]{1,0:T(8,128)}, f32[768,128]{1...) custom-call(s32[1]{0:T(128)} %bitcast.24.blocks_ref, ...), custom_call_target="tpu_custom_call", output_to_operand_aliasing={{0}: (3, {}), {1}: (4, {}), {2}: (5, {}), {3}: (6, {}), {4}... | custom-call | flops 1811939328 | bytes 3244032 | tf_op jit(solution)/shard_map/pallas_call | solution.py:485
  215.3 22.9 %shard_map.235 = (bf16[2,384,1024]{2,1,0:T(8,128)(2,1)}, bf16[2,384,1024]{2,1,0:T(8,128)(2,1)}, f32[2,8,1024]{2,1,0:T(8,128)}, bf16[768,1280]{1,0:T(8,128)(2,1)}...) custom-call(s32[2]{0:T(128)} %pad_add_fusion.1.blocks_ref, bf16[768,1024]{1,0:T(8,128)(2,1)} %get-tuple-element.312.refs_0_.refs_1_, ...), custom_call_target="tpu_custom_call" | custom-call | flops 3019898880 | bytes 2703360 | tf_op jit(solution)/shard_map/pallas_call | solution.py:485
  240.3 23.2 %shard_map.236 = (bf16[2,384,1024]{2,1,0:T(8,128)(2,1)}, bf16[2,384,1024]{2,1,0:T(8,128)(2,1)}, f32[2,8,1024]{2,1,0:T(8,128)}, bf16[768,1280]{1,0:T(8,128)(2,1)}...) custom-call(s32[2]{0:T(128)} %pad_add_fusion.blocks_ref, bf16[768,1024]{1,0:T(8,128)(2,1)} %get-tuple-element.311.refs_0_, ...), custom_call_target="tpu_custom_call" | custom-call | flops 3019898880 | bytes 2703360 | tf_op jit(solution)/shard_map/pallas_call | solution.py:485
  268.6 23.2 %shard_map.237 = (bf16[4,3,1536,128]{3,2,1,0:T(8,128)(2,1)}, bf16[4,3,1536,128]{3,2,1,0:T(8,128)(2,1)}) custom-call(s32[1]{0:T(128)} %bitcast.32.me_ref, bf16[768,1024]{1,0:T(8,128)(2,1)} %get-tuple-element.311.refs_0_, bf16[768,1024]{1,0:T(8,128)(2,1)} %get-tuple-element.312.refs_0_.refs_1_, bf16[768,1024]{1,0:T(8,128)(2,1)} %get-tuple-element.313.refs_1_.refs_2_, ...), custom_call_target="tpu_custom_call" | custom-call | flops 3623878656 | bytes 5898240 | tf_op jit(solution)/shard_map/pallas_call | solution.py:536
  296.2 20.7 %shard_map.238 = (bf16[4,3,1280,128]{3,2,1,0:T(8,128)(2,1)}, bf16[4,3,1280,128]{3,2,1,0:T(8,128)(2,1)}) custom-call(s32[1]{0:T(128)} %bitcast.32.me_ref, bf16[768,1024]{1,0:T(8,128)(2,1)} %get-tuple-element.311.refs_0_, bf16[768,1024]{1,0:T(8,128)(2,1)} %get-tuple-element.312.refs_0_.refs_1_, bf16[768,1024]{1,0:T(8,128)(2,1)} %get-tuple-element.313.refs_1_.refs_2_, ...), custom_call_target="tpu_custom_call" | custom-call | flops 3019898880 | bytes 4915200 | tf_op jit(solution)/shard_map/pallas_call | solution.py:536
  330.1 27.2 %shard_map.239 = (bf16[4,2048,128]{2,1,0:T(8,128)(2,1)}, bf16[4,2048,128]{2,1,0:T(8,128)(2,1)}, bf16[1408,1024]{1,0:T(8,128)(2,1)}, f32[384,1024]{1,0:T(8,128)}, f32[8,1024]{1,0:T(8,128)}) custom-call(s32[1]{0:T(128)} %bitcast.32.me_ref, f32[384,1024]{1,0:T(8,128)} %get-tuple-element.333.refs_0_, bf16[384,1024]{1,0:T(8,128)(2,1)} %refs_1_.1, ...), custom_call_target="tpu_custom_call" | custom-call | flops 2785017856 | bytes 10485760 | tf_op jit(solution)/shard_map/pallas_call | solution.py:345
  370.2 27.7 %shard_map.240 = (bf16[4,2080,128]{2,1,0:T(8,128)(2,1)}, bf16[4,2080,128]{2,1,0:T(8,128)(2,1)}, bf16[1152,1024]{1,0:T(8,128)(2,1)}, f32[384,1024]{1,0:T(8,128)}) custom-call(s32[1]{0:T(128)} %bitcast.32.me_ref, f32[384,1024]{1,0:T(8,128)} %get-tuple-element.364.refs_0_.dh_ref, bf16[1408,1024]{1,0:T(8,128)(2,1)} %get-tuple-element.365.refs_1_, ...), custom_call_target="tpu_custom_call" | custom-call | flops 2785017856 | bytes 10485760 | tf_op jit(solution)/shard_map/pallas_call | solution.py:345
  397.9 7.7 %collective-permute-done.27 = bf16[384,1024]{1,0:T(8,128)(2,1)} collective-permute-done((bf16[384,1024]{1,0:T(8,128)(2,1)}, bf16[384,1024]{1,0:T(8,128)(2,1)}, u32[]{:S(2)}, u32[]{:S(2)}) %collective-permute-start.27) | collective-permute-done | bytes 786464 | tf_op jit(solution)/shard_map/ppermute | solution.py:621
  420.9 16.8 %collective-permute-done.34 = bf16[384,1024]{1,0:T(8,128)(2,1)S(1)} collective-permute-done((bf16[384,1024]{1,0:T(8,128)(2,1)S(1)}, bf16[384,1024]{1,0:T(8,128)(2,1)S(1)}, u32[]{:S(2)}, u32[]{:S(2)}) %collective-permute-start.34) | collective-permute-done | bytes 786464 | tf_op jit(solution)/shard_map/ppermute | solution.py:768
  444.7 16.3 %collective-permute-done.37 = bf16[384,1024]{1,0:T(8,128)(2,1)S(1)} collective-permute-done((bf16[384,1024]{1,0:T(8,128)(2,1)S(1)}, bf16[384,1024]{1,0:T(8,128)(2,1)S(1)}, u32[]{:S(2)}, u32[]{:S(2)}) %collective-permute-start.37) | collective-permute-done | bytes 786464 | tf_op jit(solution)/shard_map/ppermute | solution.py:768
  464.3 3.3 collective-permute-done.41
  470.8 3.6 collective-permute-done.39
  475.9 3.4 collective-permute-start.40
  481.7 7.6 %collective-permute-done.38.sent_ref = bf16[384,1024]{1,0:T(8,128)(2,1)S(1)} collective-permute-done((bf16[384,1024]{1,0:T(8,128)(2,1)S(1)}, bf16[384,1024]{1,0:T(8,128)(2,1)S(1)}, u32[]{:S(2)}, u32[]{:S(2)}) %collective-permute-start.38) | collective-permute-done | bytes 786464 | tf_op jit(solution)/shard_map/ppermute | solution.py:768
  491.6 12.6 %collective-permute-done.42 = bf16[1056,128]{1,0:T(8,128)(2,1)S(1)} collective-permute-done((bf16[1056,128]{1,0:T(8,128)(2,1)S(1)}, bf16[1056,128]{1,0:T(8,128)(2,1)S(1)}, u32[]{:S(2)}, u32[]{:S(2)}) %collective-permute-start.42) | collective-permute-done | bytes 270368 | tf_op jit(solution)/shard_map/ppermute | solution.py:621
  (244 shorter events, 109.8 us)
Async XLA Ops:
  7.2 94.7 %all-gather.4.cloned.1.call-start = ((), (), s32[]{:S(2)}) async-start(), calls=%async_computation | async-start | bytes 9437184 | tf_op jit(solution)/shard_map/all_gather | solution.py:629
  33.8 119.5 %all-gather.6.cloned.1.call-start = ((), (), s32[]{:S(2)}) async-start(), calls=%async_computation.1 | async-start | bytes 10616832 | tf_op jit(solution)/shard_map/all_gather | solution.py:655
  35.3 179.9 %all-gather.8.cloned.1.call-start = ((), (), s32[]{:S(2)}) async-start(), calls=%async_computation.2 | async-start | bytes 8847360 | tf_op jit(solution)/shard_map/all_gather | solution.py:655
  95.9 37.6 %collective-permute-start.11 = (bf16[384,1024]{1,0:T(8,128)(2,1)S(1)}, bf16[384,1024]{1,0:T(8,128)(2,1)S(1)}, u32[]{:S(2)}, u32[]{:S(2)}) collective-permute-start(bf16[384,1024]{1,0:T(8,128)(2,1)S(1)} %copy-done.11), channel_id=1, source_target_pairs={{0,1},{1,0},{2,3},{3,2},{4,5},{5,4},{6,7},{7,6},{8,9},{9,8},{10,11... | collective-permute-start | bytes 2359304 | tf_op jit(solution)/shard_map/ppermute | solution.py:621
  98.4 35.0 %collective-permute-start.12 = (bf16[384,1024]{1,0:T(8,128)(2,1)S(1)}, bf16[384,1024]{1,0:T(8,128)(2,1)S(1)}, u32[]{:S(2)}, u32[]{:S(2)}) collective-permute-start(bf16[384,1024]{1,0:T(8,128)(2,1)S(1)} %copy-done.11), channel_id=1, source_target_pairs={{0,2},{1,3},{2,0},{3,1},{4,6},{5,7},{6,4},{7,5},{8,10},{9,11},{10,... | collective-permute-start | bytes 2359304 | tf_op jit(solution)/shard_map/ppermute | solution.py:621
  133.5 34.0 %collective-permute-start.14 = (bf16[384,1024]{1,0:T(8,128)(2,1)}, bf16[384,1024]{1,0:T(8,128)(2,1)S(1)}, u32[]{:S(2)}, u32[]{:S(2)}) collective-permute-start(bf16[384,1024]{1,0:T(8,128)(2,1)} %get-tuple-element.212.refs_0_), channel_id=1, source_target_pairs={{0,2},{1,3},{2,0},{3,1},{4,6},{5,7},{6,4},{7,5},{8,10},{9,11},{10,... | collective-permute-start | bytes 2359304 | tf_op jit(solution)/shard_map/ppermute | solution.py:621
  133.9 50.0 %collective-permute-start.13 = (bf16[384,1024]{1,0:T(8,128)(2,1)}, bf16[384,1024]{1,0:T(8,128)(2,1)}, u32[]{:S(2)}, u32[]{:S(2)}) collective-permute-start(bf16[384,1024]{1,0:T(8,128)(2,1)} %get-tuple-element.212.refs_0_), channel_id=1, source_target_pairs={{0,1},{1,0},{2,3},{3,2},{4,5},{5,4},{6,7},{7,6},{8,9},{9,8},{10,11... | collective-permute-start | bytes 2359304 | tf_op jit(solution)/shard_map/ppermute | solution.py:621
  148.6 49.8 %collective-permute-start.16 = (bf16[384,1024]{1,0:T(8,128)(2,1)S(1)}, bf16[384,1024]{1,0:T(8,128)(2,1)S(1)}, u32[]{:S(2)}, u32[]{:S(2)}) collective-permute-start(bf16[384,1024]{1,0:T(8,128)(2,1)S(1)} %collective-permute-done.12.refs_1_), channel_id=1, source_target_pairs={{0,1},{1,0},{2,3},{3,2},{4,5},{5,4},{6,7},{7,6},{8,9},{9,8},{10,11... | collective-permute-start | bytes 2359304 | tf_op jit(solution)/shard_map/ppermute | solution.py:621
  167.5 32.4 %collective-permute-start.15 = (bf16[384,1024]{1,0:T(8,128)(2,1)S(1)}, bf16[384,1024]{1,0:T(8,128)(2,1)S(1)}, u32[]{:S(2)}, u32[]{:S(2)}) collective-permute-start(bf16[384,1024]{1,0:T(8,128)(2,1)S(1)} %collective-permute-done.14.refs_0_), channel_id=1, source_target_pairs={{0,1},{1,0},{2,3},{3,2},{4,5},{5,4},{6,7},{7,6},{8,9},{9,8},{10,11... | collective-permute-start | bytes 2359304 | tf_op jit(solution)/shard_map/ppermute | solution.py:621
  239.5 24.1 %collective-permute-start.17 = (bf16[384,1024]{1,0:T(8,128)(2,1)S(1)}, bf16[384,1024]{1,0:T(8,128)(2,1)S(1)}, u32[]{:S(2)}, u32[]{:S(2)}) collective-permute-start(bf16[384,1024]{1,0:T(8,128)(2,1)S(1)} %slice_bitcast_fusion.4), channel_id=1, source_target_pairs={{0,1},{1,0},{2,3},{3,2},{4,5},{5,4},{6,7},{7,6},{8,9},{9,8},{10,11... | collective-permute-start | bytes 2359304 | tf_op jit(solution)/shard_map/ppermute | solution.py:621
  264.5 27.4 %collective-permute-start.19 = (bf16[384,1024]{1,0:T(8,128)(2,1)S(1)}, bf16[384,1024]{1,0:T(8,128)(2,1)S(1)}, u32[]{:S(2)}, u32[]{:S(2)}) collective-permute-start(bf16[384,1024]{1,0:T(8,128)(2,1)S(1)} %slice_bitcast_fusion.1), channel_id=1, source_target_pairs={{0,1},{1,0},{2,3},{3,2},{4,5},{5,4},{6,7},{7,6},{8,9},{9,8},{10,11... | collective-permute-start | bytes 2359304 | tf_op jit(solution)/shard_map/ppermute | solution.py:621
  266.4 25.5 %collective-permute-start.18 = (bf16[192,1024]{1,0:T(8,128)(2,1)S(1)}, bf16[192,1024]{1,0:T(8,128)(2,1)S(1)}, u32[]{:S(2)}, u32[]{:S(2)}) collective-permute-start(bf16[192,1024]{1,0:T(8,128)(2,1)S(1)} %get-tuple-element.293), channel_id=1, source_target_pairs={{0,2},{1,3},{2,0},{3,1},{4,6},{5,7},{6,4},{7,5},{8,10},{9,11},{10,... | collective-permute-start | bytes 1179656 | tf_op jit(solution)/shard_map/ppermute | solution.py:621
  291.9 28.9 %collective-permute-start.22 = (bf16[4,4608,128]{2,1,0:T(8,128)(2,1)}, bf16[4,4608,128]{2,1,0:T(8,128)(2,1)}, u32[]{:S(2)}, u32[]{:S(2)}) collective-permute-start(bf16[4,4608,128]{2,1,0:T(8,128)(2,1)} %bitcast.211), channel_id=1, source_target_pairs={{0,4},{4,0},{8,12},{12,8},{16,20},{20,16},{24,28},{28,24},{1,5},{5... | collective-permute-start | bytes 14155784 | tf_op jit(solution)/shard_map/ppermute | solution.py:621
  291.9 28.8 %collective-permute-start.20 = (bf16[384,1024]{1,0:T(8,128)(2,1)S(1)}, bf16[384,1024]{1,0:T(8,128)(2,1)S(1)}, u32[]{:S(2)}, u32[]{:S(2)}) collective-permute-start(bf16[384,1024]{1,0:T(8,128)(2,1)S(1)} %get-tuple-element.308), channel_id=1, source_target_pairs={{0,1},{1,0},{2,3},{3,2},{4,5},{5,4},{6,7},{7,6},{8,9},{9,8},{10,11... | collective-permute-start | bytes 2359304 | tf_op jit(solution)/shard_map/ppermute | solution.py:621
  294.2 25.9 %collective-permute-start.21 = (bf16[192,1024]{1,0:T(8,128)(2,1)}, bf16[192,1024]{1,0:T(8,128)(2,1)}, u32[]{:S(2)}, u32[]{:S(2)}) collective-permute-start(bf16[192,1024]{1,0:T(8,128)(2,1)} %get-tuple-element.309), channel_id=1, source_target_pairs={{0,2},{1,3},{2,0},{3,1},{4,6},{5,7},{6,4},{7,5},{8,10},{9,11},{10,... | collective-permute-start | bytes 1179656 | tf_op jit(solution)/shard_map/ppermute | solution.py:621
  324.9 32.4 %collective-permute-start.24 = (bf16[4,3840,128]{2,1,0:T(8,128)(2,1)}, bf16[4,3840,128]{2,1,0:T(8,128)(2,1)S(1)}, u32[]{:S(2)}, u32[]{:S(2)}) collective-permute-start(bf16[4,3840,128]{2,1,0:T(8,128)(2,1)} %bitcast.36), channel_id=1, source_target_pairs={{0,4},{4,0},{8,12},{12,8},{16,20},{20,16},{24,28},{28,24},{1,5},{5... | collective-permute-start | bytes 11796488 | tf_op jit(solution)/shard_map/ppermute | solution.py:621
  324.9 32.4 %collective-permute-start.25 = (bf16[4608,128]{1,0:T(8,128)(2,1)}, bf16[4608,128]{1,0:T(8,128)(2,1)}, u32[]{:S(2)}, u32[]{:S(2)}) collective-permute-start(bf16[4608,128]{1,0:T(8,128)(2,1)} %get-tuple-element.331), channel_id=1, source_target_pairs={{0,8},{4,12},{8,0},{12,4},{16,24},{20,28},{24,16},{28,20},{1,9},{5... | collective-permute-start | bytes 3538952 | tf_op jit(solution)/shard_map/ppermute | solution.py:621
  326.3 31.0 %collective-permute-start.26 = (bf16[4608,128]{1,0:T(8,128)(2,1)}, bf16[4608,128]{1,0:T(8,128)(2,1)}, u32[]{:S(2)}, u32[]{:S(2)}) collective-permute-start(bf16[4608,128]{1,0:T(8,128)(2,1)} %get-tuple-element.332), channel_id=1, source_target_pairs={{0,16},{4,20},{8,24},{12,28},{16,0},{20,4},{24,8},{28,12},{1,17},{... | collective-permute-start | bytes 3538952 | tf_op jit(solution)/shard_map/ppermute | solution.py:621
  327.6 29.6 %collective-permute-start.23 = (bf16[384,1024]{1,0:T(8,128)(2,1)}, bf16[384,1024]{1,0:T(8,128)(2,1)}, u32[]{:S(2)}, u32[]{:S(2)}) collective-permute-start(bf16[384,1024]{1,0:T(8,128)(2,1)} %slice_bitcast_fusion.3), channel_id=1, source_target_pairs={{0,1},{1,0},{2,3},{3,2},{4,5},{5,4},{6,7},{7,6},{8,9},{9,8},{10,11... | collective-permute-start | bytes 2359304 | tf_op jit(solution)/shard_map/ppermute | solution.py:621
  366.9 38.7 %collective-permute-start.28 = (bf16[4,2048,128]{2,1,0:T(8,128)(2,1)}, bf16[4,2048,128]{2,1,0:T(8,128)(2,1)}, u32[]{:S(2)}, u32[]{:S(2)}) collective-permute-start(bf16[4,2048,128]{2,1,0:T(8,128)(2,1)} %get-tuple-element.361), channel_id=1, source_target_pairs={{0,4},{4,0},{8,12},{12,8},{16,20},{20,16},{24,28},{28,24},{1,5},{5... | collective-permute-start | bytes 6291464 | tf_op jit(solution)/shard_map/ppermute | solution.py:621
  366.9 38.7 %collective-permute-start.29 = (bf16[6144,128]{1,0:T(8,128)(2,1)}, bf16[6144,128]{1,0:T(8,128)(2,1)}, u32[]{:S(2)}, u32[]{:S(2)}) collective-permute-start(bf16[6144,128]{1,0:T(8,128)(2,1)} %pad_maximum_fusion.3), channel_id=1, source_target_pairs={{0,8},{4,12},{8,0},{12,4},{16,24},{20,28},{24,16},{28,20},{1,9},{5... | collective-permute-start | bytes 4718600 | tf_op jit(solution)/shard_map/ppermute | solution.py:621
  367.4 38.2 %collective-permute-start.30 = (bf16[6144,128]{1,0:T(8,128)(2,1)}, bf16[6144,128]{1,0:T(8,128)(2,1)}, u32[]{:S(2)}, u32[]{:S(2)}) collective-permute-start(bf16[6144,128]{1,0:T(8,128)(2,1)} %pad_maximum_fusion.4), channel_id=1, source_target_pairs={{0,16},{4,20},{8,24},{12,28},{16,0},{20,4},{24,8},{28,12},{1,17},{... | collective-permute-start | bytes 4718600 | tf_op jit(solution)/shard_map/ppermute | solution.py:621
  368.1 37.5 %collective-permute-start.27 = (bf16[384,1024]{1,0:T(8,128)(2,1)}, bf16[384,1024]{1,0:T(8,128)(2,1)}, u32[]{:S(2)}, u32[]{:S(2)}) collective-permute-start(bf16[384,1024]{1,0:T(8,128)(2,1)} %bitcast_add_fusion.8), channel_id=1, source_target_pairs={{0,2},{1,3},{2,0},{3,1},{4,6},{5,7},{6,4},{7,5},{8,10},{9,11},{10,... | collective-permute-start | bytes 2359304 | tf_op jit(solution)/shard_map/ppermute | solution.py:621
  410.3 27.4 %collective-permute-start.31 = (bf16[4,2080,128]{2,1,0:T(8,128)(2,1)}, bf16[4,2080,128]{2,1,0:T(8,128)(2,1)S(1)}, u32[]{:S(2)}, u32[]{:S(2)}) collective-permute-start(bf16[4,2080,128]{2,1,0:T(8,128)(2,1)} %get-tuple-element.382), channel_id=1, source_target_pairs={{0,4},{4,0},{8,12},{12,8},{16,20},{20,16},{24,28},{28,24},{1,5},{5... | collective-permute-start | bytes 6389768 | tf_op jit(solution)/shard_map/ppermute | solution.py:621
  410.4 27.4 %collective-permute-start.32 = (bf16[3968,128]{1,0:T(8,128)(2,1)S(1)}, bf16[3968,128]{1,0:T(8,128)(2,1)S(1)}, u32[]{:S(2)}, u32[]{:S(2)}) collective-permute-start(bf16[3968,128]{1,0:T(8,128)(2,1)S(1)} %pad_maximum_fusion.9), channel_id=1, source_target_pairs={{0,16},{4,20},{8,24},{12,28},{16,0},{20,4},{24,8},{28,12},{1,17},{... | collective-permute-start | bytes 3047432 | tf_op jit(solution)/shard_map/ppermute | solution.py:621
  411.6 26.1 %collective-permute-start.33 = (bf16[3968,128]{1,0:T(8,128)(2,1)}, bf16[3968,128]{1,0:T(8,128)(2,1)S(1)}, u32[]{:S(2)}, u32[]{:S(2)}) collective-permute-start(bf16[3968,128]{1,0:T(8,128)(2,1)} %pad_maximum_fusion.10), channel_id=1, source_target_pairs={{0,8},{4,12},{8,0},{12,4},{16,24},{20,28},{24,16},{28,20},{1,9},{5... | collective-permute-start | bytes 3047432 | tf_op jit(solution)/shard_map/ppermute | solution.py:621
  416.3 21.4 %collective-permute-start.34 = (bf16[384,1024]{1,0:T(8,128)(2,1)S(1)}, bf16[384,1024]{1,0:T(8,128)(2,1)S(1)}, u32[]{:S(2)}, u32[]{:S(2)}) collective-permute-start(bf16[384,1024]{1,0:T(8,128)(2,1)S(1)} %dynamic-slice_select_fusion), channel_id=1, source_target_pairs={{1,0},{2,1},{3,2},{5,4},{6,5},{7,6},{9,8},{10,9},{11,10},{13,12},{... | collective-permute-start | bytes 2359304 | tf_op jit(solution)/shard_map/ppermute | solution.py:768
  439.4 21.6 %collective-permute-start.35 = (bf16[3104,128]{1,0:T(8,128)(2,1)S(1)}, bf16[3104,128]{1,0:T(8,128)(2,1)S(1)}, u32[]{:S(2)}, u32[]{:S(2)}) collective-permute-start(bf16[3104,128]{1,0:T(8,128)(2,1)S(1)} %pad_maximum_fusion.12), channel_id=1, source_target_pairs={{0,8},{4,12},{8,0},{12,4},{16,24},{20,28},{24,16},{28,20},{1,9},{5... | collective-permute-start | bytes 2383880 | tf_op jit(solution)/shard_map/ppermute | solution.py:621
  440.0 21.0 %collective-permute-start.36 = (bf16[3104,128]{1,0:T(8,128)(2,1)S(1)}, bf16[3104,128]{1,0:T(8,128)(2,1)S(1)}, u32[]{:S(2)}, u32[]{:S(2)}) collective-permute-start(bf16[3104,128]{1,0:T(8,128)(2,1)S(1)} %pad_maximum_fusion.13), channel_id=1, source_target_pairs={{0,16},{4,20},{8,24},{12,28},{16,0},{20,4},{24,8},{28,12},{1,17},{... | collective-permute-start | bytes 2383880 | tf_op jit(solution)/shard_map/ppermute | solution.py:621
  463.0 26.3 %collective-permute-start.38 = (bf16[384,1024]{1,0:T(8,128)(2,1)S(1)}, bf16[384,1024]{1,0:T(8,128)(2,1)S(1)}, u32[]{:S(2)}, u32[]{:S(2)}) collective-permute-start(bf16[384,1024]{1,0:T(8,128)(2,1)S(1)} %get-tuple-element.453), channel_id=1, source_target_pairs={{1,0},{2,1},{3,2},{5,4},{6,5},{7,6},{9,8},{10,9},{11,10},{13,12},{... | collective-permute-start | bytes 2359304 | tf_op jit(solution)/shard_map/ppermute | solution.py:768
  474.8 29.4 %collective-permute-start.42 = (bf16[1056,128]{1,0:T(8,128)(2,1)S(1)}, bf16[1056,128]{1,0:T(8,128)(2,1)S(1)}, u32[]{:S(2)}, u32[]{:S(2)}) collective-permute-start(bf16[1056,128]{1,0:T(8,128)(2,1)S(1)} %fusion.41), channel_id=1, source_target_pairs={{0,2},{1,3},{2,0},{3,1},{4,6},{5,7},{6,4},{7,5},{8,10},{9,11},{10,... | collective-permute-start | bytes 811016 | tf_op jit(solution)/shard_map/ppermute | solution.py:621
  475.9 28.2 %collective-permute-start.40 = (bf16[1056,128]{1,0:T(8,128)(2,1)S(1)}, bf16[1056,128]{1,0:T(8,128)(2,1)S(1)}, u32[]{:S(2)}, u32[]{:S(2)}) collective-permute-start(bf16[1056,128]{1,0:T(8,128)(2,1)S(1)} %fusion.40), channel_id=1, source_target_pairs={{0,1},{1,0},{2,3},{3,2},{4,5},{5,4},{6,7},{7,6},{8,9},{9,8},{10,11... | collective-permute-start | bytes 811016 | tf_op jit(solution)/shard_map/ppermute | solution.py:621
  (57 other events, 709.8 us)
Sparse Core Ops, SparseCore 0:
  34.0 56.2 all-gather.3
  92.7 60.5 all-gather.5
  155.8 53.6 all-gather.7

commit v5 on v4

--- a/solution.py
+++ b/solution.py
@@ -774,8 +774,7 @@
     take(got[1:])
     sent = hop(2, sent)
     sends, take = joint(heads_1, heads_0)
-    got, sent = stage(sends, sent)
-    take(got)
+    take([swap(*send) for send in sends])
     sent = hop(3, sent)
     sends, take = joint(heads_1)
     take([swap(*send) for send in sends])

time: 524 us -> 532 us (1.015)
  waiting for transfers between devices: 125 us -> 132 us
    ppermute x38, waiting for transfers between devices: 72.7 us -> 103 us  [swap(): return lax.ppermute(value, axis, [(i, i ^ bits) for i in range(size)])]
    ppermute x3, waiting for transfers between devices: 40.7 us -> 16.8 us  [hop(): return lax.ppermute(piece if sent is None else piece + sent, 'tensor', down)]
  transfers between devices with their start and end apart: 47 -> 47, of which waited for: 19 -> 18; matrix products, arithmetic and copies ran while one was open for 5% -> 5% of each run, Pallas kernels for 42% -> 41%
where the time goes in v5:
time: 532 us; the launch traced here: 523 us
  Pallas kernels  237 us (45%)
  waiting for transfers between devices  132 us (25%)
  starting transfers between devices  79.6 us (15%)
  other arithmetic  39.5 us (7%)
  local copies, waits for them, and re-layouts  19.8 us (4%)
  between operations  14.8 us (3%)
    ppermute x38, waiting for transfers between devices, swap(): return lax.ppermute(value, axis, [(i, i ^ bits) for i in range(size)])  103 us
    pallas_call x6, Pallas kernels, experts_blocks(): pl.pallas_call(body, grid_spec=pltpu.PrefetchScalarGridSpec(num_scalar_pr...  103 us
    ppermute x38, starting transfers between devices, swap(): return lax.ppermute(value, axis, [(i, i ^ bits) for i in range(size)])  62 us
    pallas_call x2, Pallas kernels, attention_backward(): pl.pallas_call(body, grid_spec=pltpu.PrefetchScalarGridSpec(num_scalar_pr...  54.9 us
    pallas_call x2, Pallas kernels, experts_weights(): pl.pallas_call(body, grid_spec=pltpu.PrefetchScalarGridSpec(num_scalar_pr...  43.9 us
    pallas_call x1, Pallas kernels, attention_forward(): pl.pallas_call(body, grid_spec=pltpu.PrefetchScalarGridSpec(num_scalar_pr...  31.6 us
    ppermute x3, waiting for transfers between devices, hop(): return lax.ppermute(piece if sent is None else piece + sent, 'tensor', down)  16.8 us
    ppermute x3, starting transfers between devices, raised(): return lax.ppermute(value, 'tensor', up)  13.3 us
  transfers between devices with their start and end apart: 47, of which 18 were waited for; matrix products, arithmetic and copies ran while one was open for 5% of the time, Pallas kernels for 41%

profile of v5, /device:TPU:0, one launch (start us, length us, event | category | flops | bytes accessed | tf_op | source)
XLA Modules:
  0.0 523.1 jit_solution(13517260445492122224)
XLA Ops:
  9.2 4.1 collective-permute-start.9
  14.8 10.5 %collective-permute-done.9 = bf16[4,128,256]{2,1,0:T(8,128)(2,1)S(1)} collective-permute-done((bf16[4,128,256]{2,1,0:T(8,128)(2,1)S(1)}, bf16[4,128,256]{2,1,0:T(8,128)(2,1)S(1)}, u32[]{:S(2)}, u32[]{:S(2)}) %collective-permute-start.9) | collective-permute-done | bytes 262176 | tf_op jit(solution)/shard_map/ppermute | solution.py:621
  25.9 6.8 %collective-permute-done.10 = bf16[4,128,256]{2,1,0:T(8,128)(2,1)S(1)} collective-permute-done((bf16[4,128,256]{2,1,0:T(8,128)(2,1)S(1)}, bf16[4,128,256]{2,1,0:T(8,128)(2,1)S(1)}, u32[]{:S(2)}, u32[]{:S(2)}) %collective-permute-start.10) | collective-permute-done | bytes 262176 | tf_op jit(solution)/shard_map/ppermute | solution.py:621
  36.5 3.4 collective-permute-start
  50.7 5.4 %collective-permute-done.4 = bf16[8,256]{1,0:T(8,128)(2,1)S(1)} collective-permute-done((bf16[8,256]{1,0:T(8,128)(2,1)S(1)}, bf16[8,256]{1,0:T(8,128)(2,1)S(1)}, u32[]{:S(2)}, u32[]{:S(2)}) %collective-permute-start.4) | collective-permute-done | bytes 4128 | tf_op jit(solution)/shard_map/ppermute | solution.py:621
  56.1 4.4 collective-permute-start.5
  60.5 3.4 collective-permute-start.6
  63.9 12.2 %collective-permute-done.6 = bf16[8,512]{1,0:T(8,128)(2,1)S(1)} collective-permute-done((bf16[8,512]{1,0:T(8,128)(2,1)S(1)}, bf16[8,512]{1,0:T(8,128)(2,1)S(1)}, u32[]{:S(2)}, u32[]{:S(2)}) %collective-permute-start.6) | collective-permute-done | bytes 8224 | tf_op jit(solution)/shard_map/ppermute | solution.py:621
  76.1 5.5 %collective-permute-start.7 = (bf16[384,1024]{1,0:T(8,128)(2,1)S(1)}, bf16[384,1024]{1,0:T(8,128)(2,1)}, u32[]{:S(2)}, u32[]{:S(2)}) collective-permute-start(bf16[384,1024]{1,0:T(8,128)(2,1)S(1)} %collective-permute-done.5.x2), channel_id=1, source_target_pairs={{0,1},{1,2},{2,3},{4,5},{5,6},{6,7},{8,9},{9,10},{10,11},{12,13},{... | collective-permute-start | bytes 2359304 | tf_op jit(solution)/shard_map/ppermute | solution.py:624
  88.9 6.9 %collective-permute-done.7.x3 = bf16[384,1024]{1,0:T(8,128)(2,1)} collective-permute-done((bf16[384,1024]{1,0:T(8,128)(2,1)S(1)}, bf16[384,1024]{1,0:T(8,128)(2,1)}, u32[]{:S(2)}, u32[]{:S(2)}) %collective-permute-start.7) | collective-permute-done | bytes 786464 | tf_op jit(solution)/shard_map/ppermute | solution.py:624
  98.4 3.4 collective-permute-start.12
  101.8 31.6 %shard_map.230 = (bf16[1408,1024]{1,0:T(8,128)(2,1)}, bf16[384,1024]{1,0:T(8,128)(2,1)}, bf16[1408,1024]{1,0:T(8,128)(2,1)}, bf16[1408,1024]{1,0:T(8,128)(2,1)},...) custom-call(s32[1]{0:T(128)} %bitcast.at_ref.blocks_ref, ...), custom_call_target="tpu_custom_call" | custom-call | flops 2785017856 | bytes 15728640 | tf_op jit(solution)/shard_map/pallas_call | solution.py:164
  133.9 14.7 %collective-permute-start.13 = (bf16[384,1024]{1,0:T(8,128)(2,1)}, bf16[384,1024]{1,0:T(8,128)(2,1)}, u32[]{:S(2)}, u32[]{:S(2)}) collective-permute-start(bf16[384,1024]{1,0:T(8,128)(2,1)} %get-tuple-element.207.refs_0_), channel_id=1, source_target_pairs={{0,1},{1,0},{2,3},{3,2},{4,5},{5,4},{6,7},{7,6},{8,9},{9,8},{10,11... | collective-permute-start | bytes 2359304 | tf_op jit(solution)/shard_map/ppermute | solution.py:621
  148.7 4.7 all-gather.6.cloned.1.call-done.refs_4_.refs_5_.refs_6_.refs_12_.refs_13_.refs_14_
  153.4 14.1 %shard_map.231 = (bf16[768,1024]{1,0:T(8,128)(2,1)}, bf16[768,1024]{1,0:T(8,128)(2,1)}, f32[768,1024]{1,0:T(8,128)}, f32[768,1024]{1,0:T(8,128)}, f32[768,128]{1...) custom-call(s32[1]{0:T(128)} %bitcast.at_ref.blocks_ref, ...), custom_call_target="tpu_custom_call" | custom-call | flops 1811939328 | bytes 3244032 | tf_op jit(solution)/shard_map/pallas_call | solution.py:485
  169.7 14.3 %shard_map.233 = (bf16[768,1024]{1,0:T(8,128)(2,1)}, bf16[768,1024]{1,0:T(8,128)(2,1)}, f32[768,1024]{1,0:T(8,128)}, f32[768,1024]{1,0:T(8,128)}, f32[768,128]{1...) custom-call(s32[1]{0:T(128)} %bitcast.25.blocks_ref, ...), custom_call_target="tpu_custom_call" | custom-call | flops 1811939328 | bytes 3244032 | tf_op jit(solution)/shard_map/pallas_call | solution.py:485
  184.0 14.5 %shard_map.232 = (bf16[768,1024]{1,0:T(8,128)(2,1)}, bf16[768,1024]{1,0:T(8,128)(2,1)}, f32[768,1024]{1,0:T(8,128)}, f32[768,1024]{1,0:T(8,128)}, f32[768,128]{1...) custom-call(s32[1]{0:T(128)} %bitcast.18.blocks_ref, ...), custom_call_target="tpu_custom_call", output_to_operand_aliasing={{0}: (3, {}), {1}: (4, {}), {2}: (5, {}), {3}: (6, {}), {4}... | custom-call | flops 1811939328 | bytes 3244032 | tf_op jit(solution)/shard_map/pallas_call | solution.py:485
  200.8 14.5 %shard_map.234 = (bf16[768,1024]{1,0:T(8,128)(2,1)}, bf16[768,1024]{1,0:T(8,128)(2,1)}, f32[768,1024]{1,0:T(8,128)}, f32[768,1024]{1,0:T(8,128)}, f32[768,128]{1...) custom-call(s32[1]{0:T(128)} %bitcast.24.blocks_ref, ...), custom_call_target="tpu_custom_call", output_to_operand_aliasing={{0}: (3, {}), {1}: (4, {}), {2}: (5, {}), {3}: (6, {}), {4}... | custom-call | flops 1811939328 | bytes 3244032 | tf_op jit(solution)/shard_map/pallas_call | solution.py:485
  215.3 22.9 %shard_map.235 = (bf16[2,384,1024]{2,1,0:T(8,128)(2,1)}, bf16[2,384,1024]{2,1,0:T(8,128)(2,1)}, f32[2,8,1024]{2,1,0:T(8,128)}, bf16[768,1280]{1,0:T(8,128)(2,1)}...) custom-call(s32[2]{0:T(128)} %pad_add_fusion.1.blocks_ref, bf16[768,1024]{1,0:T(8,128)(2,1)} %get-tuple-element.307.refs_0_.refs_1_, ...), custom_call_target="tpu_custom_call" | custom-call | flops 3019898880 | bytes 2703360 | tf_op jit(solution)/shard_map/pallas_call | solution.py:485
  240.3 23.2 %shard_map.236 = (bf16[2,384,1024]{2,1,0:T(8,128)(2,1)}, bf16[2,384,1024]{2,1,0:T(8,128)(2,1)}, f32[2,8,1024]{2,1,0:T(8,128)}, bf16[768,1280]{1,0:T(8,128)(2,1)}...) custom-call(s32[2]{0:T(128)} %pad_add_fusion.blocks_ref, bf16[768,1024]{1,0:T(8,128)(2,1)} %get-tuple-element.306.refs_0_, ...), custom_call_target="tpu_custom_call" | custom-call | flops 3019898880 | bytes 2703360 | tf_op jit(solution)/shard_map/pallas_call | solution.py:485
  268.6 23.2 %shard_map.237 = (bf16[4,3,1536,128]{3,2,1,0:T(8,128)(2,1)}, bf16[4,3,1536,128]{3,2,1,0:T(8,128)(2,1)}) custom-call(s32[1]{0:T(128)} %bitcast.32.me_ref, bf16[768,1024]{1,0:T(8,128)(2,1)} %get-tuple-element.306.refs_0_, bf16[768,1024]{1,0:T(8,128)(2,1)} %get-tuple-element.307.refs_0_.refs_1_, bf16[768,1024]{1,0:T(8,128)(2,1)} %get-tuple-element.308.refs_1_.refs_2_, ...), custom_call_target="tpu_custom_call" | custom-call | flops 3623878656 | bytes 5898240 | tf_op jit(solution)/shard_map/pallas_call | solution.py:536
  296.1 20.7 %shard_map.238 = (bf16[4,3,1280,128]{3,2,1,0:T(8,128)(2,1)}, bf16[4,3,1280,128]{3,2,1,0:T(8,128)(2,1)}) custom-call(s32[1]{0:T(128)} %bitcast.32.me_ref, bf16[768,1024]{1,0:T(8,128)(2,1)} %get-tuple-element.306.refs_0_, bf16[768,1024]{1,0:T(8,128)(2,1)} %get-tuple-element.307.refs_0_.refs_1_, bf16[768,1024]{1,0:T(8,128)(2,1)} %get-tuple-element.308.refs_1_.refs_2_, ...), custom_call_target="tpu_custom_call" | custom-call | flops 3019898880 | bytes 4915200 | tf_op jit(solution)/shard_map/pallas_call | solution.py:536
  316.8 3.2 collective-permute-done.21.refs_5_
  330.0 27.2 %shard_map.239 = (bf16[4,2048,128]{2,1,0:T(8,128)(2,1)}, bf16[4,2048,128]{2,1,0:T(8,128)(2,1)}, bf16[1408,1024]{1,0:T(8,128)(2,1)}, f32[384,1024]{1,0:T(8,128)}, f32[8,1024]{1,0:T(8,128)}) custom-call(s32[1]{0:T(128)} %bitcast.32.me_ref, f32[384,1024]{1,0:T(8,128)} %get-tuple-element.328.refs_0_, bf16[384,1024]{1,0:T(8,128)(2,1)} %refs_1_.1, ...), custom_call_target="tpu_custom_call" | custom-call | flops 2785017856 | bytes 10485760 | tf_op jit(solution)/shard_map/pallas_call | solution.py:345
  370.2 27.7 %shard_map.240 = (bf16[4,2080,128]{2,1,0:T(8,128)(2,1)}, bf16[4,2080,128]{2,1,0:T(8,128)(2,1)}, bf16[1152,1024]{1,0:T(8,128)(2,1)}, f32[384,1024]{1,0:T(8,128)}) custom-call(s32[1]{0:T(128)} %bitcast.32.me_ref, f32[384,1024]{1,0:T(8,128)} %get-tuple-element.359.refs_0_.dh_ref, bf16[1408,1024]{1,0:T(8,128)(2,1)} %get-tuple-element.360.refs_1_, ...), custom_call_target="tpu_custom_call" | custom-call | flops 2785017856 | bytes 10485760 | tf_op jit(solution)/shard_map/pallas_call | solution.py:345
  397.9 7.7 %collective-permute-done.27 = bf16[384,1024]{1,0:T(8,128)(2,1)} collective-permute-done((bf16[384,1024]{1,0:T(8,128)(2,1)}, bf16[384,1024]{1,0:T(8,128)(2,1)}, u32[]{:S(2)}, u32[]{:S(2)}) %collective-permute-start.27) | collective-permute-done | bytes 786464 | tf_op jit(solution)/shard_map/ppermute | solution.py:621
  413.2 3.0 fusion.6
  420.9 16.8 %collective-permute-done.34 = bf16[384,1024]{1,0:T(8,128)(2,1)S(1)} collective-permute-done((bf16[384,1024]{1,0:T(8,128)(2,1)S(1)}, bf16[384,1024]{1,0:T(8,128)(2,1)S(1)}, u32[]{:S(2)}, u32[]{:S(2)}) %collective-permute-start.34) | collective-permute-done | bytes 786464 | tf_op jit(solution)/shard_map/ppermute | solution.py:768
  443.6 14.4 %collective-permute-done.39 = bf16[3104,128]{1,0:T(8,128)(2,1)S(1)} collective-permute-done((bf16[3104,128]{1,0:T(8,128)(2,1)S(1)}, bf16[3104,128]{1,0:T(8,128)(2,1)S(1)}, u32[]{:S(2)}, u32[]{:S(2)}) %collective-permute-start.39) | collective-permute-done | bytes 794656 | tf_op jit(solution)/shard_map/ppermute | solution.py:621
  463.5 19.3 %collective-permute-done.41 = bf16[1040,128]{1,0:T(8,128)(2,1)S(1)} collective-permute-done((bf16[1040,128]{1,0:T(8,128)(2,1)S(1)}, bf16[1040,128]{1,0:T(8,128)(2,1)S(1)}, u32[]{:S(2)}, u32[]{:S(2)}) %collective-permute-start.41) | collective-permute-done | bytes 266272 | tf_op jit(solution)/shard_map/ppermute | solution.py:621
  495.7 5.5 %collective-permute-done.43 = bf16[1056,128]{1,0:T(8,128)(2,1)S(1)} collective-permute-done((bf16[1056,128]{1,0:T(8,128)(2,1)S(1)}, bf16[1056,128]{1,0:T(8,128)(2,1)S(1)}, u32[]{:S(2)}, u32[]{:S(2)}) %collective-permute-start.43) | collective-permute-done | bytes 270368 | tf_op jit(solution)/shard_map/ppermute | solution.py:621
  501.2 11.1 %collective-permute-done.42 = bf16[1056,128]{1,0:T(8,128)(2,1)S(1)} collective-permute-done((bf16[1056,128]{1,0:T(8,128)(2,1)S(1)}, bf16[1056,128]{1,0:T(8,128)(2,1)S(1)}, u32[]{:S(2)}, u32[]{:S(2)}) %collective-permute-start.42) | collective-permute-done | bytes 270368 | tf_op jit(solution)/shard_map/ppermute | solution.py:621
  (245 shorter events, 108.3 us)
Async XLA Ops:
  7.2 94.7 %all-gather.4.cloned.1.call-start = ((), (), s32[]{:S(2)}) async-start(), calls=%async_computation | async-start | bytes 9437184 | tf_op jit(solution)/shard_map/all_gather | solution.py:629
  33.8 119.5 %all-gather.6.cloned.1.call-start = ((), (), s32[]{:S(2)}) async-start(), calls=%async_computation.1 | async-start | bytes 10616832 | tf_op jit(solution)/shard_map/all_gather | solution.py:655
  35.3 179.9 %all-gather.8.cloned.1.call-start = ((), (), s32[]{:S(2)}) async-start(), calls=%async_computation.2 | async-start | bytes 8847360 | tf_op jit(solution)/shard_map/all_gather | solution.py:655
  56.1 20.0 %collective-permute-start.5 = (bf16[384,1024]{1,0:T(8,128)(2,1)S(1)}, bf16[384,1024]{1,0:T(8,128)(2,1)S(1)}, u32[]{:S(2)}, u32[]{:S(2)}) collective-permute-start(bf16[384,1024]{1,0:T(8,128)(2,1)S(1)} %collective-permute-done.x1), channel_id=1, source_target_pairs={{0,1},{1,2},{2,3},{4,5},{5,6},{6,7},{8,9},{9,10},{10,11},{12,13},{... | collective-permute-start | bytes 2359304 | tf_op jit(solution)/shard_map/ppermute | solution.py:624
  95.9 37.6 %collective-permute-start.11 = (bf16[384,1024]{1,0:T(8,128)(2,1)S(1)}, bf16[384,1024]{1,0:T(8,128)(2,1)S(1)}, u32[]{:S(2)}, u32[]{:S(2)}) collective-permute-start(bf16[384,1024]{1,0:T(8,128)(2,1)S(1)} %copy-done.11), channel_id=1, source_target_pairs={{0,1},{1,0},{2,3},{3,2},{4,5},{5,4},{6,7},{7,6},{8,9},{9,8},{10,11... | collective-permute-start | bytes 2359304 | tf_op jit(solution)/shard_map/ppermute | solution.py:621
  98.4 35.0 %collective-permute-start.12 = (bf16[384,1024]{1,0:T(8,128)(2,1)S(1)}, bf16[384,1024]{1,0:T(8,128)(2,1)S(1)}, u32[]{:S(2)}, u32[]{:S(2)}) collective-permute-start(bf16[384,1024]{1,0:T(8,128)(2,1)S(1)} %copy-done.11), channel_id=1, source_target_pairs={{0,2},{1,3},{2,0},{3,1},{4,6},{5,7},{6,4},{7,5},{8,10},{9,11},{10,... | collective-permute-start | bytes 2359304 | tf_op jit(solution)/shard_map/ppermute | solution.py:621
  133.5 34.0 %collective-permute-start.14 = (bf16[384,1024]{1,0:T(8,128)(2,1)}, bf16[384,1024]{1,0:T(8,128)(2,1)S(1)}, u32[]{:S(2)}, u32[]{:S(2)}) collective-permute-start(bf16[384,1024]{1,0:T(8,128)(2,1)} %get-tuple-element.207.refs_0_), channel_id=1, source_target_pairs={{0,2},{1,3},{2,0},{3,1},{4,6},{5,7},{6,4},{7,5},{8,10},{9,11},{10,... | collective-permute-start | bytes 2359304 | tf_op jit(solution)/shard_map/ppermute | solution.py:621
  133.9 50.0 %collective-permute-start.13 = (bf16[384,1024]{1,0:T(8,128)(2,1)}, bf16[384,1024]{1,0:T(8,128)(2,1)}, u32[]{:S(2)}, u32[]{:S(2)}) collective-permute-start(bf16[384,1024]{1,0:T(8,128)(2,1)} %get-tuple-element.207.refs_0_), channel_id=1, source_target_pairs={{0,1},{1,0},{2,3},{3,2},{4,5},{5,4},{6,7},{7,6},{8,9},{9,8},{10,11... | collective-permute-start | bytes 2359304 | tf_op jit(solution)/shard_map/ppermute | solution.py:621
  148.6 49.8 %collective-permute-start.16 = (bf16[384,1024]{1,0:T(8,128)(2,1)S(1)}, bf16[384,1024]{1,0:T(8,128)(2,1)S(1)}, u32[]{:S(2)}, u32[]{:S(2)}) collective-permute-start(bf16[384,1024]{1,0:T(8,128)(2,1)S(1)} %collective-permute-done.12.refs_1_), channel_id=1, source_target_pairs={{0,1},{1,0},{2,3},{3,2},{4,5},{5,4},{6,7},{7,6},{8,9},{9,8},{10,11... | collective-permute-start | bytes 2359304 | tf_op jit(solution)/shard_map/ppermute | solution.py:621
  167.5 32.4 %collective-permute-start.15 = (bf16[384,1024]{1,0:T(8,128)(2,1)S(1)}, bf16[384,1024]{1,0:T(8,128)(2,1)S(1)}, u32[]{:S(2)}, u32[]{:S(2)}) collective-permute-start(bf16[384,1024]{1,0:T(8,128)(2,1)S(1)} %collective-permute-done.14.refs_0_), channel_id=1, source_target_pairs={{0,1},{1,0},{2,3},{3,2},{4,5},{5,4},{6,7},{7,6},{8,9},{9,8},{10,11... | collective-permute-start | bytes 2359304 | tf_op jit(solution)/shard_map/ppermute | solution.py:621
  239.4 24.1 %collective-permute-start.17 = (bf16[384,1024]{1,0:T(8,128)(2,1)S(1)}, bf16[384,1024]{1,0:T(8,128)(2,1)S(1)}, u32[]{:S(2)}, u32[]{:S(2)}) collective-permute-start(bf16[384,1024]{1,0:T(8,128)(2,1)S(1)} %slice_bitcast_fusion.4), channel_id=1, source_target_pairs={{0,1},{1,0},{2,3},{3,2},{4,5},{5,4},{6,7},{7,6},{8,9},{9,8},{10,11... | collective-permute-start | bytes 2359304 | tf_op jit(solution)/shard_map/ppermute | solution.py:621
  264.4 27.4 %collective-permute-start.19 = (bf16[384,1024]{1,0:T(8,128)(2,1)S(1)}, bf16[384,1024]{1,0:T(8,128)(2,1)S(1)}, u32[]{:S(2)}, u32[]{:S(2)}) collective-permute-start(bf16[384,1024]{1,0:T(8,128)(2,1)S(1)} %slice_bitcast_fusion.1), channel_id=1, source_target_pairs={{0,1},{1,0},{2,3},{3,2},{4,5},{5,4},{6,7},{7,6},{8,9},{9,8},{10,11... | collective-permute-start | bytes 2359304 | tf_op jit(solution)/shard_map/ppermute | solution.py:621
  266.3 25.5 %collective-permute-start.18 = (bf16[192,1024]{1,0:T(8,128)(2,1)S(1)}, bf16[192,1024]{1,0:T(8,128)(2,1)S(1)}, u32[]{:S(2)}, u32[]{:S(2)}) collective-permute-start(bf16[192,1024]{1,0:T(8,128)(2,1)S(1)} %get-tuple-element.288), channel_id=1, source_target_pairs={{0,2},{1,3},{2,0},{3,1},{4,6},{5,7},{6,4},{7,5},{8,10},{9,11},{10,... | collective-permute-start | bytes 1179656 | tf_op jit(solution)/shard_map/ppermute | solution.py:621
  291.8 28.8 %collective-permute-start.22 = (bf16[4,4608,128]{2,1,0:T(8,128)(2,1)}, bf16[4,4608,128]{2,1,0:T(8,128)(2,1)}, u32[]{:S(2)}, u32[]{:S(2)}) collective-permute-start(bf16[4,4608,128]{2,1,0:T(8,128)(2,1)} %bitcast.211), channel_id=1, source_target_pairs={{0,4},{4,0},{8,12},{12,8},{16,20},{20,16},{24,28},{28,24},{1,5},{5... | collective-permute-start | bytes 14155784 | tf_op jit(solution)/shard_map/ppermute | solution.py:621
  291.9 28.7 %collective-permute-start.20 = (bf16[384,1024]{1,0:T(8,128)(2,1)S(1)}, bf16[384,1024]{1,0:T(8,128)(2,1)S(1)}, u32[]{:S(2)}, u32[]{:S(2)}) collective-permute-start(bf16[384,1024]{1,0:T(8,128)(2,1)S(1)} %get-tuple-element.303), channel_id=1, source_target_pairs={{0,1},{1,0},{2,3},{3,2},{4,5},{5,4},{6,7},{7,6},{8,9},{9,8},{10,11... | collective-permute-start | bytes 2359304 | tf_op jit(solution)/shard_map/ppermute | solution.py:621
  294.1 25.9 %collective-permute-start.21 = (bf16[192,1024]{1,0:T(8,128)(2,1)}, bf16[192,1024]{1,0:T(8,128)(2,1)}, u32[]{:S(2)}, u32[]{:S(2)}) collective-permute-start(bf16[192,1024]{1,0:T(8,128)(2,1)} %get-tuple-element.304), channel_id=1, source_target_pairs={{0,2},{1,3},{2,0},{3,1},{4,6},{5,7},{6,4},{7,5},{8,10},{9,11},{10,... | collective-permute-start | bytes 1179656 | tf_op jit(solution)/shard_map/ppermute | solution.py:621
  324.8 32.5 %collective-permute-start.24 = (bf16[4,3840,128]{2,1,0:T(8,128)(2,1)}, bf16[4,3840,128]{2,1,0:T(8,128)(2,1)S(1)}, u32[]{:S(2)}, u32[]{:S(2)}) collective-permute-start(bf16[4,3840,128]{2,1,0:T(8,128)(2,1)} %bitcast.36), channel_id=1, source_target_pairs={{0,4},{4,0},{8,12},{12,8},{16,20},{20,16},{24,28},{28,24},{1,5},{5... | collective-permute-start | bytes 11796488 | tf_op jit(solution)/shard_map/ppermute | solution.py:621
  324.8 32.5 %collective-permute-start.25 = (bf16[4608,128]{1,0:T(8,128)(2,1)}, bf16[4608,128]{1,0:T(8,128)(2,1)}, u32[]{:S(2)}, u32[]{:S(2)}) collective-permute-start(bf16[4608,128]{1,0:T(8,128)(2,1)} %get-tuple-element.326), channel_id=1, source_target_pairs={{0,8},{4,12},{8,0},{12,4},{16,24},{20,28},{24,16},{28,20},{1,9},{5... | collective-permute-start | bytes 3538952 | tf_op jit(solution)/shard_map/ppermute | solution.py:621
  326.2 31.0 %collective-permute-start.26 = (bf16[4608,128]{1,0:T(8,128)(2,1)}, bf16[4608,128]{1,0:T(8,128)(2,1)}, u32[]{:S(2)}, u32[]{:S(2)}) collective-permute-start(bf16[4608,128]{1,0:T(8,128)(2,1)} %get-tuple-element.327), channel_id=1, source_target_pairs={{0,16},{4,20},{8,24},{12,28},{16,0},{20,4},{24,8},{28,12},{1,17},{... | collective-permute-start | bytes 3538952 | tf_op jit(solution)/shard_map/ppermute | solution.py:621
  327.6 29.6 %collective-permute-start.23 = (bf16[384,1024]{1,0:T(8,128)(2,1)}, bf16[384,1024]{1,0:T(8,128)(2,1)}, u32[]{:S(2)}, u32[]{:S(2)}) collective-permute-start(bf16[384,1024]{1,0:T(8,128)(2,1)} %slice_bitcast_fusion.3), channel_id=1, source_target_pairs={{0,1},{1,0},{2,3},{3,2},{4,5},{5,4},{6,7},{7,6},{8,9},{9,8},{10,11... | collective-permute-start | bytes 2359304 | tf_op jit(solution)/shard_map/ppermute | solution.py:621
  366.9 38.7 %collective-permute-start.28 = (bf16[4,2048,128]{2,1,0:T(8,128)(2,1)}, bf16[4,2048,128]{2,1,0:T(8,128)(2,1)}, u32[]{:S(2)}, u32[]{:S(2)}) collective-permute-start(bf16[4,2048,128]{2,1,0:T(8,128)(2,1)} %get-tuple-element.356), channel_id=1, source_target_pairs={{0,4},{4,0},{8,12},{12,8},{16,20},{20,16},{24,28},{28,24},{1,5},{5... | collective-permute-start | bytes 6291464 | tf_op jit(solution)/shard_map/ppermute | solution.py:621
  366.9 38.7 %collective-permute-start.29 = (bf16[6144,128]{1,0:T(8,128)(2,1)}, bf16[6144,128]{1,0:T(8,128)(2,1)}, u32[]{:S(2)}, u32[]{:S(2)}) collective-permute-start(bf16[6144,128]{1,0:T(8,128)(2,1)} %pad_maximum_fusion.3), channel_id=1, source_target_pairs={{0,8},{4,12},{8,0},{12,4},{16,24},{20,28},{24,16},{28,20},{1,9},{5... | collective-permute-start | bytes 4718600 | tf_op jit(solution)/shard_map/ppermute | solution.py:621
  367.4 38.2 %collective-permute-start.30 = (bf16[6144,128]{1,0:T(8,128)(2,1)}, bf16[6144,128]{1,0:T(8,128)(2,1)}, u32[]{:S(2)}, u32[]{:S(2)}) collective-permute-start(bf16[6144,128]{1,0:T(8,128)(2,1)} %pad_maximum_fusion.4), channel_id=1, source_target_pairs={{0,16},{4,20},{8,24},{12,28},{16,0},{20,4},{24,8},{28,12},{1,17},{... | collective-permute-start | bytes 4718600 | tf_op jit(solution)/shard_map/ppermute | solution.py:621
  368.1 37.5 %collective-permute-start.27 = (bf16[384,1024]{1,0:T(8,128)(2,1)}, bf16[384,1024]{1,0:T(8,128)(2,1)}, u32[]{:S(2)}, u32[]{:S(2)}) collective-permute-start(bf16[384,1024]{1,0:T(8,128)(2,1)} %bitcast_add_fusion.8), channel_id=1, source_target_pairs={{0,2},{1,3},{2,0},{3,1},{4,6},{5,7},{6,4},{7,5},{8,10},{9,11},{10,... | collective-permute-start | bytes 2359304 | tf_op jit(solution)/shard_map/ppermute | solution.py:621
  410.3 27.4 %collective-permute-start.31 = (bf16[4,2080,128]{2,1,0:T(8,128)(2,1)}, bf16[4,2080,128]{2,1,0:T(8,128)(2,1)S(1)}, u32[]{:S(2)}, u32[]{:S(2)}) collective-permute-start(bf16[4,2080,128]{2,1,0:T(8,128)(2,1)} %get-tuple-element.376), channel_id=1, source_target_pairs={{0,4},{4,0},{8,12},{12,8},{16,20},{20,16},{24,28},{28,24},{1,5},{5... | collective-permute-start | bytes 6389768 | tf_op jit(solution)/shard_map/ppermute | solution.py:621
  410.3 27.4 %collective-permute-start.32 = (bf16[3968,128]{1,0:T(8,128)(2,1)S(1)}, bf16[3968,128]{1,0:T(8,128)(2,1)S(1)}, u32[]{:S(2)}, u32[]{:S(2)}) collective-permute-start(bf16[3968,128]{1,0:T(8,128)(2,1)S(1)} %pad_maximum_fusion.9), channel_id=1, source_target_pairs={{0,16},{4,20},{8,24},{12,28},{16,0},{20,4},{24,8},{28,12},{1,17},{... | collective-permute-start | bytes 3047432 | tf_op jit(solution)/shard_map/ppermute | solution.py:621
  411.7 26.1 %collective-permute-start.33 = (bf16[3968,128]{1,0:T(8,128)(2,1)}, bf16[3968,128]{1,0:T(8,128)(2,1)S(1)}, u32[]{:S(2)}, u32[]{:S(2)}) collective-permute-start(bf16[3968,128]{1,0:T(8,128)(2,1)} %pad_maximum_fusion.10), channel_id=1, source_target_pairs={{0,8},{4,12},{8,0},{12,4},{16,24},{20,28},{24,16},{28,20},{1,9},{5... | collective-permute-start | bytes 3047432 | tf_op jit(solution)/shard_map/ppermute | solution.py:621
  416.3 21.4 %collective-permute-start.34 = (bf16[384,1024]{1,0:T(8,128)(2,1)S(1)}, bf16[384,1024]{1,0:T(8,128)(2,1)S(1)}, u32[]{:S(2)}, u32[]{:S(2)}) collective-permute-start(bf16[384,1024]{1,0:T(8,128)(2,1)S(1)} %dynamic-slice_select_fusion), channel_id=1, source_target_pairs={{1,0},{2,1},{3,2},{5,4},{6,5},{7,6},{9,8},{10,9},{11,10},{13,12},{... | collective-permute-start | bytes 2359304 | tf_op jit(solution)/shard_map/ppermute | solution.py:768
  440.1 21.6 %collective-permute-start.35 = (bf16[384,1024]{1,0:T(8,128)(2,1)S(1)}, bf16[384,1024]{1,0:T(8,128)(2,1)S(1)}, u32[]{:S(2)}, u32[]{:S(2)}) collective-permute-start(bf16[384,1024]{1,0:T(8,128)(2,1)S(1)} %select_add_fusion), channel_id=1, source_target_pairs={{1,0},{2,1},{3,2},{5,4},{6,5},{7,6},{9,8},{10,9},{11,10},{13,12},{... | collective-permute-start | bytes 2359304 | tf_op jit(solution)/shard_map/ppermute | solution.py:768
  459.3 23.6 %collective-permute-start.37 = (bf16[3104,128]{1,0:T(8,128)(2,1)S(1)}, bf16[3104,128]{1,0:T(8,128)(2,1)S(1)}, u32[]{:S(2)}, u32[]{:S(2)}) collective-permute-start(bf16[3104,128]{1,0:T(8,128)(2,1)S(1)} %pad_maximum_fusion.12), channel_id=1, source_target_pairs={{0,16},{4,20},{8,24},{12,28},{16,0},{20,4},{24,8},{28,12},{1,17},{... | collective-permute-start | bytes 2383880 | tf_op jit(solution)/shard_map/ppermute | solution.py:621
  460.4 22.5 %collective-permute-start.41 = (bf16[1040,128]{1,0:T(8,128)(2,1)S(1)}, bf16[1040,128]{1,0:T(8,128)(2,1)S(1)}, u32[]{:S(2)}, u32[]{:S(2)}) collective-permute-start(bf16[1040,128]{1,0:T(8,128)(2,1)S(1)} %fusion.24), channel_id=1, source_target_pairs={{0,16},{4,20},{8,24},{12,28},{16,0},{20,4},{24,8},{28,12},{1,17},{... | collective-permute-start | bytes 798728 | tf_op jit(solution)/shard_map/ppermute | solution.py:621
  462.2 23.8 %collective-permute-start.36 = (bf16[384,1024]{1,0:T(8,128)(2,1)S(1)}, bf16[384,1024]{1,0:T(8,128)(2,1)S(1)}, u32[]{:S(2)}, u32[]{:S(2)}) collective-permute-start(bf16[384,1024]{1,0:T(8,128)(2,1)S(1)} %get-tuple-element.441), channel_id=1, source_target_pairs={{1,0},{2,1},{3,2},{5,4},{6,5},{7,6},{9,8},{10,9},{11,10},{13,12},{... | collective-permute-start | bytes 2359304 | tf_op jit(solution)/shard_map/ppermute | solution.py:768
  (57 other events, 688.7 us)
Sparse Core Ops, SparseCore 0:
  34.0 56.2 all-gather.3
  92.7 60.5 all-gather.5
  155.8 53.6 all-gather.7
